TPU v7x, 256 devices: a whole 4x4x8 slice. The times are simulated.
256 devices in a mesh: patch: 32 (over z, y), lev: 8 (over x, core).
Axes of the slice: x: 4, y: 4, z: 8, core: 2. Of those that a mesh axis runs over, the one named last changes fastest.
Arguments:
- node_state: bfloat16 [8192, 16, 192], P('patch', 'lev'), may hold values from -6 to 6
- edge_attr: bfloat16 [65536, 192], P('patch'), may hold values from -6 to 6
- edge_sender: int32 [65536], P('patch'), may hold values from 0 to 1791, as said below
- edge_receiver: int32 [65536], P('patch'), may hold values from -1 to 127, as said below
- tile_block: int32 [512], P('patch'), may hold values from 0 to 1
- halo_rows: int32 [1024, 48], P('patch'), may hold values from 0 to 255
- valid_levels: int32 [8192], P('patch'), may hold values from 12 to 16
- edge_w_in: bfloat16 [576, 192], replicated, may hold values from -0.25 to 0.25
- edge_bias: float32 [192], replicated, may hold values from -3 to 3
- edge_w_out: bfloat16 [192, 192], replicated, may hold values from -0.4375 to 0.4375
- node_w_in: bfloat16 [384, 192], replicated, may hold values from -0.3125 to 0.3125
- node_bias: float32 [192], replicated, may hold values from -3 to 3
- node_w_out: bfloat16 [192, 192], replicated, may hold values from -0.4375 to 0.4375
- node_gain: float32 [192], replicated, may hold values from 0.1 to 1.9
- attention_gain: float32 [192], replicated, may hold values from 0.1 to 1.9
- query_weight: bfloat16 [192, 192], replicated, may hold values from -12.268693 to 12.268693
- key_weight: bfloat16 [192, 192], replicated, may hold values from -0.28867513 to 0.28867513
- value_weight: bfloat16 [192, 192], replicated, may hold values from -0.4375 to 0.4375
- output_weight: bfloat16 [192, 192], replicated, may hold values from -0.4375 to 0.4375
Outputs:
- column_state: bfloat16 [8192, 16, 192], P('patch', 'lev')
Inputs may be any that keep to these rules, and one draw needn't show every extreme that they name: `edge_sender`: rows of a table below 256 are the patch's own nodes; row 256 + q * 48 + s is slot s of what patch q sends it. Empty edge slots hold 0. Slots of a send list that no edge reads may name any row. `edge_receiver`: empty slots fill whole tiles at the end of a patch's tiles; patches have from half of their 16 tiles to all of them in use, and some patch uses all.
All inputs are finite; a program needn't handle non-finite values.
Results may differ from a plain program's by a relative error of at most 0.008.
Values may be sent and summed in bfloat16 or wider, within the bound.
No kernel may reach another device: no remote copies, remote signals or barrier semaphores. Data moves between devices by JAX's collectives and lax.ppermute only.
A program may use at most 64 MiB of HBM per device.

v0:
```python
import math

import jax
import jax.numpy as jnp
from jax import lax
from jax.sharding import PartitionSpec as P

HEADS = 4


def normalize(values):
    centered = values - jnp.mean(values, axis=-1, keepdims=True)
    spread = jnp.mean(centered * centered, axis=-1, keepdims=True)
    return centered * lax.rsqrt(spread + 1e-05)


def column_attention(queries, key_rows, value_rows, key_live):
    node_count, query_levels, model_width = queries.shape
    key_levels = key_rows.shape[1]
    head_width = model_width // HEADS
    query_heads = queries.reshape(node_count, query_levels, HEADS, head_width)
    key_heads = key_rows.reshape(node_count, key_levels, HEADS, head_width)
    value_heads = value_rows.reshape(node_count, key_levels, HEADS, head_width)
    scores = jnp.einsum(
        "nlhd,nmhd->nhlm", query_heads, key_heads, preferred_element_type=jnp.float32
    ) * (1.0 / math.sqrt(head_width))
    scores = jnp.where(key_live[:, None, None, :], scores, -1e30)
    weights = jax.nn.softmax(scores, axis=-1).astype(jnp.bfloat16)
    attended = jnp.einsum(
        "nhlm,nmhd->nlhd", weights, value_heads, preferred_element_type=jnp.float32
    )
    return attended.astype(jnp.bfloat16).reshape(node_count, query_levels, model_width)


def project_rows(flat_rows, weight_matrix):
    return jnp.dot(flat_rows, weight_matrix, preferred_element_type=jnp.float32).astype(
        jnp.bfloat16
    )


def per_device(
    node_state,
    edge_attr,
    edge_sender,
    edge_receiver,
    tile_block,
    halo_rows,
    valid_levels,
    edge_w_in,
    edge_bias,
    edge_w_out,
    node_w_in,
    node_bias,
    node_w_out,
    node_gain,
    attention_gain,
    query_weight,
    key_weight,
    value_weight,
    output_weight,
):
    patch_count = lax.axis_size("patch")
    group_count = lax.axis_size("lev")
    node_dev, lev_dev, model_width = node_state.shape
    tile_count = tile_block.shape[0]
    slot_count = halo_rows.shape[1]
    blocks = node_dev // 128
    edge_base = (
        jnp.dot(edge_attr, edge_w_in[2 * model_width :], preferred_element_type=jnp.float32)
        + edge_bias
    )
    in_block = edge_receiver.reshape(tile_count, 128)
    receiver_index = jnp.where(in_block >= 0, tile_block[:, None] * 128 + in_block, 0).reshape(-1)
    edge_onehot = (in_block[:, None, :] == jnp.arange(128, dtype=jnp.int32)[None, :, None]).astype(
        jnp.bfloat16
    )
    block_onehot = (tile_block[:, None] == jnp.arange(blocks, dtype=jnp.int32)[None, :]).astype(
        jnp.float32
    )
    incoming_rows = lax.all_to_all(
        node_state[halo_rows], "patch", split_axis=0, concat_axis=0, tiled=True
    )
    updated = []
    for level_index in range(lev_dev):
        own_rows = node_state[:, level_index]
        remote_rows = incoming_rows[:, :, level_index].reshape(
            patch_count * slot_count, model_width
        )
        node_table = jnp.concatenate([own_rows, remote_rows], axis=0)
        sender_proj = jnp.dot(
            node_table, edge_w_in[:model_width], preferred_element_type=jnp.float32
        )
        receiver_proj = jnp.dot(
            own_rows, edge_w_in[model_width : 2 * model_width], preferred_element_type=jnp.float32
        )
        edge_pre = sender_proj[edge_sender] + receiver_proj[receiver_index] + edge_base
        edge_hidden = jax.nn.silu(edge_pre).astype(jnp.bfloat16)
        message = jnp.dot(edge_hidden, edge_w_out, preferred_element_type=jnp.float32).astype(
            jnp.bfloat16
        )
        tile_sums = jnp.einsum(
            "tne,ted->tnd",
            edge_onehot,
            message.reshape(tile_count, 128, model_width),
            preferred_element_type=jnp.float32,
        )
        summed = (
            jnp.einsum("tb,tnd->bnd", block_onehot, tile_sums, precision=lax.Precision.HIGHEST)
            .reshape(node_dev, model_width)
            .astype(jnp.bfloat16)
        )
        node_pre = (
            jnp.dot(own_rows, node_w_in[:model_width], preferred_element_type=jnp.float32)
            + jnp.dot(summed, node_w_in[model_width:], preferred_element_type=jnp.float32)
            + node_bias
        )
        node_hidden = jax.nn.silu(node_pre).astype(jnp.bfloat16)
        update = jnp.dot(node_hidden, node_w_out, preferred_element_type=jnp.float32)
        updated.append(
            (own_rows.astype(jnp.float32) + node_gain * normalize(update)).astype(jnp.bfloat16)
        )
    level_state = jnp.stack(updated, axis=1)
    normed = (attention_gain * normalize(level_state.astype(jnp.float32))).astype(jnp.bfloat16)
    level_ids = lax.axis_index("lev") * lev_dev + jnp.arange(lev_dev, dtype=jnp.int32)
    query_live = level_ids[None, :] < valid_levels[:, None]
    per_group = node_dev // group_count
    outgoing_cols = normed.reshape(group_count, per_group, lev_dev, model_width)
    outgoing_live = query_live.astype(jnp.bfloat16).reshape(group_count, per_group, lev_dev, 1)
    column_rows = lax.all_to_all(outgoing_cols, "lev", split_axis=0, concat_axis=2, tiled=True)
    column_live = lax.all_to_all(outgoing_live, "lev", split_axis=0, concat_axis=2, tiled=True)
    item_count = column_rows.shape[1]
    level_total = column_rows.shape[2]
    flat_rows = column_rows.reshape(item_count * level_total, model_width)
    queries = project_rows(flat_rows, query_weight).reshape(item_count, level_total, model_width)
    key_rows = project_rows(flat_rows, key_weight).reshape(item_count, level_total, model_width)
    value_rows = project_rows(flat_rows, value_weight).reshape(item_count, level_total, model_width)
    attended_cols = column_attention(queries, key_rows, value_rows, column_live[0, :, :, 0] > 0)
    attended = lax.all_to_all(
        attended_cols[None], "lev", split_axis=2, concat_axis=0, tiled=True
    ).reshape(node_dev, lev_dev, model_width)
    mixed_rows = jnp.dot(
        attended.reshape(node_dev * lev_dev, model_width),
        output_weight,
        preferred_element_type=jnp.float32,
    ).reshape(node_dev, lev_dev, model_width)
    return (
        level_state.astype(jnp.float32) + jnp.where(query_live[:, :, None], mixed_rows, 0.0)
    ).astype(jnp.bfloat16)


def solution(mesh):
    in_specs = (
        P("patch", "lev", None),
        P("patch", None),
        P("patch"),
        P("patch"),
        P("patch"),
        P("patch", None),
        P("patch"),
        P(),
        P(),
        P(),
        P(),
        P(),
        P(),
        P(),
        P(),
        P(),
        P(),
        P(),
        P(),
    )
    out_specs = P("patch", "lev", None)
    return jax.shard_map(
        per_device, mesh=mesh, in_specs=in_specs, out_specs=out_specs, check_vma=False
    )
```

profile of v0, /device:TPU:8, one launch (start us, length us, event | category | flops | bytes accessed | tf_op | source)
XLA Modules:
  0.0 135.8 jit_solution(528299933734503728)
XLA Ops:
  0.0 1.2 copy.61
  1.2 0.7 compare_select_fusion
  2.0 6.6 %gather_fusion = bf16[1536,2,192]{2,1,0:T(2,128)(2,1)S(1)} fusion(bf16[256,2,192]{2,1,0:T(2,128)(2,1)S(1)} %copy.61, s32[2048]{0:T(1024)S(1)} %pad_clamp_fusion), kind=kCustom, calls=%fused_computation | custom fusion | bytes 2365440 | tf_op jit(solution)/shard_map/gather | solution.py:81
  8.6 1.5 %copy.63 = bf16[32,48,2,192]{3,1,2,0:T(8,128)(2,1)} copy(bf16[32,48,2,192]{3,2,1,0:T(2,128)(2,1)S(1)} %bitcast.95) | data formatting | bytes 2359296 | tf_op jit(solution)/shard_map/gather | solution.py:81
  10.1 11.9 %all-to-all-start = ((bf16[32,48,2,192]{3,1,2,0:T(8,128)(2,1)}), bf16[32,48,2,192]{3,1,2,0:T(8,128)(2,1)}, u32[]{:S(2)}, u32[]{:S(2)}) async-start(bf16[32,48,2,192]{3,1,2,0:T(8,128)(2,1)} %copy.63), calls=%async_computation | async-start | bytes 3145728 | tf_op jit(solution)/shard_map/all_to_all | solution.py:80
  22.0 0.7 slice_bitcast_fusion.1
  22.6 0.8 copy.64
  23.5 1.2 fusion.65
  24.7 6.6 %gather_fusion.2 = f32[2048,192]{1,0:T(8,128)S(1)} fusion(f32[256,192]{1,0:T(8,128)S(1)} %fusion.65, s32[2048]{0:T(1024)S(1)} %fusion.74), kind=kCustom, calls=%fused_computation.2 | custom fusion | bytes 3153920 | tf_op jit(solution)/shard_map/gather | solution.py:96
  31.3 1.8 %copy.68 = f32[2048,192]{0,1:T(8,128)} copy(f32[2048,192]{1,0:T(8,128)S(1)} %gather_fusion.2) | data formatting | bytes 3145728 | tf_op jit(solution)/shard_map/gather | solution.py:96
  33.2 1.2 fusion.63
  34.4 6.6 %gather_fusion.4 = f32[2048,192]{1,0:T(8,128)S(1)} fusion(f32[256,192]{1,0:T(8,128)S(1)} %fusion.63, s32[2048]{0:T(1024)S(1)} %fusion.74), kind=kCustom, calls=%fused_computation.4 | custom fusion | bytes 3153920 | tf_op jit(solution)/shard_map/gather | solution.py:96
  41.1 1.8 %copy.75 = f32[2048,192]{0,1:T(8,128)} copy(f32[2048,192]{1,0:T(8,128)S(1)} %gather_fusion.4) | data formatting | bytes 3145728 | tf_op jit(solution)/shard_map/gather | solution.py:96
  43.0 0.7 compare_convert_fusion
  43.6 1.7 %fusion.69 = f32[256,192]{0,1:T(8,128)} fusion(bf16[384,192]{0,1:T(8,128)(2,1)} %param.29, bf16[256,2,192]{0,2,1:T(8,128)(2,1)S(1)} %copy-done.1), kind=kOutput, calls=%fused_computation.91 | convolution fusion | flops 18874368 | bytes 393216 | tf_op jit(solution)/shard_map/dot_general | solution.py:113
  45.4 1.7 %fusion.71 = f32[256,192]{0,1:T(8,128)} fusion(bf16[384,192]{0,1:T(8,128)(2,1)} %param.29, bf16[256,2,192]{0,2,1:T(8,128)(2,1)S(1)} %copy-done.1), kind=kOutput, calls=%fused_computation.93 | convolution fusion | flops 18874368 | bytes 393216 | tf_op jit(solution)/shard_map/dot_general | solution.py:113
  47.2 1.5 %convolution_add_fusion = f32[2048,192]{0,1:T(8,128)} fusion(bf16[2048,192]{0,1:T(8,128)(2,1)S(1)} %copy-done, f32[192]{0:T(256)S(1)} %copy-done.18, bf16[576,192]{0,1:T(8,128)(2,1)S(1)} %copy-done.4), kind=kOutput, calls=%fused_computation.6 | convolution fusion | flops 151388160 | bytes 2458624 | tf_op jit(solution)/shard_map/dot_general | solution.py:69
  48.7 11.7 %all-to-all-done = bf16[32,48,2,192]{3,1,2,0:T(8,128)(2,1)} async-done(((bf16[32,48,2,192]{3,1,2,0:T(8,128)(2,1)}), bf16[32,48,2,192]{3,1,2,0:T(8,128)(2,1)}, u32[]{:S(2)}, u32[]{:S(2)}) %all-to-all-start) | async-done | bytes 1179680 | tf_op jit(solution)/shard_map/all_to_all | solution.py:80
  60.4 4.3 %all-to-all-start.2 = ((bf16[8,32,2,1]{1,2,3,0:T(2,128)(2,1)}), bf16[8,32,2,1]{1,2,3,0:T(2,128)(2,1)S(1)}, u32[]{:S(2)}, u32[]{:S(2)}) async-start(bf16[8,32,2,1]{1,2,3,0:T(2,128)(2,1)} %compare_convert_fusion), calls=%async_computation.2 | async-start | bytes 8192 | tf_op jit(solution)/shard_map/all_to_all | solution.py:130
  64.7 2.5 %fusion.86 = (bf16[32,48,1,192]{3,1,2,0:T(8,128)(2,1)S(1)}, bf16[32,48,1,192]{3,1,2,0:T(8,128)(2,1)}) fusion(bf16[32,48,2,192]{3,1,2,0:T(8,128)(2,1)} %all-to-all-done), kind=kLoop, calls=%fused_computation.125 | loop fusion | bytes 2359296 | tf_op jit(solution)/shard_map/slice | solution.py:86
  67.2 0.4 fusion.23
  67.6 8.6 %gather_fusion.1 = f32[2048,192]{1,0:T(8,128)} fusion(f32[1792,192]{1,0:T(8,128)S(1)} %fusion.23, s32[2048]{0:T(1024)S(1)} %fusion.73), kind=kCustom, calls=%fused_computation.1 | custom fusion | bytes 3153920 | tf_op jit(solution)/shard_map/gather | solution.py:96
  76.2 3.0 %copy.67 = f32[2048,192]{0,1:T(8,128)} copy(f32[2048,192]{1,0:T(8,128)} %gather_fusion.1) | data formatting | bytes 3145728 | tf_op jit(solution)/shard_map/gather | solution.py:96
  79.2 2.6 %fusion.8 = bf16[24,16,8,128]{3,2,1,0:T(8,128)(2,1)S(1)} fusion(bf16[192,192]{1,0:T(8,128)(2,1)S(1)} %copy-done.21, f32[2048,192]{0,1:T(8,128)} %convolution_add_fusion, f32[2048,192]{0,1:T(8,128)} %copy.67, f32[2048,192]{0,1:T(8,128)S(1)} %copy-done.3), kind=kOutput, calls=%fused_computation.19 | convolution fusion | flops 154140672 | bytes 5578752 | tf_op jit(solution)/shard_map/dot_general | solution.py:98
  81.8 0.5 fusion.22
  82.3 1.5 %fusion.15 = bf16[2,128,192]{1,0,2:T(2,128)(2,1)S(1)} fusion(f32[16,128,192]{1,2,0:T(8,128)S(1)} %fusion.22, s32[16]{0:T(128)S(1)} %copy-done.17), kind=kOutput, calls=%fused_computation.33 | convolution fusion | flops 9486368 | bytes 1671232 | tf_op jit(solution)/shard_map/tb,tnd->bnd/dot_general | solution.py:108
  83.8 0.4 fusion.87
  84.3 1.6 %fusion.27 = f32[1792,192]{1,0:T(8,128)S(1)} fusion(bf16[1536,192]{1,0:T(8,128)(2,1)} %bitcast.96, bf16[256,192]{1,0:T(8,128)(2,1)S(1)} %copy.71, bf16[576,192]{0,1:T(8,128)(2,1)S(1)} %copy-done.4), kind=kOutput, calls=%fused_computation.43 | convolution fusion | flops 133496832 | bytes 2195456 | tf_op jit(solution)/shard_map/dot_general | solution.py:90
  85.9 8.6 %gather_fusion.3 = f32[2048,192]{1,0:T(8,128)} fusion(f32[1792,192]{1,0:T(8,128)S(1)} %fusion.27, s32[2048]{0:T(1024)S(1)} %fusion.73), kind=kCustom, calls=%fused_computation.3 | custom fusion | bytes 3153920 | tf_op jit(solution)/shard_map/gather | solution.py:96
  94.4 3.0 %copy.74 = f32[2048,192]{0,1:T(8,128)} copy(f32[2048,192]{1,0:T(8,128)} %gather_fusion.3) | data formatting | bytes 3145728 | tf_op jit(solution)/shard_map/gather | solution.py:96
  97.4 2.6 %fusion.9 = bf16[24,16,8,128]{3,2,1,0:T(8,128)(2,1)S(1)} fusion(bf16[192,192]{1,0:T(8,128)(2,1)S(1)} %copy-done.22, f32[2048,192]{0,1:T(8,128)} %convolution_add_fusion, f32[2048,192]{0,1:T(8,128)} %copy.74, f32[2048,192]{0,1:T(8,128)S(1)} %copy-done.2), kind=kOutput, calls=%fused_computation.20 | convolution fusion | flops 154140672 | bytes 5578752 | tf_op jit(solution)/shard_map/dot_general | solution.py:98
  100.0 0.5 fusion.21
  100.5 1.5 %fusion.18 = bf16[2,128,192]{1,0,2:T(2,128)(2,1)S(1)} fusion(f32[16,128,192]{1,2,0:T(8,128)S(1)} %fusion.21, s32[16]{0:T(128)S(1)} %copy-done.17), kind=kOutput, calls=%fused_computation.34 | convolution fusion | flops 9486368 | bytes 1671232 | tf_op jit(solution)/shard_map/tb,tnd->bnd/dot_general | solution.py:108
  102.1 0.4 fusion.92
  103.5 0.7 copy.80
  104.2 4.9 %all-to-all-start.1 = ((bf16[8,32,2,192]{3,1,2,0:T(8,128)(2,1)}), bf16[8,32,2,192]{3,1,2,0:T(8,128)(2,1)S(1)}, u32[]{:S(2)}, u32[]{:S(2)}) async-start(bf16[8,32,2,192]{3,1,2,0:T(8,128)(2,1)} %copy.80), calls=%async_computation.1 | async-start | bytes 524288 | tf_op jit(solution)/shard_map/all_to_all | solution.py:129
  109.3 7.4 %all-to-all-done.1 = bf16[8,32,2,192]{3,1,2,0:T(8,128)(2,1)S(1)} async-done(((bf16[8,32,2,192]{3,1,2,0:T(8,128)(2,1)}), bf16[8,32,2,192]{3,1,2,0:T(8,128)(2,1)S(1)}, u32[]{:S(2)}, u32[]{:S(2)}) %all-to-all-start.1) | async-done | bytes 196640 | tf_op jit(solution)/shard_map/all_to_all | solution.py:129
  116.7 0.3 copy.81
  117.2 0.2 convolution_convert_fusion.4
  117.6 0.3 reshape_reshape.11
  118.3 0.3 reshape_reshape.12
  119.0 0.3 reshape_reshape.10
  119.3 1.7 %fusion.97 = (f32[32,4,16]{2,1,0:T(4,128)S(1)}, f32[32,4,16,16]{2,3,1,0:T(8,128)}) fusion(bf16[32,16,4,48]{3,2,1,0:T(4,128)(2,1)S(1)} %reshape_reshape.12, bf16[32,16,4,48]{3,2,1,0:T(4,128)(2,1)S(1)} %reshape_reshape.11, pred[32,16]{1,0:T(8,128)(4,1)S(1)} %copy.83), kind=kOutput, calls=%fused_computation.128 | convolution fusion | flops 3276815 | bytes 532992 | tf_op jit(solution)/shard_map/sub | solution.py:28
  121.0 1.6 %fusion.10 = bf16[32,16,4,48]{3,1,2,0:T(8,128)(2,1)S(1)} fusion(f32[32,4,16,16]{2,3,1,0:T(8,128)} %get-tuple-element.16, bf16[32,16,4,48]{3,2,1,0:T(4,128)(2,1)S(1)} %reshape_reshape.10, f32[32,4,16]{2,1,0:T(4,128)S(1)} %get-tuple-element.15), kind=kOutput, calls=%fused_computation.22 | convolution fusion | flops 3309568 | bytes 532480 | tf_op jit(solution)/shard_map/nhlm,nmhd->nlhd/dot_general | solution.py:29
  122.9 1.0 reshape.197
  123.9 3.4 %all-to-all-start.3 = ((bf16[1,32,16,192]{3,1,0,2:T(8,128)(2,1)}), bf16[1,32,16,192]{3,1,0,2:T(8,128)(2,1)S(1)}, u32[]{:S(2)}, u32[]{:S(2)}) async-start(bf16[1,32,16,192]{3,1,0,2:T(8,128)(2,1)} %reshape.197), calls=%async_computation.3 | async-start | bytes 524288 | tf_op jit(solution)/shard_map/all_to_all | solution.py:138
  127.4 7.4 %all-to-all-done.3 = bf16[1,32,16,192]{3,1,0,2:T(8,128)(2,1)S(1)} async-done(((bf16[1,32,16,192]{3,1,0,2:T(8,128)(2,1)}), bf16[1,32,16,192]{3,1,0,2:T(8,128)(2,1)S(1)}, u32[]{:S(2)}, u32[]{:S(2)}) %all-to-all-start.3) | async-done | bytes 196640 | tf_op jit(solution)/shard_map/all_to_all | solution.py:138
  134.8 0.9 fusion.12
  (90 shorter events, 3.0 us)
Async XLA Ops:
  0.0 47.1 %copy-start = (bf16[2048,192]{0,1:T(8,128)(2,1)S(1)}, bf16[2048,192]{0,1:T(8,128)(2,1)}, u32[]{:S(2)}) copy-start(bf16[2048,192]{0,1:T(8,128)(2,1)} %param.20) | copy-start | bytes 2359300
  10.1 11.9 %copy-start.1 = (bf16[256,2,192]{0,2,1:T(8,128)(2,1)S(1)}, bf16[256,2,192]{0,2,1:T(8,128)(2,1)}, u32[]{:S(2)}) copy-start(bf16[256,2,192]{0,2,1:T(8,128)(2,1)} %param.19) | copy-start | bytes 589828
  10.1 13.3 %copy-start.17 = (s32[16]{0:T(128)S(1)}, s32[16]{0:T(128)}, u32[]{:S(2)}) copy-start(s32[16]{0:T(128)} %param.23) | copy-start | bytes 196
  10.1 13.3 %copy-start.14 = (s32[2048]{0:T(1024)S(1)}, s32[2048]{0:T(1024)}, u32[]{:S(2)}) copy-start(s32[2048]{0:T(1024)} %param.22) | copy-start | bytes 24580
  10.1 50.3 %all-to-all-start = ((bf16[32,48,2,192]{3,1,2,0:T(8,128)(2,1)}), bf16[32,48,2,192]{3,1,2,0:T(8,128)(2,1)}, u32[]{:S(2)}, u32[]{:S(2)}) async-start(bf16[32,48,2,192]{3,1,2,0:T(8,128)(2,1)} %copy.63), calls=%async_computation | async-start | bytes 3145728 | tf_op jit(solution)/shard_map/all_to_all | solution.py:80
  31.3 1.8 %copy-start.6 = (bf16[256,192]{0,1:T(8,128)(2,1)S(1)}, bf16[256,192]{0,1:T(8,128)(2,1)}, u32[]{:S(2)}) copy-start(bf16[256,192]{0,1:T(8,128)(2,1)} %get-tuple-element.10) | copy-start | bytes 294916
  41.1 1.8 %copy-start.16 = (s32[256]{0:T(256)S(1)}, s32[256]{0:T(256)}, u32[]{:S(2)}) copy-start(s32[256]{0:T(256)} %param.25) | copy-start | bytes 3076
  41.1 2.6 %copy-start.15 = (s32[2048]{0:T(1024)S(1)}, s32[2048]{0:T(1024)}, u32[]{:S(2)}) copy-start(s32[2048]{0:T(1024)} %param.21) | copy-start | bytes 24580
  41.1 6.0 %copy-start.4 = (bf16[576,192]{0,1:T(8,128)(2,1)S(1)}, bf16[576,192]{0,1:T(8,128)(2,1)}, u32[]{:S(2)}) copy-start(bf16[576,192]{0,1:T(8,128)(2,1)} %param.26) | copy-start | bytes 663556
  41.1 6.0 %copy-start.18 = (f32[192]{0:T(256)S(1)}, f32[192]{0:T(256)}, u32[]{:S(2)}) copy-start(f32[192]{0:T(256)} %param.27) | copy-start | bytes 2308
  60.4 43.9 %all-to-all-start.2 = ((bf16[8,32,2,1]{1,2,3,0:T(2,128)(2,1)}), bf16[8,32,2,1]{1,2,3,0:T(2,128)(2,1)S(1)}, u32[]{:S(2)}, u32[]{:S(2)}) async-start(bf16[8,32,2,1]{1,2,3,0:T(2,128)(2,1)} %compare_convert_fusion), calls=%async_computation.2 | async-start | bytes 8192 | tf_op jit(solution)/shard_map/all_to_all | solution.py:130
  64.7 2.5 %copy-start.5 = (bf16[256,192]{1,0:T(8,128)(2,1)S(1)}, bf16[256,192]{1,0:T(8,128)(2,1)}, u32[]{:S(2)}) copy-start(bf16[256,192]{1,0:T(8,128)(2,1)} %copy.64) | copy-start | bytes 294916
  76.2 3.0 %copy-start.3 = (f32[2048,192]{0,1:T(8,128)S(1)}, f32[2048,192]{0,1:T(8,128)}, u32[]{:S(2)}) copy-start(f32[2048,192]{0,1:T(8,128)} %copy.68) | copy-start | bytes 4718596
  76.2 3.0 %copy-start.21 = (bf16[192,192]{1,0:T(8,128)(2,1)S(1)}, bf16[192,192]{1,0:T(8,128)(2,1)}, u32[]{:S(2)}) copy-start(bf16[192,192]{1,0:T(8,128)(2,1)} %param.28) | copy-start | bytes 221188
  81.7 2.0 %copy-start.7 = (bf16[384,192]{0,1:T(8,128)(2,1)S(1)}, bf16[384,192]{0,1:T(8,128)(2,1)}, u32[]{:S(2)}) copy-start(bf16[384,192]{0,1:T(8,128)(2,1)} %param.29) | copy-start | bytes 442372
  81.8 2.0 %copy-start.10 = (f32[256,192]{0,1:T(8,128)S(1)}, f32[256,192]{0,1:T(8,128)}, u32[]{:S(2)}) copy-start(f32[256,192]{0,1:T(8,128)} %fusion.69) | copy-start | bytes 589828
  81.8 2.0 %copy-start.23 = (bf16[192,192]{1,0:T(8,128)(2,1)S(1)}, bf16[192,192]{1,0:T(8,128)(2,1)}, u32[]{:S(2)}) copy-start(bf16[192,192]{1,0:T(8,128)(2,1)} %param.31) | copy-start | bytes 221188
  81.8 2.0 %copy-start.26 = (f32[192]{0:T(256)S(1)}, f32[192]{0:T(256)}, u32[]{:S(2)}) copy-start(f32[192]{0:T(256)} %param.30) | copy-start | bytes 2308
  94.4 3.0 %copy-start.2 = (f32[2048,192]{0,1:T(8,128)S(1)}, f32[2048,192]{0,1:T(8,128)}, u32[]{:S(2)}) copy-start(f32[2048,192]{0,1:T(8,128)} %copy.75) | copy-start | bytes 4718596
  94.4 3.0 %copy-start.22 = (bf16[192,192]{1,0:T(8,128)(2,1)S(1)}, bf16[192,192]{1,0:T(8,128)(2,1)}, u32[]{:S(2)}) copy-start(bf16[192,192]{1,0:T(8,128)(2,1)} %param.28) | copy-start | bytes 221188
  100.0 2.0 %copy-start.8 = (bf16[384,192]{0,1:T(8,128)(2,1)S(1)}, bf16[384,192]{0,1:T(8,128)(2,1)}, u32[]{:S(2)}) copy-start(bf16[384,192]{0,1:T(8,128)(2,1)} %param.29) | copy-start | bytes 442372
  100.0 2.0 %copy-start.9 = (f32[256,192]{0,1:T(8,128)S(1)}, f32[256,192]{0,1:T(8,128)}, u32[]{:S(2)}) copy-start(f32[256,192]{0,1:T(8,128)} %fusion.71) | copy-start | bytes 589828
  100.0 2.0 %copy-start.24 = (bf16[192,192]{1,0:T(8,128)(2,1)S(1)}, bf16[192,192]{1,0:T(8,128)(2,1)}, u32[]{:S(2)}) copy-start(bf16[192,192]{1,0:T(8,128)(2,1)} %param.31) | copy-start | bytes 221188
  100.5 2.1 %copy-start.19 = (f32[192]{0:T(256)S(1)}, f32[192]{0:T(256)}, u32[]{:S(2)}) copy-start(f32[192]{0:T(256)} %param.32) | copy-start | bytes 2308
  102.1 1.2 copy-start.20
  102.9 14.3 %copy-start.11 = (bf16[192,192]{1,0:T(8,128)(2,1)S(1)}, bf16[192,192]{1,0:T(8,128)(2,1)}, u32[]{:S(2)}) copy-start(bf16[192,192]{1,0:T(8,128)(2,1)} %param.34) | copy-start | bytes 221188
  104.2 13.7 %copy-start.12 = (bf16[192,192]{1,0:T(8,128)(2,1)S(1)}, bf16[192,192]{1,0:T(8,128)(2,1)}, u32[]{:S(2)}) copy-start(bf16[192,192]{1,0:T(8,128)(2,1)} %param.35) | copy-start | bytes 221188
  104.2 12.5 %all-to-all-start.1 = ((bf16[8,32,2,192]{3,1,2,0:T(8,128)(2,1)}), bf16[8,32,2,192]{3,1,2,0:T(8,128)(2,1)S(1)}, u32[]{:S(2)}, u32[]{:S(2)}) async-start(bf16[8,32,2,192]{3,1,2,0:T(8,128)(2,1)} %copy.80), calls=%async_computation.1 | async-start | bytes 524288 | tf_op jit(solution)/shard_map/all_to_all | solution.py:129
  117.5 1.2 copy-start.13
  122.6 12.2 %copy-start.25 = (bf16[192,192]{1,0:T(8,128)(2,1)S(1)}, bf16[192,192]{1,0:T(8,128)(2,1)}, u32[]{:S(2)}) copy-start(bf16[192,192]{1,0:T(8,128)(2,1)} %param.37) | copy-start | bytes 221188
  123.9 10.9 %all-to-all-start.3 = ((bf16[1,32,16,192]{3,1,0,2:T(8,128)(2,1)}), bf16[1,32,16,192]{3,1,0,2:T(8,128)(2,1)S(1)}, u32[]{:S(2)}, u32[]{:S(2)}) async-start(bf16[1,32,16,192]{3,1,0,2:T(8,128)(2,1)} %reshape.197), calls=%async_computation.3 | async-start | bytes 524288 | tf_op jit(solution)/shard_map/all_to_all | solution.py:138
where the time goes:
time: 138 us; the launch traced here: 136 us
  local copies, waits for them, and re-layouts  57.8 us (42%)
  waiting for transfers between devices  26.5 us (19%)
  starting transfers between devices  24.5 us (18%)
  matrix products  24.3 us (18%)
  other arithmetic  2.13 us (2%)
    gather x4, local copies, waits for them, and re-layouts, per_device(): sender_proj[edge_sender] + receiver_proj[receiver_index] + edge_base  23.1 us
    gather x4, local copies, waits for them, and re-layouts, per_device(): receiver_proj[receiver_index]  16.9 us
    all_to_all x1, starting transfers between devices, per_device(): lax.all_to_all(node_state[halo_rows], 'patch', split_axis=0, concat_axis=...  11.9 us
    all_to_all x1, waiting for transfers between devices, per_device(): lax.all_to_all(node_state[halo_rows], 'patch', split_axis=0, concat_axis=...  11.7 us
    gather x2, local copies, waits for them, and re-layouts, per_device(): node_state[halo_rows]  8.06 us
    all_to_all x1, waiting for transfers between devices, per_device(): lax.all_to_all(outgoing_cols, 'lev', split_axis=0, concat_axis=2, tiled=T...  7.41 us
    all_to_all x1, waiting for transfers between devices, per_device(): lax.all_to_all(attended_cols[None], 'lev', split_axis=2, concat_axis=0, t...  7.38 us
    dot_general x2, matrix products, per_device(): jnp.dot(edge_hidden, edge_w_out, preferred_element_type=jnp.float32)  5.11 us
  transfers between devices with their start and end apart: 4, of which 3 were waited for; matrix products, arithmetic and copies ran while one was open for 49% of the time, Pallas kernels for 0%

commit v1 on v0

v1 whole, which is shorter than its diff:
```python
import math

import jax
import jax.numpy as jnp
from jax import lax
from jax.experimental import pallas as pl
from jax.experimental.pallas import tpu as pltpu
from jax.sharding import PartitionSpec as P

HEADS = 4
BF16 = jnp.bfloat16
F32 = jnp.float32
VMEM_BYTES = 48 * 1024 * 1024


def dot(a, b):
    return jnp.dot(a, b, preferred_element_type=F32)


def silu(v):
    return v / (1.0 + jnp.exp(-v))


def normalize(values):
    centered = values - jnp.mean(values, axis=-1, keepdims=True)
    spread = jnp.mean(centered * centered, axis=-1, keepdims=True)
    return centered * lax.rsqrt(spread + 1e-05)


def onehot(column, width):
    lanes = lax.broadcasted_iota(jnp.int32, (column.shape[0], width), 1).astype(F32)
    return jnp.where(column == lanes, 1.0, 0.0).astype(BF16)


def level_pair(merged, weight):
    depth, width = weight.shape
    half = merged.shape[1] // 2
    cut = half // 128 * 128
    filler = jnp.zeros((half - cut, width), weight.dtype)
    first = jnp.concatenate([weight, filler], axis=0)
    second = jnp.concatenate([filler, weight], axis=0)
    return (
        dot(merged[:, : half + half - cut], first),
        dot(merged[:, cut:], second),
    )


def merge_levels(first, second):
    return jnp.concatenate([first, second], axis=1)


def halo_kernel(halo_ref, own_ref, out_ref, pick_ref):
    patch_count, slot_count = halo_ref.shape
    columns = halo_ref[...].astype(F32).T
    for patch in range(patch_count):
        pick_ref[patch * slot_count : (patch + 1) * slot_count, :] = onehot(
            columns[:, patch : patch + 1], own_ref.shape[0]
        )
    out_ref[...] = dot(pick_ref[...], own_ref[...]).astype(BF16)


def local_kernel(
    sender_ref, receiver_ref, attr_ref, own_ref, w_in_ref, bias_ref, pre0_ref, pre1_ref, deliver_ref
):
    tile_count, tile = sender_ref.shape
    width = attr_ref.shape[1]
    node_dev = own_ref.shape[0]
    own = own_ref[...]
    sender_columns = sender_ref[...].astype(F32).T
    receiver_columns = receiver_ref[...].astype(F32).T
    w_send = w_in_ref[0:width, :]
    w_recv = w_in_ref[width : 2 * width, :]
    w_attr = w_in_ref[2 * width : 3 * width, :]
    for index in range(tile_count):
        rows = slice(index * tile, (index + 1) * tile)
        base = dot(attr_ref[rows, :], w_attr) + bias_ref[...]
        send_rows = dot(onehot(sender_columns[:, index : index + 1], node_dev), own).astype(BF16)
        recv_rows = dot(onehot(receiver_columns[:, index : index + 1], node_dev), own).astype(BF16)
        send0, send1 = level_pair(send_rows, w_send)
        recv0, recv1 = level_pair(recv_rows, w_recv)
        pre0_ref[rows, :] = base + send0 + recv0
        pre1_ref[rows, :] = base + send1 + recv1
        nodes = lax.broadcasted_iota(jnp.int32, (node_dev, tile), 0)
        deliver_ref[:, rows] = jnp.where(
            nodes == receiver_ref[index : index + 1, :], 1.0, 0.0
        ).astype(BF16)


def edge_kernel(
    sender_ref,
    pre0_ref,
    pre1_ref,
    deliver_ref,
    remote_ref,
    own_ref,
    w_in_ref,
    w_out_ref,
    node_w_in_ref,
    node_bias_ref,
    node_w_out_ref,
    node_gain_ref,
    attention_gain_ref,
    state_ref,
    normed_ref,
    message0_ref,
    message1_ref,
):
    tile_count, tile = sender_ref.shape
    node_dev = own_ref.shape[0]
    width = w_out_ref.shape[0]
    remote = remote_ref[...]
    w_send = w_in_ref[0:width, :]
    w_out = w_out_ref[...]
    columns = (sender_ref[...] - node_dev).astype(F32).T
    for index in range(tile_count):
        rows = slice(index * tile, (index + 1) * tile)
        send_rows = dot(
            onehot(columns[:, index : index + 1], remote.shape[0]), remote
        ).astype(BF16)
        send0, send1 = level_pair(send_rows, w_send)
        hidden0 = silu(pre0_ref[rows, :] + send0).astype(BF16)
        hidden1 = silu(pre1_ref[rows, :] + send1).astype(BF16)
        message0_ref[rows, :] = dot(hidden0, w_out).astype(BF16)
        message1_ref[rows, :] = dot(hidden1, w_out).astype(BF16)
    deliver = deliver_ref[...]
    own = own_ref[...]
    own_pair = level_pair(own, node_w_in_ref[0:width, :])
    own_values = (own[:, :width], own[:, width:])
    states = []
    normed = []
    for level, message_ref in enumerate((message0_ref, message1_ref)):
        summed = dot(deliver, message_ref[...]).astype(BF16)
        node_pre = (
            own_pair[level] + dot(summed, node_w_in_ref[width : 2 * width, :]) + node_bias_ref[...]
        )
        update = dot(silu(node_pre).astype(BF16), node_w_out_ref[...])
        state = (
            own_values[level].astype(F32) + node_gain_ref[...] * normalize(update)
        ).astype(BF16)
        states.append(state)
        normed.append(
            (attention_gain_ref[...] * normalize(state.astype(F32))).astype(BF16)
        )
    state_ref[...] = merge_levels(*states)
    normed_ref[...] = merge_levels(*normed)


def attention_kernel(
    rows_ref, bias_ref, query_ref, key_ref, value_ref, out_ref
):
    group_count, item_count, merged = rows_ref.shape
    width = merged // 2
    head_width = width // HEADS
    scale = 1.0 / math.sqrt(head_width)
    chunk = 16
    half = group_count * chunk
    total = 2 * half
    head_of = lax.broadcasted_iota(jnp.int32, (1, width), 1) // head_width
    row_node = lax.broadcasted_iota(jnp.int32, (total, total), 0) % chunk
    col_node = lax.broadcasted_iota(jnp.int32, (total, total), 1) % chunk
    same_node = row_node == col_node
    for part in range(item_count // chunk):
        items = slice(part * chunk, (part + 1) * chunk)
        merged_rows = rows_ref[:, items, :].reshape(half, merged)

        def project(weight_ref):
            pair = level_pair(merged_rows, weight_ref[...])
            return jnp.concatenate([p.astype(BF16) for p in pair], axis=0)

        queries, keys, values = project(query_ref), project(key_ref), project(value_ref)
        bias = jnp.where(same_node, bias_ref[part], -1e30)
        attended = jnp.zeros((total, width), F32)
        for head in range(HEADS):
            in_head = head_of == head
            head_keys = jnp.where(in_head, keys, 0.0).astype(BF16)
            head_values = jnp.where(in_head, values, 0.0).astype(BF16)
            scores = lax.dot_general(
                queries, head_keys, (((1,), (1,)), ((), ())), preferred_element_type=F32
            )
            scores = scores * scale + bias
            powers = jnp.exp(scores - jnp.max(scores, axis=-1, keepdims=True))
            weights = powers / jnp.sum(powers, axis=-1, keepdims=True)
            attended = attended + dot(weights.astype(BF16), head_values)
        attended = attended.astype(BF16)
        out_ref[:, items, :] = merge_levels(attended[:half], attended[half:]).reshape(
            group_count, chunk, merged
        )


def output_kernel(state_ref, attended_ref, live_ref, weight_ref, out_ref):
    width = weight_ref.shape[0]
    mixed = level_pair(attended_ref[...], weight_ref[...])
    state = state_ref[...].astype(F32)
    for level in range(2):
        kept = mixed[level] * live_ref[:, level : level + 1]
        out_ref[level] = (state[:, level * width : (level + 1) * width] + kept).astype(BF16)


def call(kernel, out_shape, *operands, scratch=()):
    return pl.pallas_call(
        kernel,
        out_shape=out_shape,
        scratch_shapes=list(scratch),
        compiler_params=pltpu.CompilerParams(vmem_limit_bytes=VMEM_BYTES),
    )(*operands)


def shape(dims, dtype=BF16):
    return jax.ShapeDtypeStruct(dims, dtype)


def per_device(
    node_state,
    edge_attr,
    edge_sender,
    edge_receiver,
    tile_block,
    halo_rows,
    valid_levels,
    edge_w_in,
    edge_bias,
    edge_w_out,
    node_w_in,
    node_bias,
    node_w_out,
    node_gain,
    attention_gain,
    query_weight,
    key_weight,
    value_weight,
    output_weight,
):
    group_count = lax.axis_size("lev")
    node_dev, lev_dev, width = node_state.shape
    tile_count = tile_block.shape[0]
    patch_count, slot_count = halo_rows.shape
    merged = lev_dev * width
    own = node_state.reshape(node_dev, merged)
    outgoing = call(
        halo_kernel,
        shape((patch_count * slot_count, merged)),
        halo_rows,
        own,
        scratch=[pltpu.VMEM((patch_count * slot_count, node_dev), BF16)],
    )
    incoming = lax.all_to_all(
        outgoing.reshape(patch_count, slot_count, merged),
        "patch",
        split_axis=0,
        concat_axis=0,
        tiled=True,
    ).reshape(patch_count * slot_count, merged)

    senders = edge_sender.reshape(tile_count, 128)
    in_block = edge_receiver.reshape(tile_count, 128)
    receivers = jnp.where(in_block >= 0, tile_block[:, None] * 128 + in_block, -1)
    edge_count = edge_attr.shape[0]
    pre0, pre1, deliver = call(
        local_kernel,
        (
            shape((edge_count, width), F32),
            shape((edge_count, width), F32),
            shape((node_dev, edge_count)),
        ),
        senders,
        receivers,
        edge_attr,
        own,
        edge_w_in,
        edge_bias[None, :],
    )
    state, normed = call(
        edge_kernel,
        (shape((node_dev, merged)), shape((node_dev, merged))),
        senders,
        pre0,
        pre1,
        deliver,
        incoming,
        own,
        edge_w_in,
        edge_w_out,
        node_w_in,
        node_bias[None, :],
        node_w_out,
        node_gain[None, :],
        attention_gain[None, :],
        scratch=[
            pltpu.VMEM((edge_count, width), BF16),
            pltpu.VMEM((edge_count, width), BF16),
        ],
    )
    per_group = node_dev // group_count
    chunk = 16
    me = lax.axis_index("lev")
    mine = lax.dynamic_slice_in_dim(valid_levels, me * per_group, per_group)
    level_of = (
        jnp.arange(group_count, dtype=jnp.int32)[None, :, None] * lev_dev
        + jnp.arange(lev_dev, dtype=jnp.int32)[:, None, None]
    )
    key_bias = jnp.where(
        level_of[None] < mine.reshape(per_group // chunk, 1, 1, chunk), 0.0, -1e30
    ).reshape(per_group // chunk, 1, lev_dev * group_count * chunk)
    columns = lax.all_to_all(
        normed.reshape(group_count, per_group, merged),
        "lev",
        split_axis=0,
        concat_axis=0,
        tiled=True,
    )
    attended = call(
        attention_kernel,
        shape((group_count, per_group, merged)),
        columns,
        key_bias,
        query_weight,
        key_weight,
        value_weight,
    )
    returned = lax.all_to_all(
        attended, "lev", split_axis=0, concat_axis=0, tiled=True
    ).reshape(node_dev, merged)
    levels = me * lev_dev + jnp.arange(lev_dev, dtype=jnp.int32)
    live = (levels[None, :] < valid_levels[:, None]).astype(F32)
    out = call(
        output_kernel,
        shape((lev_dev, node_dev, width)),
        state,
        returned,
        live,
        output_weight,
    )
    return out.transpose(1, 0, 2)


def solution(mesh):
    in_specs = (
        P("patch", "lev", None),
        P("patch", None),
        P("patch"),
        P("patch"),
        P("patch"),
        P("patch", None),
        P("patch"),
    ) + (P(),) * 12
    out_specs = P("patch", "lev", None)
    return jax.shard_map(
        per_device, mesh=mesh, in_specs=in_specs, out_specs=out_specs, check_vma=False
    )
```

time: 138 us -> 90.3 us (0.65)
  local copies, waits for them, and re-layouts: 57.8 us -> 11.8 us
  matrix products: 24.3 us -> 0 us
  Pallas kernels: 0 us -> 23.7 us
  waiting for transfers between devices: 26.5 us -> 34 us
  starting transfers between devices: 24.5 us -> 19.5 us
  other arithmetic: 2.13 us -> 0.19 us
    gather x10 -> x0, local copies, waits for them, and re-layouts: 48 us -> none  [the longest x4 23.1 us: per_device(): sender_proj[edge_sender] + receiver_proj[receiver_index] + edge_base]
    pallas_call x0 -> x5, Pallas kernels: none -> 23.7 us  [call(): pl.pallas_call(kernel, out_shape=out_shape, scratch_shapes=list(scratch),...]
    dot_general x20 -> x0, matrix products: 22.6 us -> none  [the longest x2 5.11 us: per_device(): jnp.dot(edge_hidden, edge_w_out, preferred_element_type=jnp.float32)]
    unnamed x55 -> x45, local copies, waits for them, and re-layouts: 1.32 us -> 9.43 us
    all_to_all x4 -> x3, waiting for transfers between devices: 26.5 us -> 34 us  [the longest x1 20.5 us: per_device(): lax.all_to_all(outgoing.reshape(patch_count, slot_count, merged), 'patch'...]
    all_to_all x4 -> x3, starting transfers between devices: 24.5 us -> 19.5 us  [the longest x1 11.8 us: per_device(): lax.all_to_all(outgoing.reshape(patch_count, slot_count, merged), 'patch'...]
    slice x1 -> x0, local copies, waits for them, and re-layouts: 2.49 us -> none  [per_device(): incoming_rows[:, :, level_index]]
    another operation x5 -> x0, local copies, waits for them, and re-layouts: 2.13 us -> none  [the longest x2 1.26 us: per_device(): attended_cols[None]]
  transfers between devices with their start and end apart: 4 -> 3, of which waited for: 3 -> 3; matrix products, arithmetic and copies ran while one was open for 49% -> 3% of each run, Pallas kernels for 0% -> 6%
where the time goes in v1:
time: 90.3 us; the launch traced here: 89.4 us
  waiting for transfers between devices  34 us (38%)
  Pallas kernels  23.7 us (26%)
  starting transfers between devices  19.5 us (22%)
  local copies, waits for them, and re-layouts  11.8 us (13%)
    pallas_call x5, Pallas kernels, call(): pl.pallas_call(kernel, out_shape=out_shape, scratch_shapes=list(scratch),...  23.7 us
    all_to_all x1, waiting for transfers between devices, per_device(): lax.all_to_all(outgoing.reshape(patch_count, slot_count, merged), 'patch'...  20.5 us
    all_to_all x1, starting transfers between devices, per_device(): lax.all_to_all(outgoing.reshape(patch_count, slot_count, merged), 'patch'...  11.8 us
    unnamed x45, local copies, waits for them, and re-layouts  9.43 us
    all_to_all x1, waiting for transfers between devices, per_device(): lax.all_to_all(normed.reshape(group_count, per_group, merged), 'lev', spl...  6.83 us
    all_to_all x1, waiting for transfers between devices, per_device(): lax.all_to_all(attended, 'lev', split_axis=0, concat_axis=0, tiled=True)  6.65 us
    all_to_all x1, starting transfers between devices, per_device(): lax.all_to_all(normed.reshape(group_count, per_group, merged), 'lev', spl...  4.3 us
    all_to_all x1, starting transfers between devices, per_device(): lax.all_to_all(attended, 'lev', split_axis=0, concat_axis=0, tiled=True)  3.39 us
  transfers between devices with their start and end apart: 3, of which 3 were waited for; matrix products, arithmetic and copies ran while one was open for 3% of the time, Pallas kernels for 6%

profile of v1, /device:TPU:8, one launch (start us, length us, event | category | flops | bytes accessed | tf_op | source)
XLA Modules:
  0.0 89.4 jit_solution(9664580810048675376)
XLA Ops:
  0.0 1.1 %copy.35.own_ref = bf16[256,384]{1,0:T(8,128)(2,1)S(1)} copy(bf16[256,384]{0,1:T(8,128)(2,1)} %bitcast.29) | data formatting | bytes 393216 | tf_op jit(solution)/shard_map/reshape | solution.py:238
  1.1 0.0 copy-start.11
  1.1 0.7 copy-done.11
  1.9 1.8 %shard_map.182 = bf16[1536,384]{1,0:T(8,128)(2,1)} custom-call(s32[32,48]{1,0:T(8,128)S(1)} %copy-done.11, bf16[256,384]{1,0:T(8,128)(2,1)S(1)} %copy.35.own_ref), custom_call_target="tpu_custom_call" | custom-call | tf_op jit(solution)/shard_map/pallas_call | solution.py:200
  3.6 0.0 copy-start.10
  3.6 0.0 copy-start.15
  3.6 11.8 %all-to-all-start = ((bf16[32,48,384]{2,1,0:T(8,128)(2,1)}), bf16[32,48,384]{2,1,0:T(8,128)(2,1)S(1)}, u32[]{:S(2)}, u32[]{:S(2)}) async-start(bf16[32,48,384]{2,1,0:T(8,128)(2,1)} %bitcast.4), calls=%async_computation | async-start | bytes 2359296 | tf_op jit(solution)/shard_map/all_to_all | solution.py:246
  15.5 0.0 copy-done.16
  15.5 0.0 copy-start.4
  15.5 0.0 copy-start.5
  15.5 0.0 copy-start.12
  15.5 0.0 copy-start.13
  15.6 0.0 copy-start.14
  15.6 0.2 copy.36.w_in_ref
  15.7 1.4 %copy.34.attr_ref = bf16[2048,192]{1,0:T(8,128)(2,1)S(1)} copy(bf16[2048,192]{0,1:T(8,128)(2,1)} %param.20) | data formatting | bytes 1572864 | tf_op args[1]
  17.2 0.0 copy-done.17
  17.2 0.1 copy.40.node_w_in_ref
  17.3 0.0 copy-done.19
  17.4 0.1 dynamic_slice.3
  17.4 0.1 lt.48
  17.5 0.1 lt.50
  17.6 0.1 lt.44
  17.7 0.1 lt.45
  17.8 0.0 copy-done.20
  17.8 0.0 copy-done.18
  17.8 0.1 fusion.receiver_ref
  17.9 0.0 copy-done.10
  17.9 0.0 copy-done.15
  17.9 5.7 %shard_map.181 = (f32[2048,192]{1,0:T(8,128)S(1)}, f32[2048,192]{1,0:T(8,128)}, bf16[256,2048]{1,0:T(8,128)(2,1)S(1)}) custom-call(s32[16,128]{1,0:T(8,128)S(1)} %bitcast.23, s32[16,128]{1,0:T(8,128)S(1)} %fusion.receiver_ref, bf16[2048,192]{1,0:T(8,128)(2,1)S(1)} %copy.34.attr_ref, bf16[256,384]{1,0:T(8,128)(2,1)S(1)} %copy.35.own_ref, ...), custom_call_target="tpu_custom_call" | custom-call | tf_op jit(solution)/shard_map/pallas_call | solution.py:200
  23.6 1.3 %copy-done = f32[2048,192]{1,0:T(8,128)} copy-done((f32[2048,192]{1,0:T(8,128)}, f32[2048,192]{1,0:T(8,128)S(1)}, u32[]{:S(2)}) %copy-start) | copy-done | bytes 1572888
  24.9 1.0 %copy-done.2 = bf16[256,2048]{1,0:T(8,128)(2,1)} copy-done((bf16[256,2048]{1,0:T(8,128)(2,1)}, bf16[256,2048]{1,0:T(8,128)(2,1)S(1)}, u32[]{:S(2)}) %copy-start.2) | copy-done | bytes 1048600
  25.9 20.5 %all-to-all-done = bf16[32,48,384]{2,1,0:T(8,128)(2,1)S(1)} async-done(((bf16[32,48,384]{2,1,0:T(8,128)(2,1)}), bf16[32,48,384]{2,1,0:T(8,128)(2,1)S(1)}, u32[]{:S(2)}, u32[]{:S(2)}) %all-to-all-start) | async-done | bytes 1179680 | tf_op jit(solution)/shard_map/all_to_all | solution.py:246
  46.4 0.0 copy-done.4
  46.4 0.0 copy-done.12
  46.4 1.6 %copy-done.1 = f32[2048,192]{1,0:T(8,128)S(1)} copy-done((f32[2048,192]{1,0:T(8,128)S(1)}, f32[2048,192]{1,0:T(8,128)}, u32[]{:S(2)}) %copy-start.1) | copy-done | bytes 1572888
  48.0 1.2 %copy-done.3 = bf16[256,2048]{1,0:T(8,128)(2,1)S(1)} copy-done((bf16[256,2048]{1,0:T(8,128)(2,1)S(1)}, bf16[256,2048]{1,0:T(8,128)(2,1)}, u32[]{:S(2)}) %copy-start.3) | copy-done | bytes 1048600
  49.2 13.3 %shard_map.183 = (bf16[256,384]{1,0:T(8,128)(2,1)S(1)}, bf16[256,384]{1,0:T(8,128)(2,1)}) custom-call(s32[16,128]{1,0:T(8,128)S(1)} %bitcast.24, f32[2048,192]{1,0:T(8,128)S(1)} %copy-done.1, f32[2048,192]{1,0:T(8,128)} %get-tuple-element.11.pre1_ref, bf16[256,2048]{1,0:T(8,128)(2,1)S(1)} %copy-done.3, bf16[1536,384]{1,0:T(8,128)(2,1)S(1)} %bitcast.20, ...), custom_call_target="tpu_custom_call" | custom-call | tf_op jit(solution)/shard_map/pallas_call | solution.py:200
  62.5 4.3 %all-to-all-start.1 = ((bf16[8,32,384]{2,1,0:T(8,128)(2,1)}), bf16[8,32,384]{2,1,0:T(8,128)(2,1)S(1)}, u32[]{:S(2)}, u32[]{:S(2)}) async-start(bf16[8,32,384]{2,1,0:T(8,128)(2,1)} %bitcast.9), calls=%async_computation.1 | async-start | bytes 393216 | tf_op jit(solution)/shard_map/all_to_all | solution.py:304
  66.8 6.8 %all-to-all-done.1.rows_ref = bf16[8,32,384]{2,1,0:T(8,128)(2,1)S(1)} async-done(((bf16[8,32,384]{2,1,0:T(8,128)(2,1)}), bf16[8,32,384]{2,1,0:T(8,128)(2,1)S(1)}, u32[]{:S(2)}, u32[]{:S(2)}) %all-to-all-start.1) | async-done | bytes 196640 | tf_op jit(solution)/shard_map/all_to_all | solution.py:304
  73.7 0.0 copy-done.7
  73.7 0.9 copy-done.8
  74.6 0.9 copy-done.9
  75.4 2.6 %shard_map.184 = bf16[8,32,384]{2,1,0:T(8,128)(2,1)} custom-call(bf16[8,32,384]{2,1,0:T(8,128)(2,1)S(1)} %all-to-all-done.1.rows_ref, f32[2,1,256]{2,1,0:T(1,128)S(1)} %compare_select_fusion.bias_ref, bf16[192,192]{1,0:T(8,128)(2,1)S(1)} %copy-done.7, bf16[192,192]{1,0:T(8,128)(2,1)S(1)} %copy-done.8, bf16[192,192]{1,0:T(8,128)(2,1)S(1)} %copy-done.9), custom_call_target="tpu_custom_call" | custom-call | tf_op jit(solution)/shard_map/pallas_call | solution.py:200
  78.0 3.4 %all-to-all-start.2 = ((bf16[8,32,384]{2,1,0:T(8,128)(2,1)}), bf16[8,32,384]{2,1,0:T(8,128)(2,1)S(1)}, u32[]{:S(2)}, u32[]{:S(2)}) async-start(bf16[8,32,384]{2,1,0:T(8,128)(2,1)} %shard_map.184), calls=%async_computation.2 | async-start | bytes 393216 | tf_op jit(solution)/shard_map/all_to_all | solution.py:320
  81.4 0.1 compare_convert_fusion.live_ref
  81.5 6.6 %all-to-all-done.2 = bf16[8,32,384]{2,1,0:T(8,128)(2,1)S(1)} async-done(((bf16[8,32,384]{2,1,0:T(8,128)(2,1)}), bf16[8,32,384]{2,1,0:T(8,128)(2,1)S(1)}, u32[]{:S(2)}, u32[]{:S(2)}) %all-to-all-start.2) | async-done | bytes 196640 | tf_op jit(solution)/shard_map/all_to_all | solution.py:320
  88.2 0.4 shard_map.185
  88.6 0.8 copy.42
  (23 shorter events, 0.1 us)
Async XLA Ops:
  0.0 15.5 %copy-start.16 = (bf16[576,192]{0,1:T(8,128)(2,1)S(1)}, bf16[576,192]{0,1:T(8,128)(2,1)}, u32[]{:S(2)}) copy-start(bf16[576,192]{0,1:T(8,128)(2,1)} %param.26) | copy-start | bytes 663556
  1.1 0.7 copy-start.11
  3.6 13.6 %copy-start.17 = (bf16[384,192]{0,1:T(8,128)(2,1)S(1)}, bf16[384,192]{0,1:T(8,128)(2,1)}, u32[]{:S(2)}) copy-start(bf16[384,192]{0,1:T(8,128)(2,1)} %param.29) | copy-start | bytes 442372
  3.6 13.7 %copy-start.19 = (s32[256]{0:T(256)S(1)}, s32[256]{0:T(256)}, u32[]{:S(2)}) copy-start(s32[256]{0:T(256)} %param.25) | copy-start | bytes 3076
  3.6 14.2 %copy-start.20 = (s32[16]{0:T(128)S(1)}, s32[16]{0:T(128)}, u32[]{:S(2)}) copy-start(s32[16]{0:T(128)} %param.23) | copy-start | bytes 196
  3.6 14.2 %copy-start.18 = (s32[2048]{0:T(1024)S(1)}, s32[2048]{0:T(1024)}, u32[]{:S(2)}) copy-start(s32[2048]{0:T(1024)} %param.22) | copy-start | bytes 24580
  3.6 14.2 %copy-start.10 = (s32[2048]{0:T(1024)S(1)}, s32[2048]{0:T(1024)}, u32[]{:S(2)}) copy-start(s32[2048]{0:T(1024)} %param.21) | copy-start | bytes 24580
  3.6 14.2 %copy-start.15 = (f32[192]{0:T(256)S(1)}, f32[192]{0:T(256)}, u32[]{:S(2)}) copy-start(f32[192]{0:T(256)} %param.27) | copy-start | bytes 2308
  3.6 42.7 %all-to-all-start = ((bf16[32,48,384]{2,1,0:T(8,128)(2,1)}), bf16[32,48,384]{2,1,0:T(8,128)(2,1)S(1)}, u32[]{:S(2)}, u32[]{:S(2)}) async-start(bf16[32,48,384]{2,1,0:T(8,128)(2,1)} %bitcast.4), calls=%async_computation | async-start | bytes 2359296 | tf_op jit(solution)/shard_map/all_to_all | solution.py:246
  15.5 30.9 %copy-start.4 = (bf16[192,192]{1,0:T(8,128)(2,1)S(1)}, bf16[192,192]{1,0:T(8,128)(2,1)}, u32[]{:S(2)}) copy-start(bf16[192,192]{1,0:T(8,128)(2,1)} %w_out_ref.1) | copy-start | bytes 221188
  15.5 30.9 %copy-start.5 = (bf16[192,192]{1,0:T(8,128)(2,1)S(1)}, bf16[192,192]{1,0:T(8,128)(2,1)}, u32[]{:S(2)}) copy-start(bf16[192,192]{1,0:T(8,128)(2,1)} %node_w_out_ref.1) | copy-start | bytes 221188
  15.5 30.8 %copy-start.12 = (f32[192]{0:T(256)S(1)}, f32[192]{0:T(256)}, u32[]{:S(2)}) copy-start(f32[192]{0:T(256)} %param.30) | copy-start | bytes 2308
  15.5 30.8 %copy-start.13 = (f32[192]{0:T(256)S(1)}, f32[192]{0:T(256)}, u32[]{:S(2)}) copy-start(f32[192]{0:T(256)} %param.32) | copy-start | bytes 2308
  15.6 30.8 %copy-start.14 = (f32[192]{0:T(256)S(1)}, f32[192]{0:T(256)}, u32[]{:S(2)}) copy-start(f32[192]{0:T(256)} %param.33) | copy-start | bytes 2308
  23.6 1.3 %copy-start = (f32[2048,192]{1,0:T(8,128)}, f32[2048,192]{1,0:T(8,128)S(1)}, u32[]{:S(2)}) copy-start(f32[2048,192]{1,0:T(8,128)S(1)} %get-tuple-element.10.pre0_ref) | copy-start | bytes 4718596
  24.9 1.0 %copy-start.2 = (bf16[256,2048]{1,0:T(8,128)(2,1)}, bf16[256,2048]{1,0:T(8,128)(2,1)S(1)}, u32[]{:S(2)}) copy-start(bf16[256,2048]{1,0:T(8,128)(2,1)S(1)} %get-tuple-element.12.deliver_ref) | copy-start | bytes 3145732
  46.4 1.6 %copy-start.1 = (f32[2048,192]{1,0:T(8,128)S(1)}, f32[2048,192]{1,0:T(8,128)}, u32[]{:S(2)}) copy-start(f32[2048,192]{1,0:T(8,128)} %copy-done) | copy-start | bytes 4718596
  48.0 1.2 %copy-start.3 = (bf16[256,2048]{1,0:T(8,128)(2,1)S(1)}, bf16[256,2048]{1,0:T(8,128)(2,1)}, u32[]{:S(2)}) copy-start(bf16[256,2048]{1,0:T(8,128)(2,1)} %copy-done.2) | copy-start | bytes 3145732
  49.2 24.4 %copy-start.7 = (bf16[192,192]{1,0:T(8,128)(2,1)S(1)}, bf16[192,192]{1,0:T(8,128)(2,1)}, u32[]{:S(2)}) copy-start(bf16[192,192]{1,0:T(8,128)(2,1)} %query_ref.1) | copy-start | bytes 221188
  49.2 38.9 %copy-start.6 = (bf16[192,192]{1,0:T(8,128)(2,1)S(1)}, bf16[192,192]{1,0:T(8,128)(2,1)}, u32[]{:S(2)}) copy-start(bf16[192,192]{1,0:T(8,128)(2,1)} %weight_ref.1) | copy-start | bytes 221188
  62.5 11.1 %all-to-all-start.1 = ((bf16[8,32,384]{2,1,0:T(8,128)(2,1)}), bf16[8,32,384]{2,1,0:T(8,128)(2,1)S(1)}, u32[]{:S(2)}, u32[]{:S(2)}) async-start(bf16[8,32,384]{2,1,0:T(8,128)(2,1)} %bitcast.9), calls=%async_computation.1 | async-start | bytes 393216 | tf_op jit(solution)/shard_map/all_to_all | solution.py:304
  73.7 0.9 copy-start.8
  74.6 0.9 copy-start.9
  78.0 10.2 %all-to-all-start.2 = ((bf16[8,32,384]{2,1,0:T(8,128)(2,1)}), bf16[8,32,384]{2,1,0:T(8,128)(2,1)S(1)}, u32[]{:S(2)}, u32[]{:S(2)}) async-start(bf16[8,32,384]{2,1,0:T(8,128)(2,1)} %shard_map.184), calls=%async_computation.2 | async-start | bytes 393216 | tf_op jit(solution)/shard_map/all_to_all | solution.py:320

commit v2 on v1

v2 whole, which is shorter than its diff:
```python
import math

import jax
import jax.numpy as jnp
from jax import lax
from jax.experimental import pallas as pl
from jax.experimental.pallas import tpu as pltpu
from jax.sharding import PartitionSpec as P

HEADS = 4
BF16 = jnp.bfloat16
F32 = jnp.float32
VMEM_BYTES = 60 * 1024 * 1024
LATE_TILES = 6
LATE_STEP = 2


def dot(a, b):
    return jnp.dot(a, b, preferred_element_type=F32)


def dot_lanes(a, b):
    return lax.dot_general(a, b, (((1,), (1,)), ((), ())), preferred_element_type=F32)


def silu(v):
    return v / (1.0 + jnp.exp(-v))


def normalize(values):
    centered = values - jnp.mean(values, axis=-1, keepdims=True)
    spread = jnp.mean(centered * centered, axis=-1, keepdims=True)
    return centered * lax.rsqrt(spread + 1e-05)


def onehot(column, width):
    lanes = lax.broadcasted_iota(jnp.int32, (column.shape[0], width), 1).astype(F32)
    return jnp.where(column == lanes, 1.0, 0.0).astype(BF16)


def level_pair(merged, weight):
    depth, width = weight.shape
    half = merged.shape[1] // 2
    cut = half // 128 * 128
    filler = jnp.zeros((half - cut, width), weight.dtype)
    first = jnp.concatenate([weight, filler], axis=0)
    second = jnp.concatenate([filler, weight], axis=0)
    return (
        dot(merged[:, : half + half - cut], first),
        dot(merged[:, cut:], second),
    )


def merge_levels(first, second):
    return jnp.concatenate([first, second], axis=1)


def halo_kernel(halo_ref, own_ref, out_ref, pick_ref):
    patch_count, slot_count = halo_ref.shape
    columns = halo_ref[...].astype(F32).T
    for patch in range(patch_count):
        pick_ref[patch * slot_count : (patch + 1) * slot_count, :] = onehot(
            columns[:, patch : patch + 1], own_ref.shape[1]
        )
    out_ref[...] = dot_lanes(pick_ref[...], own_ref[...]).astype(BF16)


def running_count(flags):
    tile_count, tile = flags.shape
    flags = flags.astype(BF16)
    before = lax.broadcasted_iota(jnp.int32, (tile, tile), 0) < lax.broadcasted_iota(
        jnp.int32, (tile, tile), 1
    )
    above = lax.broadcasted_iota(jnp.int32, (tile_count, tile_count), 1) < lax.broadcasted_iota(
        jnp.int32, (tile_count, tile_count), 0
    )
    inside = dot(flags, jnp.where(before, 1.0, 0.0).astype(BF16))
    totals = dot(flags, jnp.ones((tile, tile), BF16)).astype(BF16)
    return (
        inside + dot(jnp.where(above, 1.0, 0.0).astype(BF16), totals),
        dot(jnp.ones((tile_count, tile_count), BF16), totals),
    )


def local_kernel(
    sender_ref,
    receiver_ref,
    attr_ref,
    own_ref,
    w_in_ref,
    bias_ref,
    w_out_ref,
    tiles_ref,
    pre0_ref,
    pre1_ref,
    wanted_ref,
    deliver_ref,
    sum0_ref,
    sum1_ref,
    own_rows_ref,
    position_ref,
    table_ref,
):
    tile_count, tile = sender_ref.shape
    width, edge_count = attr_ref.shape
    node_dev = own_ref.shape[1]
    eye = jnp.where(
        lax.broadcasted_iota(jnp.int32, (node_dev, node_dev), 0)
        == lax.broadcasted_iota(jnp.int32, (node_dev, node_dev), 1),
        1.0,
        0.0,
    ).astype(BF16)
    own_rows_ref[...] = dot_lanes(eye, own_ref[...]).astype(BF16)
    senders = sender_ref[...]
    receivers = receiver_ref[...]
    used = receivers >= 0
    is_remote = jnp.where(used & (senders >= node_dev), 1.0, 0.0)
    is_local = jnp.where(used & (senders < node_dev), 1.0, 0.0)
    is_empty = jnp.where(used, 0.0, 1.0)
    remote_rank, remote_total = running_count(is_remote)
    local_rank, local_total = running_count(is_local)
    empty_rank, _ = running_count(is_empty)
    position_ref[...] = jnp.where(
        is_remote > 0.0,
        remote_rank,
        jnp.where(
            is_local > 0.0, remote_total + local_rank, remote_total + local_total + empty_rank
        ),
    )
    remote_tiles = (jnp.sum(is_remote).astype(jnp.int32) + tile - 1) // tile
    used_tiles = (jnp.sum(1.0 - is_empty).astype(jnp.int32) + tile - 1) // tile
    late_tiles = jnp.maximum(remote_tiles, LATE_TILES)
    tiles_ref[0] = late_tiles
    table_ref[0:width, :] = attr_ref[...]
    table_ref[width:, :] = jnp.zeros((table_ref.shape[0] - width, edge_count), BF16)
    for index in range(tile_count):
        lanes = slice(index * tile, (index + 1) * tile)
        row = senders[index : index + 1, :]
        table_ref[width : width + 16, lanes] = jnp.concatenate(
            [
                (row // tile).astype(F32),
                (row % tile).astype(F32),
                receivers[index : index + 1, :].astype(F32),
                jnp.zeros((13, tile), F32),
            ],
            axis=0,
        ).astype(BF16)
    w_send = w_in_ref[0:width, :]
    w_recv = w_in_ref[width : 2 * width, :]
    w_attr = w_in_ref[2 * width : 3 * width, :]
    sum0_ref[...] = jnp.zeros_like(sum0_ref)
    sum1_ref[...] = jnp.zeros_like(sum1_ref)

    def arrange(index):
        wanted = lax.broadcasted_iota(jnp.int32, (tile, tile), 0).astype(F32) + (
            index * tile
        ).astype(F32)
        order = jnp.concatenate(
            [
                jnp.where(position_ref[t : t + 1, :] == wanted, 1.0, 0.0).astype(BF16)
                for t in range(tile_count)
            ],
            axis=1,
        )
        table = table_ref[...]
        moved = dot_lanes(order, table)
        receiver_row = dot_lanes(table[width : width + 16, :], order)[2:3, :]
        sender_column = moved[:, width : width + 1] * tile + moved[:, width + 1 : width + 2]
        receiver_column = moved[:, width + 2 : width + 3]
        own = own_rows_ref[...]
        send_rows = dot(onehot(sender_column, node_dev), own).astype(BF16)
        recv_rows = dot(onehot(receiver_column, node_dev), own).astype(BF16)
        base = dot(moved[:, :width].astype(BF16), w_attr) + bias_ref[...]
        send0, send1 = level_pair(send_rows, w_send)
        recv0, recv1 = level_pair(recv_rows, w_recv)
        nodes = lax.broadcasted_iota(jnp.int32, (node_dev, tile), 0).astype(F32)
        deliver = jnp.where(nodes == receiver_row, 1.0, 0.0).astype(BF16)
        return base + send0 + recv0, base + send1 + recv1, deliver, sender_column

    @pl.loop(0, late_tiles)
    def _(index):
        pre0, pre1, deliver, sender_column = arrange(index)
        rows = pl.ds(pl.multiple_of(index * tile, tile), tile)
        pre0_ref[rows, :] = pre0
        pre1_ref[rows, :] = pre1
        deliver_ref[index] = deliver
        wanted_ref[rows, :] = jnp.broadcast_to(sender_column - node_dev, (tile, 128))

    @pl.loop(late_tiles, jnp.maximum(used_tiles, late_tiles))
    def _(index):
        pre0, pre1, deliver, _ = arrange(index)
        w_out = w_out_ref[...]
        sum0_ref[...] += dot(deliver, dot(silu(pre0).astype(BF16), w_out).astype(BF16))
        sum1_ref[...] += dot(deliver, dot(silu(pre1).astype(BF16), w_out).astype(BF16))


def edge_kernel(
    tiles_ref,
    pre0_hbm,
    pre1_hbm,
    wanted_hbm,
    deliver_hbm,
    sum0_hbm,
    sum1_hbm,
    remote_hbm,
    own_hbm,
    w_in_hbm,
    w_out_hbm,
    node_w_in_hbm,
    node_bias_ref,
    node_w_out_hbm,
    node_gain_ref,
    attention_gain_ref,
    state_ref,
    normed_ref,
    pre0_ref,
    pre1_ref,
    wanted_ref,
    deliver_ref,
    total0_ref,
    total1_ref,
    remote_ref,
    own_ref,
    w_send_ref,
    w_out_ref,
    node_w_in_ref,
    node_w_out_ref,
    arrived,
):
    tile = deliver_ref.shape[2]
    width = w_out_ref.shape[0]
    late = LATE_TILES * tile
    fetches = [
        pltpu.make_async_copy(source, target, arrived.at[index])
        for index, (source, target) in enumerate(
            (
                (wanted_hbm.at[0:late], wanted_ref),
                (remote_hbm, remote_ref),
                (w_in_hbm.at[0:width], w_send_ref),
                (pre0_hbm.at[0:late], pre0_ref),
                (pre1_hbm.at[0:late], pre1_ref),
                (w_out_hbm, w_out_ref),
                (deliver_hbm.at[0:LATE_TILES], deliver_ref),
                (sum0_hbm, total0_ref),
                (sum1_hbm, total1_ref),
                (own_hbm, own_ref),
                (node_w_in_hbm, node_w_in_ref),
                (node_w_out_hbm, node_w_out_ref),
            )
        )
    ]
    for fetch in fetches:
        fetch.start()

    def messages(wanted, pre0, pre1):
        rows = wanted.shape[0]
        lanes = lax.broadcasted_iota(jnp.int32, (rows, 128), 1).astype(F32)
        pick = jnp.concatenate(
            [
                jnp.where(wanted == lanes + float(first), 1.0, 0.0).astype(BF16)
                for first in range(0, remote_ref.shape[0], 128)
            ],
            axis=1,
        )
        send_rows = dot(pick, remote_ref[...]).astype(BF16)
        send0, send1 = level_pair(send_rows, w_send_ref[...])
        hidden0 = silu(pre0 + send0).astype(BF16)
        hidden1 = silu(pre1 + send1).astype(BF16)
        w_out = w_out_ref[...]
        return dot(hidden0, w_out).astype(BF16), dot(hidden1, w_out).astype(BF16)

    for fetch in fetches[:9]:
        fetch.wait()
    total0, total1 = total0_ref[...], total1_ref[...]
    step = LATE_STEP
    for start in range(0, LATE_TILES, step):
        rows = slice(start * tile, (start + step) * tile)
        message0, message1 = messages(wanted_ref[rows, :], pre0_ref[rows, :], pre1_ref[rows, :])
        deliver = jnp.concatenate([deliver_ref[start + i] for i in range(step)], axis=1)
        total0 += dot(deliver, message0)
        total1 += dot(deliver, message1)
    total0_ref[...] = total0
    total1_ref[...] = total1

    @pl.loop(LATE_TILES, tiles_ref[0])
    def _(index):
        rows = pl.ds(pl.multiple_of(index * tile, tile), tile)
        tail = [
            pltpu.make_async_copy(source, target, arrived.at[slot])
            for slot, (source, target) in enumerate(
                (
                    (wanted_hbm.at[rows], wanted_ref.at[0:tile]),
                    (pre0_hbm.at[rows], pre0_ref.at[0:tile]),
                    (pre1_hbm.at[rows], pre1_ref.at[0:tile]),
                    (deliver_hbm.at[pl.ds(index, 1)], deliver_ref.at[0:1]),
                )
            )
        ]
        for fetch in tail:
            fetch.start()
        for fetch in tail:
            fetch.wait()
        message0, message1 = messages(
            wanted_ref[0:tile, :], pre0_ref[0:tile, :], pre1_ref[0:tile, :]
        )
        deliver = deliver_ref[0]
        total0_ref[...] += dot(deliver, message0)
        total1_ref[...] += dot(deliver, message1)

    for fetch in fetches[9:]:
        fetch.wait()
    own = own_ref[...]
    own_pair = level_pair(own, node_w_in_ref[0:width, :])
    own_values = (own[:, :width], own[:, width:])
    states = []
    normed = []
    for level, total_ref in enumerate((total0_ref, total1_ref)):
        summed = total_ref[...].astype(BF16)
        node_pre = (
            own_pair[level] + dot(summed, node_w_in_ref[width : 2 * width, :]) + node_bias_ref[...]
        )
        update = dot(silu(node_pre).astype(BF16), node_w_out_ref[...])
        state = (
            own_values[level].astype(F32) + node_gain_ref[...] * normalize(update)
        ).astype(BF16)
        states.append(state)
        normed.append(
            (attention_gain_ref[...] * normalize(state.astype(F32))).astype(BF16)
        )
    state_ref[...] = merge_levels(*states)
    normed_ref[...] = merge_levels(*normed)


def attention_kernel(rows_ref, bias_ref, query_ref, key_ref, value_ref, out_ref, mix_ref):
    group_count, item_count, merged = rows_ref.shape
    width = merged // 2
    head_width = width // HEADS
    scale = 1.0 / math.sqrt(head_width)
    chunk = 8
    half = group_count * chunk
    total = 2 * half
    head_of = lax.broadcasted_iota(jnp.int32, (1, width), 1) // head_width
    row_node = lax.broadcasted_iota(jnp.int32, (total, total), 0) % chunk
    col_node = lax.broadcasted_iota(jnp.int32, (total, total), 1) % chunk
    same_node = row_node == col_node
    merged_rows = rows_ref[...].reshape(group_count * item_count, merged)

    def project(weight_ref):
        return [
            p.reshape(group_count, item_count, width)
            for p in level_pair(merged_rows, weight_ref[...])
        ]

    def rows_of(pair, part):
        items = slice(part * chunk, (part + 1) * chunk)
        return jnp.concatenate([p[:, items, :].reshape(half, width) for p in pair], axis=0)

    queries, keys, values = project(query_ref), project(key_ref), project(value_ref)
    ones = jnp.concatenate(
        [
            jnp.broadcast_to(jnp.where(head_of == head, 1.0, 0.0), (total, width))
            for head in range(HEADS)
        ],
        axis=0,
    ).astype(BF16)
    for part in range(item_count // chunk):
        part_queries = rows_of(queries, part).astype(BF16)
        part_keys = rows_of(keys, part)
        part_values = rows_of(values, part)
        bias = jnp.where(same_node, bias_ref[part], -1e30)
        stacked_keys = jnp.concatenate(
            [jnp.where(head_of == head, part_keys, 0.0).astype(BF16) for head in range(HEADS)],
            axis=0,
        )
        stacked_values = jnp.concatenate(
            [jnp.where(head_of == head, part_values, 0.0).astype(BF16) for head in range(HEADS)],
            axis=0,
        )
        scores = dot_lanes(part_queries, stacked_keys)
        powers = []
        for head in range(HEADS):
            own_scores = scores[:, head * total : (head + 1) * total] * scale + bias
            top = jnp.max(own_scores, axis=-1, keepdims=True)
            powers.append(jnp.exp(own_scores - top).astype(BF16))
        powers = jnp.concatenate(powers, axis=1)
        attended = dot(powers, stacked_values) / dot(powers, ones)
        items = slice(part * chunk, (part + 1) * chunk)
        for level in range(2):
            mix_ref[level, :, items, :] = attended[level * half : (level + 1) * half].reshape(
                group_count, chunk, width
            )
    mixed = [
        mix_ref[level].reshape(group_count * item_count, width).astype(BF16) for level in range(2)
    ]
    out_ref[...] = merge_levels(*mixed).reshape(group_count, item_count, merged)


def output_kernel(state_ref, attended_ref, live_ref, weight_ref, out_ref):
    width = weight_ref.shape[0]
    mixed = level_pair(attended_ref[...], weight_ref[...])
    state = state_ref[...].astype(F32)
    for level in range(2):
        kept = mixed[level] * live_ref[:, level : level + 1]
        result = state[:, level * width : (level + 1) * width] + kept
        out_ref[level] = result.T.astype(BF16)


def call(kernel, out_shape, *operands, scratch=(), **specs):
    return pl.pallas_call(
        kernel,
        out_shape=out_shape,
        **specs,
        scratch_shapes=list(scratch),
        compiler_params=pltpu.CompilerParams(vmem_limit_bytes=VMEM_BYTES),
    )(*operands)


def shape(dims, dtype=BF16):
    return jax.ShapeDtypeStruct(dims, dtype)


def per_device(
    node_state,
    edge_attr,
    edge_sender,
    edge_receiver,
    tile_block,
    halo_rows,
    valid_levels,
    edge_w_in,
    edge_bias,
    edge_w_out,
    node_w_in,
    node_bias,
    node_w_out,
    node_gain,
    attention_gain,
    query_weight,
    key_weight,
    value_weight,
    output_weight,
):
    group_count = lax.axis_size("lev")
    node_dev, lev_dev, width = node_state.shape
    tile_count = tile_block.shape[0]
    patch_count, slot_count = halo_rows.shape
    merged = lev_dev * width
    own = node_state.transpose(1, 2, 0).reshape(merged, node_dev)
    outgoing = call(
        halo_kernel,
        shape((patch_count * slot_count, merged)),
        halo_rows,
        own,
        scratch=[pltpu.VMEM((patch_count * slot_count, node_dev), BF16)],
    )
    incoming = lax.all_to_all(
        outgoing.reshape(patch_count, slot_count, merged),
        "patch",
        split_axis=0,
        concat_axis=0,
        tiled=True,
    ).reshape(patch_count * slot_count, merged)

    senders = edge_sender.reshape(tile_count, 128)
    in_block = edge_receiver.reshape(tile_count, 128)
    receivers = jnp.where(in_block >= 0, tile_block[:, None] * 128 + in_block, -1)
    edge_count = edge_attr.shape[0]
    sums = [shape((node_dev, width), F32)] * 2
    tiles, pre0, pre1, wanted, deliver, sum0, sum1, own_rows = call(
        local_kernel,
        (
            shape((1,), jnp.int32),
            shape((edge_count, width), F32),
            shape((edge_count, width), F32),
            shape((edge_count, 128), F32),
            shape((tile_count, node_dev, 128)),
            *sums,
            shape((node_dev, merged)),
        ),
        senders,
        receivers,
        edge_attr.T,
        own,
        edge_w_in,
        edge_bias[None, :],
        edge_w_out,
        scratch=[
            pltpu.VMEM((tile_count, 128), F32),
            pltpu.VMEM((width + 16, edge_count), BF16),
        ],
        out_specs=[pl.BlockSpec(memory_space=pltpu.SMEM)]
        + [pl.BlockSpec(memory_space=pltpu.VMEM)] * 7,
    )
    late = LATE_TILES * 128
    state, normed = call(
        edge_kernel,
        (shape((node_dev, merged)), shape((node_dev, merged))),
        tiles,
        pre0,
        pre1,
        wanted,
        deliver,
        sum0,
        sum1,
        incoming,
        own_rows,
        edge_w_in,
        edge_w_out,
        node_w_in,
        node_bias[None, :],
        node_w_out,
        node_gain[None, :],
        attention_gain[None, :],
        scratch=[
            pltpu.VMEM((late, width), F32),
            pltpu.VMEM((late, width), F32),
            pltpu.VMEM((late, 128), F32),
            pltpu.VMEM((LATE_TILES, node_dev, 128), BF16),
            pltpu.VMEM((node_dev, width), F32),
            pltpu.VMEM((node_dev, width), F32),
            pltpu.VMEM((patch_count * slot_count, merged), BF16),
            pltpu.VMEM((node_dev, merged), BF16),
            pltpu.VMEM((width, width), BF16),
            pltpu.VMEM((width, width), BF16),
            pltpu.VMEM((2 * width, width), BF16),
            pltpu.VMEM((width, width), BF16),
            pltpu.SemaphoreType.DMA((12,)),
        ],
        in_specs=[pl.BlockSpec(memory_space=pltpu.SMEM)]
        + [pl.BlockSpec(memory_space=pl.ANY)] * 11
        + [pl.BlockSpec(memory_space=pltpu.VMEM)]
        + [pl.BlockSpec(memory_space=pl.ANY)]
        + [pl.BlockSpec(memory_space=pltpu.VMEM)] * 2,
    )
    per_group = node_dev // group_count
    chunk = 8
    me = lax.axis_index("lev")
    mine = lax.dynamic_slice_in_dim(valid_levels, me * per_group, per_group)
    level_of = (
        jnp.arange(group_count, dtype=jnp.int32)[None, :, None] * lev_dev
        + jnp.arange(lev_dev, dtype=jnp.int32)[:, None, None]
    )
    key_bias = jnp.where(
        level_of[None] < mine.reshape(per_group // chunk, 1, 1, chunk), 0.0, -1e30
    ).reshape(per_group // chunk, 1, lev_dev * group_count * chunk)
    columns = lax.all_to_all(
        normed.reshape(group_count, per_group, merged),
        "lev",
        split_axis=0,
        concat_axis=0,
        tiled=True,
    )
    attended = call(
        attention_kernel,
        shape((group_count, per_group, merged)),
        columns,
        key_bias,
        query_weight,
        key_weight,
        value_weight,
        scratch=[pltpu.VMEM((lev_dev, group_count, per_group, width), F32)],
    )
    returned = lax.all_to_all(
        attended, "lev", split_axis=0, concat_axis=0, tiled=True
    ).reshape(node_dev, merged)
    levels = me * lev_dev + jnp.arange(lev_dev, dtype=jnp.int32)
    live = (levels[None, :] < valid_levels[:, None]).astype(F32)
    out = call(
        output_kernel,
        shape((lev_dev, width, node_dev)),
        state,
        returned,
        live,
        output_weight,
    )
    return out.transpose(2, 0, 1)


def solution(mesh):
    in_specs = (
        P("patch", "lev", None),
        P("patch", None),
        P("patch"),
        P("patch"),
        P("patch"),
        P("patch", None),
        P("patch"),
    ) + (P(),) * 12
    out_specs = P("patch", "lev", None)
    return jax.shard_map(
        per_device, mesh=mesh, in_specs=in_specs, out_specs=out_specs, check_vma=False
    )
```

time: 90.3 us -> 84.4 us (0.935)
  waiting for transfers between devices: 34 us -> 16.1 us
  Pallas kernels: 23.7 us -> 41.5 us
  local copies, waits for them, and re-layouts: 11.8 us -> 4.5 us
  other arithmetic: 0.19 us -> 2.03 us
    pallas_call x5, Pallas kernels: 23.7 us -> 41.5 us  [call(): pl.pallas_call(kernel, out_shape=out_shape, **specs, scratch_shapes=list(...]
    all_to_all x1, waiting for transfers between devices: 20.5 us -> 3.83 us  [per_device(): lax.all_to_all(outgoing.reshape(patch_count, slot_count, merged), 'patch'...]
    unnamed x45 -> x18, local copies, waits for them, and re-layouts: 9.43 us -> 4.08 us
    reshape x1 -> x0, local copies, waits for them, and re-layouts: 1.13 us -> none  [per_device(): own = node_state.reshape(node_dev, merged)]
  transfers between devices with their start and end apart: 3 -> 3, of which waited for: 3 -> 3; matrix products, arithmetic and copies ran while one was open for 3% -> 5% of each run, Pallas kernels for 6% -> 29%
where the time goes in v2:
time: 84.4 us; the launch traced here: 83.7 us
  Pallas kernels  41.5 us (49%)
  starting transfers between devices  19.4 us (23%)
  waiting for transfers between devices  16.1 us (19%)
  local copies, waits for them, and re-layouts  4.5 us (5%)
  other arithmetic  2.03 us (2%)
    pallas_call x5, Pallas kernels, call(): pl.pallas_call(kernel, out_shape=out_shape, **specs, scratch_shapes=list(...  41.5 us
    all_to_all x1, starting transfers between devices, per_device(): lax.all_to_all(outgoing.reshape(patch_count, slot_count, merged), 'patch'...  11.7 us
    all_to_all x1, waiting for transfers between devices, per_device(): lax.all_to_all(normed.reshape(group_count, per_group, merged), 'lev', spl...  6.24 us
    all_to_all x1, waiting for transfers between devices, per_device(): lax.all_to_all(attended, 'lev', split_axis=0, concat_axis=0, tiled=True)  6 us
    all_to_all x1, starting transfers between devices, per_device(): lax.all_to_all(normed.reshape(group_count, per_group, merged), 'lev', spl...  4.31 us
    unnamed x18, local copies, waits for them, and re-layouts  4.08 us
    all_to_all x1, waiting for transfers between devices, per_device(): lax.all_to_all(outgoing.reshape(patch_count, slot_count, merged), 'patch'...  3.83 us
    all_to_all x1, starting transfers between devices, per_device(): lax.all_to_all(attended, 'lev', split_axis=0, concat_axis=0, tiled=True)  3.39 us
  transfers between devices with their start and end apart: 3, of which 3 were waited for; matrix products, arithmetic and copies ran while one was open for 5% of the time, Pallas kernels for 29%

profile of v2, /device:TPU:8, one launch (start us, length us, event | category | flops | bytes accessed | tf_op | source)
XLA Modules:
  0.0 83.7 jit_solution(2475635312889429082)
XLA Ops:
  0.0 0.0 copy-start.6
  0.0 0.0 copy-start.4
  0.0 0.0 copy-start.3
  0.0 0.0 copy-start.7
  0.0 0.0 copy-start.5
  0.0 2.7 %shard_map.182 = bf16[1536,384]{1,0:T(8,128)(2,1)} custom-call(s32[32,48]{1,0:T(8,128)} %halo_ref.1, bf16[384,256]{1,0:T(8,128)(2,1)} %bitcast.27), custom_call_target="tpu_custom_call" | custom-call | tf_op jit(solution)/shard_map/pallas_call | solution.py:409
  2.7 11.7 %all-to-all-start = ((bf16[32,48,384]{2,1,0:T(8,128)(2,1)}), bf16[32,48,384]{2,1,0:T(8,128)(2,1)S(1)}, u32[]{:S(2)}, u32[]{:S(2)}) async-start(bf16[32,48,384]{2,1,0:T(8,128)(2,1)} %bitcast.23), calls=%async_computation | async-start | bytes 2359296 | tf_op jit(solution)/shard_map/all_to_all | solution.py:456
  14.5 0.0 copy-done.6
  14.5 0.1 dynamic_slice.3
  14.5 0.1 lt.48
  14.6 0.1 lt.44
  14.7 0.1 lt.45
  14.8 0.1 lt.50
  14.9 0.0 copy-done.4
  14.9 0.8 copy.25.node_w_in_hbm
  15.7 0.0 copy-done.3
  15.7 0.9 %copy.23.w_in_ref.w_in_hbm = bf16[576,192]{1,0:T(8,128)(2,1)} copy(bf16[576,192]{0,1:T(8,128)(2,1)S(1)} %copy-done.3) | data formatting | bytes 442368 | tf_op args[7]
  16.6 0.0 copy-done.7
  16.6 0.0 copy-done.5
  16.6 0.7 fusion.receiver_ref
  17.3 24.2 %shard_map.181 = (s32[1]{0:T(128)}, f32[2048,192]{1,0:T(8,128)}, f32[2048,192]{1,0:T(8,128)}, f32[2048,128]{1,0:T(8,128)}, bf16[16,256,128]{2,1,0:T(8,128)(2,1)}...) custom-call(s32[16,128]{1,0:T(8,128)} %bitcast.30, s32[16,128]{1,0:T(8,128)} %fusion.receiver_ref, ...), custom_call_target="tpu_custom_call" | custom-call | tf_op jit(solution)/shard_map/pallas_call | solution.py:409
  41.5 3.8 %all-to-all-done = bf16[32,48,384]{2,1,0:T(8,128)(2,1)S(1)} async-done(((bf16[32,48,384]{2,1,0:T(8,128)(2,1)}), bf16[32,48,384]{2,1,0:T(8,128)(2,1)S(1)}, u32[]{:S(2)}, u32[]{:S(2)}) %all-to-all-start) | async-done | bytes 1179680 | tf_op jit(solution)/shard_map/all_to_all | solution.py:456
  45.3 0.0 copy-start
  45.3 1.0 %copy-done = bf16[32,48,384]{2,1,0:T(8,128)(2,1)} copy-done((bf16[32,48,384]{2,1,0:T(8,128)(2,1)}, bf16[32,48,384]{2,1,0:T(8,128)(2,1)S(1)}, u32[]{:S(2)}) %copy-start) | copy-done | bytes 1179672
  46.3 8.7 %shard_map.183 = (bf16[256,384]{1,0:T(8,128)(2,1)}, bf16[256,384]{1,0:T(8,128)(2,1)}) custom-call(s32[1]{0:T(128)} %get-tuple-element.15.tiles_ref, f32[2048,192]{1,0:T(8,128)} %get-tuple-element.16.pre0_hbm, f32[2048,192]{1,0:T(8,128)} %get-tuple-element.17.pre1_hbm, f32[2048,128]{1,0:T(8,128)} %get-tuple-element.18.wanted_hbm, ...), custom_call_target="tpu_custom_call" | custom-call | tf_op jit(solution)/shard_map/pallas_call | solution.py:409
  55.0 4.3 %all-to-all-start.1 = ((bf16[8,32,384]{2,1,0:T(8,128)(2,1)}), bf16[8,32,384]{2,1,0:T(8,128)(2,1)S(1)}, u32[]{:S(2)}, u32[]{:S(2)}) async-start(bf16[8,32,384]{2,1,0:T(8,128)(2,1)} %bitcast.29), calls=%async_computation.1 | async-start | bytes 393216 | tf_op jit(solution)/shard_map/all_to_all | solution.py:546
  59.3 0.6 compare_select_fusion.bias_ref
  59.9 6.2 %all-to-all-done.1.rows_ref = bf16[8,32,384]{2,1,0:T(8,128)(2,1)S(1)} async-done(((bf16[8,32,384]{2,1,0:T(8,128)(2,1)}), bf16[8,32,384]{2,1,0:T(8,128)(2,1)S(1)}, u32[]{:S(2)}, u32[]{:S(2)}) %all-to-all-start.1) | async-done | bytes 196640 | tf_op jit(solution)/shard_map/all_to_all | solution.py:546
  66.2 0.0 copy-start.2
  66.2 0.7 copy-done.2
  66.9 3.7 %shard_map.184 = bf16[8,32,384]{2,1,0:T(8,128)(2,1)} custom-call(bf16[8,32,384]{2,1,0:T(8,128)(2,1)} %copy-done.2, f32[4,1,128]{2,1,0:T(1,128)} %compare_select_fusion.bias_ref, bf16[192,192]{1,0:T(8,128)(2,1)} %query_ref.1, bf16[192,192]{1,0:T(8,128)(2,1)} %key_ref.1, bf16[192,192]{1,0:T(8,128)(2,1)} %value_ref.1), custom_call_target="tpu_custom_call" | custom-call | tf_op jit(solution)/shard_map/pallas_call | solution.py:409
  70.5 3.4 %all-to-all-start.2 = ((bf16[8,32,384]{2,1,0:T(8,128)(2,1)}), bf16[8,32,384]{2,1,0:T(8,128)(2,1)S(1)}, u32[]{:S(2)}, u32[]{:S(2)}) async-start(bf16[8,32,384]{2,1,0:T(8,128)(2,1)} %shard_map.184), calls=%async_computation.2 | async-start | bytes 393216 | tf_op jit(solution)/shard_map/all_to_all | solution.py:563
  73.9 0.8 compare_convert_fusion.live_ref
  74.7 6.0 %all-to-all-done.2 = bf16[8,32,384]{2,1,0:T(8,128)(2,1)S(1)} async-done(((bf16[8,32,384]{2,1,0:T(8,128)(2,1)}), bf16[8,32,384]{2,1,0:T(8,128)(2,1)S(1)}, u32[]{:S(2)}, u32[]{:S(2)}) %all-to-all-start.2) | async-done | bytes 196640 | tf_op jit(solution)/shard_map/all_to_all | solution.py:563
  80.7 0.0 copy-start.1
  80.7 0.7 copy-done.1
  81.4 2.3 %shard_map.185 = bf16[2,192,256]{2,1,0:T(8,128)(2,1)} custom-call(bf16[256,384]{1,0:T(8,128)(2,1)} %get-tuple-element.23.state_ref, bf16[256,384]{1,0:T(8,128)(2,1)} %bitcast.26, f32[256,2]{1,0:T(8,128)} %compare_convert_fusion.live_ref, bf16[192,192]{1,0:T(8,128)(2,1)} %weight_ref.1), custom_call_target="tpu_custom_call" | custom-call | tf_op jit(solution)/shard_map/pallas_call | solution.py:409
  (5 shorter events, 0.0 us)
Async XLA Ops:
  0.0 14.5 %copy-start.6 = (s32[256]{0:T(256)S(1)}, s32[256]{0:T(256)}, u32[]{:S(2)}) copy-start(s32[256]{0:T(256)} %param.25) | copy-start | bytes 3076
  0.0 14.9 %copy-start.4 = (bf16[384,192]{0,1:T(8,128)(2,1)S(1)}, bf16[384,192]{0,1:T(8,128)(2,1)}, u32[]{:S(2)}) copy-start(bf16[384,192]{0,1:T(8,128)(2,1)} %param.29) | copy-start | bytes 442372
  0.0 15.7 %copy-start.3 = (bf16[576,192]{0,1:T(8,128)(2,1)S(1)}, bf16[576,192]{0,1:T(8,128)(2,1)}, u32[]{:S(2)}) copy-start(bf16[576,192]{0,1:T(8,128)(2,1)} %param.26) | copy-start | bytes 663556
  0.0 16.6 %copy-start.7 = (s32[16]{0:T(128)S(1)}, s32[16]{0:T(128)}, u32[]{:S(2)}) copy-start(s32[16]{0:T(128)} %param.23) | copy-start | bytes 196
  0.0 16.6 %copy-start.5 = (s32[2048]{0:T(1024)S(1)}, s32[2048]{0:T(1024)}, u32[]{:S(2)}) copy-start(s32[2048]{0:T(1024)} %param.22) | copy-start | bytes 24580
  2.7 42.6 %all-to-all-start = ((bf16[32,48,384]{2,1,0:T(8,128)(2,1)}), bf16[32,48,384]{2,1,0:T(8,128)(2,1)S(1)}, u32[]{:S(2)}, u32[]{:S(2)}) async-start(bf16[32,48,384]{2,1,0:T(8,128)(2,1)} %bitcast.23), calls=%async_computation | async-start | bytes 2359296 | tf_op jit(solution)/shard_map/all_to_all | solution.py:456
  45.3 1.0 %copy-start = (bf16[32,48,384]{2,1,0:T(8,128)(2,1)}, bf16[32,48,384]{2,1,0:T(8,128)(2,1)S(1)}, u32[]{:S(2)}) copy-start(bf16[32,48,384]{2,1,0:T(8,128)(2,1)S(1)} %all-to-all-done) | copy-start | bytes 3538948
  55.0 11.1 %all-to-all-start.1 = ((bf16[8,32,384]{2,1,0:T(8,128)(2,1)}), bf16[8,32,384]{2,1,0:T(8,128)(2,1)S(1)}, u32[]{:S(2)}, u32[]{:S(2)}) async-start(bf16[8,32,384]{2,1,0:T(8,128)(2,1)} %bitcast.29), calls=%async_computation.1 | async-start | bytes 393216 | tf_op jit(solution)/shard_map/all_to_all | solution.py:546
  66.2 0.7 copy-start.2
  70.5 10.2 %all-to-all-start.2 = ((bf16[8,32,384]{2,1,0:T(8,128)(2,1)}), bf16[8,32,384]{2,1,0:T(8,128)(2,1)S(1)}, u32[]{:S(2)}, u32[]{:S(2)}) async-start(bf16[8,32,384]{2,1,0:T(8,128)(2,1)} %shard_map.184), calls=%async_computation.2 | async-start | bytes 393216 | tf_op jit(solution)/shard_map/all_to_all | solution.py:563
  80.7 0.7 copy-start.1

commit v3 on v2

--- a/solution.py
+++ b/solution.py
@@ -10,9 +10,10 @@
 HEADS = 4
 BF16 = jnp.bfloat16
 F32 = jnp.float32
-VMEM_BYTES = 60 * 1024 * 1024
-LATE_TILES = 6
-LATE_STEP = 2
+VMEM_BYTES = 20 * 1024 * 1024
+WIDE = 256
+LATE_TILES = 3
+CHUNK = 8
 
 
 def dot(a, b):
@@ -55,14 +56,36 @@
     return jnp.concatenate([first, second], axis=1)
 
 
-def halo_kernel(halo_ref, own_ref, out_ref, pick_ref):
+def halo_kernel(halo_hbm, own_hbm, out_hbm, halo_ref, own_ref, rows_ref, arrived, sent):
     patch_count, slot_count = halo_ref.shape
+    fetches = [
+        pltpu.make_async_copy(halo_hbm, halo_ref, arrived.at[0]),
+        pltpu.make_async_copy(own_hbm, own_ref, arrived.at[1]),
+    ]
+    for fetch in fetches:
+        fetch.start()
+    fetches[0].wait()
     columns = halo_ref[...].astype(F32).T
-    for patch in range(patch_count):
-        pick_ref[patch * slot_count : (patch + 1) * slot_count, :] = onehot(
-            columns[:, patch : patch + 1], own_ref.shape[1]
-        )
-    out_ref[...] = dot_lanes(pick_ref[...], own_ref[...]).astype(BF16)
+    sends = []
+    step = patch_count // 4
+    for part in range(4):
+        pick = jnp.concatenate(
+            [
+                onehot(columns[:, patch : patch + 1], own_ref.shape[1])
+                for patch in range(part * step, (part + 1) * step)
+            ],
+            axis=0,
+        )
+        if part == 0:
+            fetches[1].wait()
+        rows = slice(part * step * slot_count, (part + 1) * step * slot_count)
+        rows_ref[rows, :] = dot_lanes(pick, own_ref[...]).astype(BF16)
+        sends.append(
+            pltpu.make_async_copy(rows_ref.at[rows], out_hbm.at[rows], sent.at[part])
+        )
+        sends[-1].start()
+    for send in sends:
+        send.wait()
 
 
 def running_count(flags):
@@ -85,32 +108,48 @@
 def local_kernel(
     sender_ref,
     receiver_ref,
-    attr_ref,
-    own_ref,
+    attr_hbm,
+    own_hbm,
     w_in_ref,
     bias_ref,
     w_out_ref,
     tiles_ref,
+    late_wanted_ref,
     pre0_ref,
     pre1_ref,
-    wanted_ref,
-    deliver_ref,
+    late_deliver_ref,
+    own_rows_ref,
     sum0_ref,
     sum1_ref,
-    own_rows_ref,
+    pre0_hbm,
+    pre1_hbm,
+    wanted_hbm,
+    deliver_hbm,
+    own_ref,
     position_ref,
     table_ref,
+    rest0_ref,
+    rest1_ref,
+    rest2_ref,
+    rest3_ref,
+    sent,
+    arrived,
 ):
+    fetches = [
+        pltpu.make_async_copy(own_hbm, own_ref, arrived.at[0]),
+        pltpu.make_async_copy(attr_hbm, table_ref.at[0 : attr_hbm.shape[0]], arrived.at[1]),
+    ]
+    for fetch in fetches:
+        fetch.start()
     tile_count, tile = sender_ref.shape
-    width, edge_count = attr_ref.shape
-    node_dev = own_ref.shape[1]
+    width, edge_count = attr_hbm.shape
+    merged, node_dev = own_ref.shape
     eye = jnp.where(
         lax.broadcasted_iota(jnp.int32, (node_dev, node_dev), 0)
         == lax.broadcasted_iota(jnp.int32, (node_dev, node_dev), 1),
         1.0,
         0.0,
     ).astype(BF16)
-    own_rows_ref[...] = dot_lanes(eye, own_ref[...]).astype(BF16)
     senders = sender_ref[...]
     receivers = receiver_ref[...]
     used = receivers >= 0
@@ -127,11 +166,13 @@
             is_local > 0.0, remote_total + local_rank, remote_total + local_total + empty_rank
         ),
     )
-    remote_tiles = (jnp.sum(is_remote).astype(jnp.int32) + tile - 1) // tile
-    used_tiles = (jnp.sum(1.0 - is_empty).astype(jnp.int32) + tile - 1) // tile
+    remote_tiles = (jnp.sum(is_remote).astype(jnp.int32) + WIDE - 1) // WIDE
+    used_tiles = (jnp.sum(1.0 - is_empty).astype(jnp.int32) + WIDE - 1) // WIDE
     late_tiles = jnp.maximum(remote_tiles, LATE_TILES)
     tiles_ref[0] = late_tiles
-    table_ref[0:width, :] = attr_ref[...]
+    for fetch in fetches:
+        fetch.wait()
+    own_rows_ref[...] = dot_lanes(eye, own_ref[...]).astype(BF16)
     table_ref[width:, :] = jnp.zeros((table_ref.shape[0] - width, edge_count), BF16)
     for index in range(tile_count):
         lanes = slice(index * tile, (index + 1) * tile)
@@ -152,8 +193,8 @@
     sum1_ref[...] = jnp.zeros_like(sum1_ref)
 
     def arrange(index):
-        wanted = lax.broadcasted_iota(jnp.int32, (tile, tile), 0).astype(F32) + (
-            index * tile
+        wanted = lax.broadcasted_iota(jnp.int32, (WIDE, tile), 0).astype(F32) + (
+            index * WIDE
         ).astype(F32)
         order = jnp.concatenate(
             [
@@ -162,9 +203,8 @@
             ],
             axis=1,
         )
-        table = table_ref[...]
-        moved = dot_lanes(order, table)
-        receiver_row = dot_lanes(table[width : width + 16, :], order)[2:3, :]
+        moved = dot_lanes(order, table_ref[...])
+        receiver_row = dot_lanes(table_ref[width : width + 16, :], order)[2:3, :]
         sender_column = moved[:, width : width + 1] * tile + moved[:, width + 1 : width + 2]
         receiver_column = moved[:, width + 2 : width + 3]
         own = own_rows_ref[...]
@@ -173,18 +213,38 @@
         base = dot(moved[:, :width].astype(BF16), w_attr) + bias_ref[...]
         send0, send1 = level_pair(send_rows, w_send)
         recv0, recv1 = level_pair(recv_rows, w_recv)
-        nodes = lax.broadcasted_iota(jnp.int32, (node_dev, tile), 0).astype(F32)
+        nodes = lax.broadcasted_iota(jnp.int32, (node_dev, WIDE), 0).astype(F32)
         deliver = jnp.where(nodes == receiver_row, 1.0, 0.0).astype(BF16)
-        return base + send0 + recv0, base + send1 + recv1, deliver, sender_column
-
-    @pl.loop(0, late_tiles)
+        return base + send0 + recv0, base + send1 + recv1, deliver, sender_column - node_dev
+
+    @pl.loop(0, LATE_TILES)
     def _(index):
-        pre0, pre1, deliver, sender_column = arrange(index)
-        rows = pl.ds(pl.multiple_of(index * tile, tile), tile)
+        pre0, pre1, deliver, wanted = arrange(index)
+        rows = pl.ds(pl.multiple_of(index * WIDE, WIDE), WIDE)
         pre0_ref[rows, :] = pre0
         pre1_ref[rows, :] = pre1
-        deliver_ref[index] = deliver
-        wanted_ref[rows, :] = jnp.broadcast_to(sender_column - node_dev, (tile, 128))
+        late_deliver_ref[index] = deliver
+        late_wanted_ref[rows, :] = jnp.broadcast_to(wanted, (WIDE, 128))
+
+    @pl.loop(LATE_TILES, late_tiles)
+    def _(index):
+        rest0_ref[...], rest1_ref[...], rest3_ref[0], wanted = arrange(index)
+        rest2_ref[...] = jnp.broadcast_to(wanted, rest2_ref.shape)
+        sends = [
+            pltpu.make_async_copy(source, target.at[index - LATE_TILES], sent.at[slot])
+            for slot, (source, target) in enumerate(
+                (
+                    (rest0_ref, pre0_hbm),
+                    (rest1_ref, pre1_hbm),
+                    (rest2_ref, wanted_hbm),
+                    (rest3_ref.at[0], deliver_hbm),
+                )
+            )
+        ]
+        for send in sends:
+            send.start()
+        for send in sends:
+            send.wait()
 
     @pl.loop(late_tiles, jnp.maximum(used_tiles, late_tiles))
     def _(index):
@@ -196,65 +256,60 @@
 
 def edge_kernel(
     tiles_ref,
+    late_wanted_ref,
+    late_pre0_hbm,
+    late_pre1_hbm,
+    late_deliver_hbm,
+    own_hbm,
+    sum0_hbm,
+    sum1_hbm,
     pre0_hbm,
     pre1_hbm,
     wanted_hbm,
     deliver_hbm,
-    sum0_hbm,
-    sum1_hbm,
-    remote_hbm,
-    own_hbm,
-    w_in_hbm,
-    w_out_hbm,
-    node_w_in_hbm,
+    w_in_ref,
+    w_out_ref,
+    node_w_in_ref,
     node_bias_ref,
-    node_w_out_hbm,
+    node_w_out_ref,
     node_gain_ref,
     attention_gain_ref,
+    remote_ref,
     state_ref,
     normed_ref,
     pre0_ref,
     pre1_ref,
-    wanted_ref,
-    deliver_ref,
+    late_deliver_ref,
+    own_ref,
     total0_ref,
     total1_ref,
-    remote_ref,
-    own_ref,
-    w_send_ref,
-    w_out_ref,
-    node_w_in_ref,
-    node_w_out_ref,
+    rest0_ref,
+    rest1_ref,
+    rest2_ref,
+    rest3_ref,
+    early_arrived,
     arrived,
 ):
-    tile = deliver_ref.shape[2]
     width = w_out_ref.shape[0]
-    late = LATE_TILES * tile
-    fetches = [
-        pltpu.make_async_copy(source, target, arrived.at[index])
-        for index, (source, target) in enumerate(
+    early = [
+        pltpu.make_async_copy(source, target, early_arrived.at[slot])
+        for slot, (source, target) in enumerate(
             (
-                (wanted_hbm.at[0:late], wanted_ref),
-                (remote_hbm, remote_ref),
-                (w_in_hbm.at[0:width], w_send_ref),
-                (pre0_hbm.at[0:late], pre0_ref),
-                (pre1_hbm.at[0:late], pre1_ref),
-                (w_out_hbm, w_out_ref),
-                (deliver_hbm.at[0:LATE_TILES], deliver_ref),
+                (late_pre0_hbm, pre0_ref),
+                (late_pre1_hbm, pre1_ref),
+                (late_deliver_hbm, late_deliver_ref),
                 (sum0_hbm, total0_ref),
                 (sum1_hbm, total1_ref),
                 (own_hbm, own_ref),
-                (node_w_in_hbm, node_w_in_ref),
-                (node_w_out_hbm, node_w_out_ref),
             )
         )
     ]
-    for fetch in fetches:
+    for fetch in early:
         fetch.start()
-
-    def messages(wanted, pre0, pre1):
-        rows = wanted.shape[0]
-        lanes = lax.broadcasted_iota(jnp.int32, (rows, 128), 1).astype(F32)
+    w_send = w_in_ref[0:width, :]
+
+    def gather(wanted):
+        lanes = lax.broadcasted_iota(jnp.int32, wanted.shape, 1).astype(F32)
         pick = jnp.concatenate(
             [
                 jnp.where(wanted == lanes + float(first), 1.0, 0.0).astype(BF16)
@@ -262,53 +317,43 @@
             ],
             axis=1,
         )
-        send_rows = dot(pick, remote_ref[...]).astype(BF16)
-        send0, send1 = level_pair(send_rows, w_send_ref[...])
-        hidden0 = silu(pre0 + send0).astype(BF16)
-        hidden1 = silu(pre1 + send1).astype(BF16)
-        w_out = w_out_ref[...]
-        return dot(hidden0, w_out).astype(BF16), dot(hidden1, w_out).astype(BF16)
-
-    for fetch in fetches[:9]:
+        return level_pair(dot(pick, remote_ref[...]).astype(BF16), w_send)
+
+    def messages(pre, sent):
+        return dot(silu(pre + sent).astype(BF16), w_out_ref[...]).astype(BF16)
+
+    sent0, sent1 = gather(late_wanted_ref[...])
+    early[0].wait()
+    message0 = messages(pre0_ref[...], sent0)
+    early[1].wait()
+    message1 = messages(pre1_ref[...], sent1)
+    for fetch in early[2:]:
         fetch.wait()
-    total0, total1 = total0_ref[...], total1_ref[...]
-    step = LATE_STEP
-    for start in range(0, LATE_TILES, step):
-        rows = slice(start * tile, (start + step) * tile)
-        message0, message1 = messages(wanted_ref[rows, :], pre0_ref[rows, :], pre1_ref[rows, :])
-        deliver = jnp.concatenate([deliver_ref[start + i] for i in range(step)], axis=1)
-        total0 += dot(deliver, message0)
-        total1 += dot(deliver, message1)
-    total0_ref[...] = total0
-    total1_ref[...] = total1
+    deliver = jnp.concatenate([late_deliver_ref[i] for i in range(LATE_TILES)], axis=1)
+    total0_ref[...] += dot(deliver, message0)
+    total1_ref[...] += dot(deliver, message1)
 
     @pl.loop(LATE_TILES, tiles_ref[0])
     def _(index):
-        rows = pl.ds(pl.multiple_of(index * tile, tile), tile)
-        tail = [
-            pltpu.make_async_copy(source, target, arrived.at[slot])
+        fetches = [
+            pltpu.make_async_copy(source.at[index - LATE_TILES], target, arrived.at[slot])
             for slot, (source, target) in enumerate(
                 (
-                    (wanted_hbm.at[rows], wanted_ref.at[0:tile]),
-                    (pre0_hbm.at[rows], pre0_ref.at[0:tile]),
-                    (pre1_hbm.at[rows], pre1_ref.at[0:tile]),
-                    (deliver_hbm.at[pl.ds(index, 1)], deliver_ref.at[0:1]),
+                    (pre0_hbm, rest0_ref),
+                    (pre1_hbm, rest1_ref),
+                    (wanted_hbm, rest2_ref),
+                    (deliver_hbm, rest3_ref.at[0]),
                 )
             )
         ]
-        for fetch in tail:
+        for fetch in fetches:
             fetch.start()
-        for fetch in tail:
+        for fetch in fetches:
             fetch.wait()
-        message0, message1 = messages(
-            wanted_ref[0:tile, :], pre0_ref[0:tile, :], pre1_ref[0:tile, :]
-        )
-        deliver = deliver_ref[0]
-        total0_ref[...] += dot(deliver, message0)
-        total1_ref[...] += dot(deliver, message1)
-
-    for fetch in fetches[9:]:
-        fetch.wait()
+        sent0, sent1 = gather(rest2_ref[...])
+        total0_ref[...] += dot(rest3_ref[0], messages(rest0_ref[...], sent0))
+        total1_ref[...] += dot(rest3_ref[0], messages(rest1_ref[...], sent1))
+
     own = own_ref[...]
     own_pair = level_pair(own, node_w_in_ref[0:width, :])
     own_values = (own[:, :width], own[:, width:])
@@ -336,7 +381,7 @@
     width = merged // 2
     head_width = width // HEADS
     scale = 1.0 / math.sqrt(head_width)
-    chunk = 8
+    chunk = CHUNK
     half = group_count * chunk
     total = 2 * half
     head_of = lax.broadcasted_iota(jnp.int32, (1, width), 1) // head_width
@@ -417,6 +462,19 @@
 
 def shape(dims, dtype=BF16):
     return jax.ShapeDtypeStruct(dims, dtype)
+
+
+def kept(array):
+    return pltpu.with_memory_space_constraint(array, pltpu.VMEM)
+
+
+def in_hbm(array):
+    return pltpu.with_memory_space_constraint(array, pltpu.HBM)
+
+
+IN_SMEM = pl.BlockSpec(memory_space=pltpu.SMEM)
+IN_VMEM = pl.BlockSpec(memory_space=pltpu.VMEM)
+ANYWHERE = pl.BlockSpec(memory_space=pl.ANY)
 
 
 def per_device(
@@ -445,13 +503,23 @@
     tile_count = tile_block.shape[0]
     patch_count, slot_count = halo_rows.shape
     merged = lev_dev * width
+    remote_count = patch_count * slot_count
+    edge_count = edge_attr.shape[0]
     own = node_state.transpose(1, 2, 0).reshape(merged, node_dev)
     outgoing = call(
         halo_kernel,
-        shape((patch_count * slot_count, merged)),
-        halo_rows,
-        own,
-        scratch=[pltpu.VMEM((patch_count * slot_count, node_dev), BF16)],
+        shape((remote_count, merged)),
+        in_hbm(halo_rows),
+        in_hbm(own),
+        in_specs=[ANYWHERE] * 2,
+        out_specs=ANYWHERE,
+        scratch=[
+            pltpu.VMEM((patch_count, slot_count), jnp.int32),
+            pltpu.VMEM((merged, node_dev), BF16),
+            pltpu.VMEM((remote_count, merged), BF16),
+            pltpu.SemaphoreType.DMA((2,)),
+            pltpu.SemaphoreType.DMA((4,)),
+        ],
     )
     incoming = lax.all_to_all(
         outgoing.reshape(patch_count, slot_count, merged),
@@ -459,51 +527,72 @@
         split_axis=0,
         concat_axis=0,
         tiled=True,
-    ).reshape(patch_count * slot_count, merged)
+    ).reshape(remote_count, merged)
 
     senders = edge_sender.reshape(tile_count, 128)
     in_block = edge_receiver.reshape(tile_count, 128)
     receivers = jnp.where(in_block >= 0, tile_block[:, None] * 128 + in_block, -1)
-    edge_count = edge_attr.shape[0]
-    sums = [shape((node_dev, width), F32)] * 2
-    tiles, pre0, pre1, wanted, deliver, sum0, sum1, own_rows = call(
+    per_group = node_dev // group_count
+    me = lax.axis_index("lev")
+    mine = lax.dynamic_slice_in_dim(valid_levels, me * per_group, per_group)
+    level_of = (
+        jnp.arange(group_count, dtype=jnp.int32)[None, :, None] * lev_dev
+        + jnp.arange(lev_dev, dtype=jnp.int32)[:, None, None]
+    )
+    key_bias = jnp.where(
+        level_of[None] < mine.reshape(per_group // CHUNK, 1, 1, CHUNK), 0.0, -1e30
+    ).reshape(per_group // CHUNK, 1, lev_dev * group_count * CHUNK)
+    levels = me * lev_dev + jnp.arange(lev_dev, dtype=jnp.int32)
+    live = (levels[None, :] < valid_levels[:, None]).astype(F32)
+
+    rest = edge_count // WIDE - LATE_TILES
+    late = LATE_TILES * WIDE
+    rest_shapes = [
+        ((WIDE, width), F32),
+        ((WIDE, width), F32),
+        ((WIDE, 128), F32),
+        ((1, node_dev, WIDE), BF16),
+    ]
+    tiles, wanted, *tail = call(
         local_kernel,
         (
             shape((1,), jnp.int32),
-            shape((edge_count, width), F32),
-            shape((edge_count, width), F32),
-            shape((edge_count, 128), F32),
-            shape((tile_count, node_dev, 128)),
-            *sums,
-            shape((node_dev, merged)),
+            pltpu.VMEM((late, 128), F32),
+            pltpu.HBM((late, width), F32),
+            pltpu.HBM((late, width), F32),
+            pltpu.HBM((LATE_TILES, node_dev, WIDE), BF16),
+            pltpu.HBM((node_dev, merged), BF16),
+            pltpu.HBM((node_dev, width), F32),
+            pltpu.HBM((node_dev, width), F32),
+            pltpu.HBM((rest, WIDE, width), F32),
+            pltpu.HBM((rest, WIDE, width), F32),
+            pltpu.HBM((rest, WIDE, 128), F32),
+            pltpu.HBM((rest, node_dev, WIDE), BF16),
         ),
         senders,
         receivers,
-        edge_attr.T,
-        own,
+        in_hbm(edge_attr.T),
+        in_hbm(own),
         edge_w_in,
         edge_bias[None, :],
         edge_w_out,
         scratch=[
+            pltpu.VMEM((merged, node_dev), BF16),
             pltpu.VMEM((tile_count, 128), F32),
             pltpu.VMEM((width + 16, edge_count), BF16),
+            *(pltpu.VMEM(*entry) for entry in rest_shapes),
+            pltpu.SemaphoreType.DMA((4,)),
+            pltpu.SemaphoreType.DMA((2,)),
         ],
-        out_specs=[pl.BlockSpec(memory_space=pltpu.SMEM)]
-        + [pl.BlockSpec(memory_space=pltpu.VMEM)] * 7,
-    )
-    late = LATE_TILES * 128
+        in_specs=[IN_VMEM] * 2 + [ANYWHERE] * 2 + [IN_VMEM] * 3,
+        out_specs=[IN_SMEM] + [IN_VMEM] * 7 + [ANYWHERE] * 4,
+    )
     state, normed = call(
         edge_kernel,
-        (shape((node_dev, merged)), shape((node_dev, merged))),
+        (pltpu.VMEM((node_dev, merged), BF16), shape((node_dev, merged))),
         tiles,
-        pre0,
-        pre1,
-        wanted,
-        deliver,
-        sum0,
-        sum1,
-        incoming,
-        own_rows,
+        kept(wanted),
+        *(in_hbm(array) for array in tail),
         edge_w_in,
         edge_w_out,
         node_w_in,
@@ -511,38 +600,20 @@
         node_w_out,
         node_gain[None, :],
         attention_gain[None, :],
+        incoming,
         scratch=[
             pltpu.VMEM((late, width), F32),
             pltpu.VMEM((late, width), F32),
-            pltpu.VMEM((late, 128), F32),
-            pltpu.VMEM((LATE_TILES, node_dev, 128), BF16),
+            pltpu.VMEM((LATE_TILES, node_dev, WIDE), BF16),
+            pltpu.VMEM((node_dev, merged), BF16),
             pltpu.VMEM((node_dev, width), F32),
             pltpu.VMEM((node_dev, width), F32),
-            pltpu.VMEM((patch_count * slot_count, merged), BF16),
-            pltpu.VMEM((node_dev, merged), BF16),
-            pltpu.VMEM((width, width), BF16),
-            pltpu.VMEM((width, width), BF16),
-            pltpu.VMEM((2 * width, width), BF16),
-            pltpu.VMEM((width, width), BF16),
-            pltpu.SemaphoreType.DMA((12,)),
+            *(pltpu.VMEM(*entry) for entry in rest_shapes),
+            pltpu.SemaphoreType.DMA((6,)),
+            pltpu.SemaphoreType.DMA((4,)),
         ],
-        in_specs=[pl.BlockSpec(memory_space=pltpu.SMEM)]
-        + [pl.BlockSpec(memory_space=pl.ANY)] * 11
-        + [pl.BlockSpec(memory_space=pltpu.VMEM)]
-        + [pl.BlockSpec(memory_space=pl.ANY)]
-        + [pl.BlockSpec(memory_space=pltpu.VMEM)] * 2,
-    )
-    per_group = node_dev // group_count
-    chunk = 8
-    me = lax.axis_index("lev")
-    mine = lax.dynamic_slice_in_dim(valid_levels, me * per_group, per_group)
-    level_of = (
-        jnp.arange(group_count, dtype=jnp.int32)[None, :, None] * lev_dev
-        + jnp.arange(lev_dev, dtype=jnp.int32)[:, None, None]
-    )
-    key_bias = jnp.where(
-        level_of[None] < mine.reshape(per_group // chunk, 1, 1, chunk), 0.0, -1e30
-    ).reshape(per_group // chunk, 1, lev_dev * group_count * chunk)
+        in_specs=[IN_SMEM, IN_VMEM] + [ANYWHERE] * 10 + [IN_VMEM] * 8,
+    )
     columns = lax.all_to_all(
         normed.reshape(group_count, per_group, merged),
         "lev",
@@ -563,12 +634,10 @@
     returned = lax.all_to_all(
         attended, "lev", split_axis=0, concat_axis=0, tiled=True
     ).reshape(node_dev, merged)
-    levels = me * lev_dev + jnp.arange(lev_dev, dtype=jnp.int32)
-    live = (levels[None, :] < valid_levels[:, None]).astype(F32)
     out = call(
         output_kernel,
         shape((lev_dev, width, node_dev)),
-        state,
+        kept(state),
         returned,
         live,
         output_weight,

time: 84.4 us -> 77.4 us (0.917)
  Pallas kernels: 41.5 us -> 28.2 us
  waiting for transfers between devices: 16.1 us -> 27.5 us
  local copies, waits for them, and re-layouts: 4.5 us -> 0.82 us
  other arithmetic: 2.03 us -> 0.2 us
    pallas_call x5, Pallas kernels: 41.5 us -> 28.2 us  [call(): pl.pallas_call(kernel, out_shape=out_shape, **specs, scratch_shapes=list(...]
    all_to_all x1, waiting for transfers between devices: 3.83 us -> 14 us  [per_device(): lax.all_to_all(outgoing.reshape(patch_count, slot_count, merged), 'patch'...]
    unnamed x18 -> x34, local copies, waits for them, and re-layouts: 4.08 us -> 0.4 us
  transfers between devices with their start and end apart: 3 -> 3, of which waited for: 3 -> 3; matrix products, arithmetic and copies ran while one was open for 5% -> 1% of each run, Pallas kernels for 29% -> 21%
where the time goes in v3:
time: 77.4 us; the launch traced here: 76.7 us
  Pallas kernels  28.2 us (36%)
  waiting for transfers between devices  27.5 us (36%)
  starting transfers between devices  19.7 us (25%)
  local copies, waits for them, and re-layouts  0.82 us (1%)
    pallas_call x5, Pallas kernels, call(): pl.pallas_call(kernel, out_shape=out_shape, **specs, scratch_shapes=list(...  28.2 us
    all_to_all x1, waiting for transfers between devices, per_device(): lax.all_to_all(outgoing.reshape(patch_count, slot_count, merged), 'patch'...  14 us
    all_to_all x1, starting transfers between devices, per_device(): lax.all_to_all(outgoing.reshape(patch_count, slot_count, merged), 'patch'...  11.8 us
    all_to_all x1, waiting for transfers between devices, per_device(): lax.all_to_all(normed.reshape(group_count, per_group, merged), 'lev', spl...  6.83 us
    all_to_all x1, waiting for transfers between devices, per_device(): lax.all_to_all(attended, 'lev', split_axis=0, concat_axis=0, tiled=True)  6.65 us
    all_to_all x1, starting transfers between devices, per_device(): lax.all_to_all(normed.reshape(group_count, per_group, merged), 'lev', spl...  4.44 us
    all_to_all x1, starting transfers between devices, per_device(): lax.all_to_all(attended, 'lev', split_axis=0, concat_axis=0, tiled=True)  3.39 us
  transfers between devices with their start and end apart: 3, of which 3 were waited for; matrix products, arithmetic and copies ran while one was open for 1% of the time, Pallas kernels for 21%

profile of v3, /device:TPU:8, one launch (start us, length us, event | category | flops | bytes accessed | tf_op | source)
XLA Modules:
  0.0 76.7 jit_solution(15315735275777213934)
XLA Ops:
  0.0 2.3 %shard_map.182 = bf16[1536,384]{1,0:T(8,128)(2,1)} custom-call(s32[32,48]{1,0:T(8,128)} %halo_hbm.1, bf16[384,256]{1,0:T(8,128)(2,1)} %bitcast.31), custom_call_target="tpu_custom_call" | custom-call | tf_op jit(solution)/shard_map/pallas_call | solution.py:454
  2.3 0.0 copy-start.14
  2.3 0.0 copy-start.12
  2.4 0.0 copy-start.11
  2.4 0.0 copy-start.15
  2.4 0.0 copy-start.13
  2.4 0.0 copy-start
  2.4 0.0 copy-start.6
  2.4 0.0 copy-start.7
  2.4 11.8 %all-to-all-start = ((bf16[32,48,384]{2,1,0:T(8,128)(2,1)}), bf16[32,48,384]{2,1,0:T(8,128)(2,1)S(1)}, u32[]{:S(2)}, u32[]{:S(2)}) async-start(bf16[32,48,384]{2,1,0:T(8,128)(2,1)} %bitcast.10), calls=%async_computation | async-start | bytes 2359296 | tf_op jit(solution)/shard_map/all_to_all | solution.py:524
  14.3 0.0 copy-start.1
  14.3 0.0 copy-start.8
  14.3 0.0 copy-start.9
  14.3 0.0 copy-start.10
  14.3 0.0 copy-done.14
  14.3 0.1 dynamic_slice.3
  14.4 0.1 lt.48
  14.5 0.1 lt.44
  14.6 0.1 lt.45
  14.7 0.1 lt.50
  14.8 0.0 copy-done.12
  14.8 0.1 copy.25.node_w_in_ref
  14.9 0.0 copy-done.11
  15.0 0.2 copy.23.w_in_ref
  15.1 0.0 copy-done.15
  15.1 0.0 copy-done.13
  15.1 0.1 fusion.receiver_ref
  15.2 0.0 copy-done
  15.2 0.0 copy-done.6
  15.2 0.0 copy-done.7
  15.2 15.9 %shard_map.181 = (s32[1]{0:T(128)}, f32[768,128]{1,0:T(8,128)S(1)}, f32[768,192]{1,0:T(8,128)}, f32[768,192]{1,0:T(8,128)}, bf16[3,256,256]{2,1,0:T(8,128)(2,1)}...) custom-call(s32[16,128]{1,0:T(8,128)S(1)} %bitcast.25, ...), custom_call_target="tpu_custom_call" | custom-call | tf_op jit(solution)/shard_map/pallas_call | solution.py:454
  31.1 14.0 %all-to-all-done = bf16[32,48,384]{2,1,0:T(8,128)(2,1)S(1)} async-done(((bf16[32,48,384]{2,1,0:T(8,128)(2,1)}), bf16[32,48,384]{2,1,0:T(8,128)(2,1)S(1)}, u32[]{:S(2)}, u32[]{:S(2)}) %all-to-all-start) | async-done | bytes 1179680 | tf_op jit(solution)/shard_map/all_to_all | solution.py:524
  45.2 0.0 copy-done.1
  45.2 0.0 copy-done.8
  45.2 0.0 copy-done.9
  45.2 0.0 copy-done.10
  45.2 0.0 copy-start.3
  45.2 0.0 copy-start.4
  45.2 0.0 copy-start.5
  45.2 6.3 %shard_map.183 = (bf16[256,384]{1,0:T(8,128)(2,1)S(1)}, bf16[256,384]{1,0:T(8,128)(2,1)}) custom-call(s32[1]{0:T(128)} %get-tuple-element.19.tiles_ref, f32[768,128]{1,0:T(8,128)S(1)} %get-tuple-element.20.late_wanted_ref, f32[768,192]{1,0:T(8,128)} %get-tuple-element.21.late_pre0_hbm, f32[768,192]{1,0:T(8,128)} %get-tuple-element.22.late_pre1_hbm, ...), custom_call_target="tpu_custom_call" | custom-call | tf_op jit(solution)/shard_map/pallas_call | solution.py:454
  51.5 0.0 copy-start.2
  51.5 4.4 %all-to-all-start.1 = ((bf16[8,32,384]{2,1,0:T(8,128)(2,1)}), bf16[8,32,384]{2,1,0:T(8,128)(2,1)S(1)}, u32[]{:S(2)}, u32[]{:S(2)}) async-start(bf16[8,32,384]{2,1,0:T(8,128)(2,1)} %bitcast.12), calls=%async_computation.1 | async-start | bytes 393216 | tf_op jit(solution)/shard_map/all_to_all | solution.py:617
  56.0 6.8 %all-to-all-done.1.rows_ref = bf16[8,32,384]{2,1,0:T(8,128)(2,1)S(1)} async-done(((bf16[8,32,384]{2,1,0:T(8,128)(2,1)}), bf16[8,32,384]{2,1,0:T(8,128)(2,1)S(1)}, u32[]{:S(2)}, u32[]{:S(2)}) %all-to-all-start.1) | async-done | bytes 196640 | tf_op jit(solution)/shard_map/all_to_all | solution.py:617
  62.8 2.6 %shard_map.184 = bf16[8,32,384]{2,1,0:T(8,128)(2,1)} custom-call(bf16[8,32,384]{2,1,0:T(8,128)(2,1)S(1)} %all-to-all-done.1.rows_ref, f32[4,1,128]{2,1,0:T(1,128)S(1)} %compare_select_fusion.bias_ref, bf16[192,192]{1,0:T(8,128)(2,1)S(1)} %copy-done.3, bf16[192,192]{1,0:T(8,128)(2,1)S(1)} %copy-done.4, bf16[192,192]{1,0:T(8,128)(2,1)S(1)} %copy-done.5), custom_call_target="tpu_custom_call" | custom-call | tf_op jit(solution)/shard_map/pallas_call | solution.py:454
  65.4 3.4 %all-to-all-start.2 = ((bf16[8,32,384]{2,1,0:T(8,128)(2,1)}), bf16[8,32,384]{2,1,0:T(8,128)(2,1)S(1)}, u32[]{:S(2)}, u32[]{:S(2)}) async-start(bf16[8,32,384]{2,1,0:T(8,128)(2,1)} %shard_map.184), calls=%async_computation.2 | async-start | bytes 393216 | tf_op jit(solution)/shard_map/all_to_all | solution.py:634
  68.8 0.1 compare_convert_fusion.live_ref
  68.9 6.6 %all-to-all-done.2 = bf16[8,32,384]{2,1,0:T(8,128)(2,1)S(1)} async-done(((bf16[8,32,384]{2,1,0:T(8,128)(2,1)}), bf16[8,32,384]{2,1,0:T(8,128)(2,1)S(1)}, u32[]{:S(2)}, u32[]{:S(2)}) %all-to-all-start.2) | async-done | bytes 196640 | tf_op jit(solution)/shard_map/all_to_all | solution.py:634
  75.5 1.2 %shard_map.185 = bf16[2,192,256]{2,1,0:T(8,128)(2,1)} custom-call(bf16[256,384]{1,0:T(8,128)(2,1)S(1)} %get-tuple-element.31.state_ref, bf16[256,384]{1,0:T(8,128)(2,1)S(1)} %bitcast.24, f32[256,2]{1,0:T(8,128)S(1)} %compare_convert_fusion.live_ref, bf16[192,192]{1,0:T(8,128)(2,1)S(1)} %copy-done.2), custom_call_target="tpu_custom_call" | custom-call | tf_op jit(solution)/shard_map/pallas_call | solution.py:454
  (10 shorter events, 0.0 us)
Async XLA Ops:
  2.3 12.0 %copy-start.14 = (s32[256]{0:T(256)S(1)}, s32[256]{0:T(256)}, u32[]{:S(2)}) copy-start(s32[256]{0:T(256)} %param.25) | copy-start | bytes 3076
  2.3 12.4 %copy-start.12 = (bf16[384,192]{0,1:T(8,128)(2,1)S(1)}, bf16[384,192]{0,1:T(8,128)(2,1)}, u32[]{:S(2)}) copy-start(bf16[384,192]{0,1:T(8,128)(2,1)} %param.29) | copy-start | bytes 442372
  2.4 12.6 %copy-start.11 = (bf16[576,192]{0,1:T(8,128)(2,1)S(1)}, bf16[576,192]{0,1:T(8,128)(2,1)}, u32[]{:S(2)}) copy-start(bf16[576,192]{0,1:T(8,128)(2,1)} %param.26) | copy-start | bytes 663556
  2.4 12.8 %copy-start.15 = (s32[16]{0:T(128)S(1)}, s32[16]{0:T(128)}, u32[]{:S(2)}) copy-start(s32[16]{0:T(128)} %param.23) | copy-start | bytes 196
  2.4 12.8 %copy-start.13 = (s32[2048]{0:T(1024)S(1)}, s32[2048]{0:T(1024)}, u32[]{:S(2)}) copy-start(s32[2048]{0:T(1024)} %param.22) | copy-start | bytes 24580
  2.4 12.8 %copy-start = (bf16[192,192]{1,0:T(8,128)(2,1)S(1)}, bf16[192,192]{1,0:T(8,128)(2,1)}, u32[]{:S(2)}) copy-start(bf16[192,192]{1,0:T(8,128)(2,1)} %w_out_ref.3) | copy-start | bytes 221188
  2.4 12.8 %copy-start.6 = (s32[2048]{0:T(1024)S(1)}, s32[2048]{0:T(1024)}, u32[]{:S(2)}) copy-start(s32[2048]{0:T(1024)} %param.21) | copy-start | bytes 24580
  2.4 12.8 %copy-start.7 = (f32[192]{0:T(256)S(1)}, f32[192]{0:T(256)}, u32[]{:S(2)}) copy-start(f32[192]{0:T(256)} %param.27) | copy-start | bytes 2308
  2.4 42.7 %all-to-all-start = ((bf16[32,48,384]{2,1,0:T(8,128)(2,1)}), bf16[32,48,384]{2,1,0:T(8,128)(2,1)S(1)}, u32[]{:S(2)}, u32[]{:S(2)}) async-start(bf16[32,48,384]{2,1,0:T(8,128)(2,1)} %bitcast.10), calls=%async_computation | async-start | bytes 2359296 | tf_op jit(solution)/shard_map/all_to_all | solution.py:524
  14.3 30.9 %copy-start.1 = (bf16[192,192]{1,0:T(8,128)(2,1)S(1)}, bf16[192,192]{1,0:T(8,128)(2,1)}, u32[]{:S(2)}) copy-start(bf16[192,192]{1,0:T(8,128)(2,1)} %node_w_out_ref.1) | copy-start | bytes 221188
  14.3 30.9 %copy-start.8 = (f32[192]{0:T(256)S(1)}, f32[192]{0:T(256)}, u32[]{:S(2)}) copy-start(f32[192]{0:T(256)} %param.30) | copy-start | bytes 2308
  14.3 30.9 %copy-start.9 = (f32[192]{0:T(256)S(1)}, f32[192]{0:T(256)}, u32[]{:S(2)}) copy-start(f32[192]{0:T(256)} %param.32) | copy-start | bytes 2308
  14.3 30.9 %copy-start.10 = (f32[192]{0:T(256)S(1)}, f32[192]{0:T(256)}, u32[]{:S(2)}) copy-start(f32[192]{0:T(256)} %param.33) | copy-start | bytes 2308
  45.2 17.6 %copy-start.3 = (bf16[192,192]{1,0:T(8,128)(2,1)S(1)}, bf16[192,192]{1,0:T(8,128)(2,1)}, u32[]{:S(2)}) copy-start(bf16[192,192]{1,0:T(8,128)(2,1)} %query_ref.1) | copy-start | bytes 221188
  45.2 17.6 %copy-start.4 = (bf16[192,192]{1,0:T(8,128)(2,1)S(1)}, bf16[192,192]{1,0:T(8,128)(2,1)}, u32[]{:S(2)}) copy-start(bf16[192,192]{1,0:T(8,128)(2,1)} %key_ref.1) | copy-start | bytes 221188
  45.2 17.6 %copy-start.5 = (bf16[192,192]{1,0:T(8,128)(2,1)S(1)}, bf16[192,192]{1,0:T(8,128)(2,1)}, u32[]{:S(2)}) copy-start(bf16[192,192]{1,0:T(8,128)(2,1)} %value_ref.1) | copy-start | bytes 221188
  51.5 24.0 %copy-start.2 = (bf16[192,192]{1,0:T(8,128)(2,1)S(1)}, bf16[192,192]{1,0:T(8,128)(2,1)}, u32[]{:S(2)}) copy-start(bf16[192,192]{1,0:T(8,128)(2,1)} %weight_ref.1) | copy-start | bytes 221188
  51.5 11.3 %all-to-all-start.1 = ((bf16[8,32,384]{2,1,0:T(8,128)(2,1)}), bf16[8,32,384]{2,1,0:T(8,128)(2,1)S(1)}, u32[]{:S(2)}, u32[]{:S(2)}) async-start(bf16[8,32,384]{2,1,0:T(8,128)(2,1)} %bitcast.12), calls=%async_computation.1 | async-start | bytes 393216 | tf_op jit(solution)/shard_map/all_to_all | solution.py:617
  65.4 10.2 %all-to-all-start.2 = ((bf16[8,32,384]{2,1,0:T(8,128)(2,1)}), bf16[8,32,384]{2,1,0:T(8,128)(2,1)S(1)}, u32[]{:S(2)}, u32[]{:S(2)}) async-start(bf16[8,32,384]{2,1,0:T(8,128)(2,1)} %shard_map.184), calls=%async_computation.2 | async-start | bytes 393216 | tf_op jit(solution)/shard_map/all_to_all | solution.py:634

commit v4 on v3

--- a/solution.py
+++ b/solution.py
@@ -14,6 +14,8 @@
 WIDE = 256
 LATE_TILES = 3
 CHUNK = 8
+CHIPS = 4
+CORES = 2
 
 
 def dot(a, b):
@@ -106,6 +108,7 @@
 
 
 def local_kernel(
+    place_ref,
     sender_ref,
     receiver_ref,
     attr_hbm,
@@ -170,6 +173,7 @@
     used_tiles = (jnp.sum(1.0 - is_empty).astype(jnp.int32) + WIDE - 1) // WIDE
     late_tiles = jnp.maximum(remote_tiles, LATE_TILES)
     tiles_ref[0] = late_tiles
+    tiles_ref[1] = place_ref[0]
     for fetch in fetches:
         fetch.wait()
     own_rows_ref[...] = dot_lanes(eye, own_ref[...]).astype(BF16)
@@ -276,6 +280,10 @@
     attention_gain_ref,
     remote_ref,
     state_ref,
+    out0_ref,
+    out1_ref,
+    out2_ref,
+    out3_ref,
     normed_ref,
     pre0_ref,
     pre1_ref,
@@ -374,79 +382,78 @@
         )
     state_ref[...] = merge_levels(*states)
     normed_ref[...] = merge_levels(*normed)
-
-
-def attention_kernel(rows_ref, bias_ref, query_ref, key_ref, value_ref, out_ref, mix_ref):
-    group_count, item_count, merged = rows_ref.shape
+    share = out0_ref.shape[0]
+    for shift, out_ref in enumerate((out0_ref, out1_ref, out2_ref, out3_ref)):
+        block = lax.rem(tiles_ref[1] + shift, CHIPS)
+        out_ref[...] = normed_ref[pl.ds(pl.multiple_of(block * share, share), share), :]
+
+
+def attention_kernel(*refs):
+    block_refs, refs = refs[: CHIPS * CORES], refs[CHIPS * CORES :]
+    bias_ref, query_ref, key_ref, value_ref, *out_refs, mix_ref = refs
+    block_count = len(block_refs)
+    item_count, merged = block_refs[0].shape
     width = merged // 2
     head_width = width // HEADS
     scale = 1.0 / math.sqrt(head_width)
-    chunk = CHUNK
-    half = group_count * chunk
-    total = 2 * half
+    key_total = 2 * block_count * CHUNK
+    query_total = 2 * CHIPS * CHUNK
     head_of = lax.broadcasted_iota(jnp.int32, (1, width), 1) // head_width
-    row_node = lax.broadcasted_iota(jnp.int32, (total, total), 0) % chunk
-    col_node = lax.broadcasted_iota(jnp.int32, (total, total), 1) % chunk
-    same_node = row_node == col_node
-    merged_rows = rows_ref[...].reshape(group_count * item_count, merged)
-
-    def project(weight_ref):
+    same_node = (
+        lax.broadcasted_iota(jnp.int32, (query_total, key_total), 0) % CHUNK
+        == lax.broadcasted_iota(jnp.int32, (query_total, key_total), 1) % CHUNK
+    )
+    blocks = jnp.concatenate([ref[...] for ref in block_refs], axis=0)
+
+    def project(count, weight_ref):
         return [
-            p.reshape(group_count, item_count, width)
-            for p in level_pair(merged_rows, weight_ref[...])
+            p.reshape(count, item_count, width)
+            for p in level_pair(blocks[: count * item_count], weight_ref[...])
         ]
 
     def rows_of(pair, part):
-        items = slice(part * chunk, (part + 1) * chunk)
-        return jnp.concatenate([p[:, items, :].reshape(half, width) for p in pair], axis=0)
-
-    queries, keys, values = project(query_ref), project(key_ref), project(value_ref)
-    ones = jnp.concatenate(
-        [
-            jnp.broadcast_to(jnp.where(head_of == head, 1.0, 0.0), (total, width))
-            for head in range(HEADS)
-        ],
-        axis=0,
-    ).astype(BF16)
-    for part in range(item_count // chunk):
-        part_queries = rows_of(queries, part).astype(BF16)
-        part_keys = rows_of(keys, part)
-        part_values = rows_of(values, part)
+        items = slice(part * CHUNK, (part + 1) * CHUNK)
+        return jnp.concatenate([p[:, items, :].reshape(-1, width) for p in pair], axis=0)
+
+    def per_head(rows):
+        return jnp.concatenate(
+            [jnp.where(head_of == head, rows, 0.0).astype(BF16) for head in range(HEADS)], axis=0
+        )
+
+    queries = project(CHIPS, query_ref)
+    keys, values = project(block_count, key_ref), project(block_count, value_ref)
+    ones = per_head(jnp.ones((key_total, width), F32))
+    for part in range(item_count // CHUNK):
         bias = jnp.where(same_node, bias_ref[part], -1e30)
-        stacked_keys = jnp.concatenate(
-            [jnp.where(head_of == head, part_keys, 0.0).astype(BF16) for head in range(HEADS)],
-            axis=0,
-        )
-        stacked_values = jnp.concatenate(
-            [jnp.where(head_of == head, part_values, 0.0).astype(BF16) for head in range(HEADS)],
-            axis=0,
-        )
-        scores = dot_lanes(part_queries, stacked_keys)
+        scores = dot_lanes(rows_of(queries, part).astype(BF16), per_head(rows_of(keys, part)))
         powers = []
         for head in range(HEADS):
-            own_scores = scores[:, head * total : (head + 1) * total] * scale + bias
+            own_scores = scores[:, head * key_total : (head + 1) * key_total] * scale + bias
             top = jnp.max(own_scores, axis=-1, keepdims=True)
             powers.append(jnp.exp(own_scores - top).astype(BF16))
         powers = jnp.concatenate(powers, axis=1)
-        attended = dot(powers, stacked_values) / dot(powers, ones)
-        items = slice(part * chunk, (part + 1) * chunk)
-        for level in range(2):
-            mix_ref[level, :, items, :] = attended[level * half : (level + 1) * half].reshape(
-                group_count, chunk, width
-            )
-    mixed = [
-        mix_ref[level].reshape(group_count * item_count, width).astype(BF16) for level in range(2)
-    ]
-    out_ref[...] = merge_levels(*mixed).reshape(group_count, item_count, merged)
-
-
-def output_kernel(state_ref, attended_ref, live_ref, weight_ref, out_ref):
+        attended = dot(powers, per_head(rows_of(values, part))) / dot(powers, ones)
+        mix_ref[:, :, part * CHUNK : (part + 1) * CHUNK, :] = attended.reshape(
+            2, CHIPS, CHUNK, width
+        )
+    for chip, out_ref in enumerate(out_refs):
+        out_ref[...] = merge_levels(mix_ref[0, chip].astype(BF16), mix_ref[1, chip].astype(BF16))
+
+
+def output_kernel(
+    place_ref, state_ref, part0_ref, part1_ref, part2_ref, part3_ref, live_ref, weight_ref, out_ref,
+    attended_ref,
+):
     width = weight_ref.shape[0]
+    share = part0_ref.shape[0]
+    for shift, part_ref in enumerate((part0_ref, part1_ref, part2_ref, part3_ref)):
+        block = lax.rem(place_ref[1] + shift, CHIPS)
+        attended_ref[pl.ds(pl.multiple_of(block * share, share), share), :] = part_ref[...]
     mixed = level_pair(attended_ref[...], weight_ref[...])
     state = state_ref[...].astype(F32)
     for level in range(2):
-        kept = mixed[level] * live_ref[:, level : level + 1]
-        result = state[:, level * width : (level + 1) * width] + kept
+        live_part = mixed[level] * live_ref[:, level : level + 1]
+        result = state[:, level * width : (level + 1) * width] + live_part
         out_ref[level] = result.T.astype(BF16)
 
 
@@ -532,16 +539,20 @@
     senders = edge_sender.reshape(tile_count, 128)
     in_block = edge_receiver.reshape(tile_count, 128)
     receivers = jnp.where(in_block >= 0, tile_block[:, None] * 128 + in_block, -1)
-    per_group = node_dev // group_count
+    share = node_dev // CHIPS
     me = lax.axis_index("lev")
-    mine = lax.dynamic_slice_in_dim(valid_levels, me * per_group, per_group)
+    chip, core = me // CORES, me % CORES
+    mine = lax.dynamic_slice_in_dim(valid_levels, chip * share, share)
+    block = jnp.arange(CHIPS * CORES, dtype=jnp.int32)
+    from_chip = (chip - block % CHIPS) % CHIPS
+    from_core = jnp.where(block < CHIPS, core, 1 - core)
     level_of = (
-        jnp.arange(group_count, dtype=jnp.int32)[None, :, None] * lev_dev
+        ((from_chip * CORES + from_core) * lev_dev)[None, :, None]
         + jnp.arange(lev_dev, dtype=jnp.int32)[:, None, None]
     )
     key_bias = jnp.where(
-        level_of[None] < mine.reshape(per_group // CHUNK, 1, 1, CHUNK), 0.0, -1e30
-    ).reshape(per_group // CHUNK, 1, lev_dev * group_count * CHUNK)
+        level_of[None] < mine.reshape(share // CHUNK, 1, 1, CHUNK), 0.0, -1e30
+    ).reshape(share // CHUNK, 1, lev_dev * group_count * CHUNK)
     levels = me * lev_dev + jnp.arange(lev_dev, dtype=jnp.int32)
     live = (levels[None, :] < valid_levels[:, None]).astype(F32)
 
@@ -556,7 +567,7 @@
     tiles, wanted, *tail = call(
         local_kernel,
         (
-            shape((1,), jnp.int32),
+            shape((2,), jnp.int32),
             pltpu.VMEM((late, 128), F32),
             pltpu.HBM((late, width), F32),
             pltpu.HBM((late, width), F32),
@@ -569,6 +580,7 @@
             pltpu.HBM((rest, WIDE, 128), F32),
             pltpu.HBM((rest, node_dev, WIDE), BF16),
         ),
+        chip.reshape(1),
         senders,
         receivers,
         in_hbm(edge_attr.T),
@@ -584,12 +596,12 @@
             pltpu.SemaphoreType.DMA((4,)),
             pltpu.SemaphoreType.DMA((2,)),
         ],
-        in_specs=[IN_VMEM] * 2 + [ANYWHERE] * 2 + [IN_VMEM] * 3,
+        in_specs=[IN_SMEM] + [IN_VMEM] * 2 + [ANYWHERE] * 2 + [IN_VMEM] * 3,
         out_specs=[IN_SMEM] + [IN_VMEM] * 7 + [ANYWHERE] * 4,
     )
-    state, normed = call(
+    state, *blocks = call(
         edge_kernel,
-        (pltpu.VMEM((node_dev, merged), BF16), shape((node_dev, merged))),
+        (pltpu.VMEM((node_dev, merged), BF16), *[shape((share, merged))] * CHIPS),
         tiles,
         kept(wanted),
         *(in_hbm(array) for array in tail),
@@ -602,6 +614,7 @@
         attention_gain[None, :],
         incoming,
         scratch=[
+            pltpu.VMEM((node_dev, merged), BF16),
             pltpu.VMEM((late, width), F32),
             pltpu.VMEM((late, width), F32),
             pltpu.VMEM((LATE_TILES, node_dev, WIDE), BF16),
@@ -614,33 +627,44 @@
         ],
         in_specs=[IN_SMEM, IN_VMEM] + [ANYWHERE] * 10 + [IN_VMEM] * 8,
     )
-    columns = lax.all_to_all(
-        normed.reshape(group_count, per_group, merged),
-        "lev",
-        split_axis=0,
-        concat_axis=0,
-        tiled=True,
-    )
+
+    def to_chip(array, shift):
+        return lax.ppermute(
+            array,
+            "lev",
+            [
+                (a * CORES + b, (a + shift) % CHIPS * CORES + b)
+                for a in range(CHIPS)
+                for b in range(CORES)
+            ],
+        )
+
+    def to_core(array):
+        return lax.ppermute(array, "lev", [(a, a ^ 1) for a in range(CHIPS * CORES)])
+
+    blocks = blocks[:1] + [to_chip(blocks[shift], shift) for shift in range(1, CHIPS)]
+    blocks = blocks + [to_core(array) for array in blocks]
     attended = call(
         attention_kernel,
-        shape((group_count, per_group, merged)),
-        columns,
+        [shape((share, merged))] * CHIPS,
+        *blocks,
         key_bias,
         query_weight,
         key_weight,
         value_weight,
-        scratch=[pltpu.VMEM((lev_dev, group_count, per_group, width), F32)],
-    )
-    returned = lax.all_to_all(
-        attended, "lev", split_axis=0, concat_axis=0, tiled=True
-    ).reshape(node_dev, merged)
+        scratch=[pltpu.VMEM((lev_dev, CHIPS, share, width), F32)],
+    )
+    returned = [attended[0]] + [to_chip(attended[shift], -shift) for shift in range(1, CHIPS)]
     out = call(
         output_kernel,
         shape((lev_dev, width, node_dev)),
+        tiles,
         kept(state),
-        returned,
+        *returned,
         live,
         output_weight,
+        scratch=[pltpu.VMEM((node_dev, merged), BF16)],
+        in_specs=[IN_SMEM] + [IN_VMEM] * 7,
     )
     return out.transpose(2, 0, 1)
 

time: 77.4 us -> 74.2 us (0.959)
  waiting for transfers between devices: 27.5 us -> 22.1 us
  starting transfers between devices: 19.7 us -> 21.8 us
    all_to_all x2 -> x0, waiting for transfers between devices: 13.5 us -> none  [the longest x1 6.83 us: per_device(): lax.all_to_all(normed.reshape(group_count, per_group, merged), 'lev', spl...]
    ppermute x0 -> x10, starting transfers between devices: none -> 9.92 us  [the longest x6 9.41 us: to_chip(): lax.ppermute(array, 'lev', [(a * CORES + b, (a + shift) % CHIPS * CORES +...]
    ppermute x0 -> x10, waiting for transfers between devices: none -> 8.1 us  [the longest x6 6.9 us: to_chip(): lax.ppermute(array, 'lev', [(a * CORES + b, (a + shift) % CHIPS * CORES +...]
    all_to_all x2 -> x0, starting transfers between devices: 7.83 us -> none  [the longest x1 4.44 us: per_device(): lax.all_to_all(normed.reshape(group_count, per_group, merged), 'lev', spl...]
  transfers between devices with their start and end apart: 3 -> 11, of which waited for: 3 -> 7; matrix products, arithmetic and copies ran while one was open for 1% -> 1% of each run, Pallas kernels for 21% -> 22%
where the time goes in v4:
time: 74.2 us; the launch traced here: 73.9 us
  Pallas kernels  28.7 us (39%)
  waiting for transfers between devices  22.1 us (30%)
  starting transfers between devices  21.8 us (29%)
  local copies, waits for them, and re-layouts  0.82 us (1%)
    pallas_call x5, Pallas kernels, call(): pl.pallas_call(kernel, out_shape=out_shape, **specs, scratch_shapes=list(...  28.7 us
    all_to_all x1, waiting for transfers between devices, per_device(): lax.all_to_all(outgoing.reshape(patch_count, slot_count, merged), 'patch'...  14 us
    all_to_all x1, starting transfers between devices, per_device(): lax.all_to_all(outgoing.reshape(patch_count, slot_count, merged), 'patch'...  11.8 us
    ppermute x6, starting transfers between devices, to_chip(): lax.ppermute(array, 'lev', [(a * CORES + b, (a + shift) % CHIPS * CORES +...  9.41 us
    ppermute x6, waiting for transfers between devices, to_chip(): lax.ppermute(array, 'lev', [(a * CORES + b, (a + shift) % CHIPS * CORES +...  6.9 us
  transfers between devices with their start and end apart: 11, of which 7 were waited for; matrix products, arithmetic and copies ran while one was open for 1% of the time, Pallas kernels for 22%

profile of v4, /device:TPU:8, one launch (start us, length us, event | category | flops | bytes accessed | tf_op | source)
XLA Modules:
  0.0 73.9 jit_solution(2560493793827237810)
XLA Ops:
  0.0 2.3 %shard_map.182 = bf16[1536,384]{1,0:T(8,128)(2,1)} custom-call(s32[32,48]{1,0:T(8,128)} %halo_hbm.1, bf16[384,256]{1,0:T(8,128)(2,1)} %bitcast.29), custom_call_target="tpu_custom_call" | custom-call | tf_op jit(solution)/shard_map/pallas_call | solution.py:461
  2.3 0.0 copy-start.14
  2.3 0.0 copy-start.12
  2.4 0.0 copy-start.11
  2.4 0.0 copy-start.15
  2.4 0.0 copy-start.13
  2.4 0.0 copy-start
  2.4 0.0 copy-start.6
  2.4 0.0 copy-start.7
  2.4 11.8 %all-to-all-start = ((bf16[32,48,384]{2,1,0:T(8,128)(2,1)}), bf16[32,48,384]{2,1,0:T(8,128)(2,1)S(1)}, u32[]{:S(2)}, u32[]{:S(2)}) async-start(bf16[32,48,384]{2,1,0:T(8,128)(2,1)} %bitcast.11), calls=%async_computation | async-start | bytes 2359296 | tf_op jit(solution)/shard_map/all_to_all | solution.py:531
  14.3 0.0 copy-start.1
  14.3 0.0 copy-start.8
  14.3 0.0 copy-start.9
  14.3 0.0 copy-start.10
  14.4 0.1 dynamic_slice.3
  14.4 0.1 lt.75
  14.6 0.1 lt.71
  14.6 0.1 lt.72
  14.7 0.1 lt.77
  14.8 0.1 copy.25.node_w_in_ref
  15.0 0.2 copy.23.w_in_ref
  15.2 0.1 fusion.receiver_ref
  15.3 15.9 %shard_map.181 = (s32[2]{0:T(128)S(1)}, f32[768,128]{1,0:T(8,128)S(1)}, f32[768,192]{1,0:T(8,128)}, f32[768,192]{1,0:T(8,128)}, bf16[3,256,256]{2,1,0:T(8,128)(2...) custom-call(s32[1]{0:T(128)} %bitcast.place_ref, ...), custom_call_target="tpu_custom_call" | custom-call | tf_op jit(solution)/shard_map/pallas_call | solution.py:461
  31.2 14.0 %all-to-all-done = bf16[32,48,384]{2,1,0:T(8,128)(2,1)S(1)} async-done(((bf16[32,48,384]{2,1,0:T(8,128)(2,1)}), bf16[32,48,384]{2,1,0:T(8,128)(2,1)S(1)}, u32[]{:S(2)}, u32[]{:S(2)}) %all-to-all-start) | async-done | bytes 1179680 | tf_op jit(solution)/shard_map/all_to_all | solution.py:531
  45.2 0.0 copy-start.2
  45.2 0.0 copy-start.3
  45.2 0.0 copy-start.4
  45.2 0.0 copy-start.5
  45.2 5.5 %shard_map.183 = (bf16[256,384]{1,0:T(8,128)(2,1)S(1)}, bf16[64,384]{1,0:T(8,128)(2,1)S(1)}, bf16[64,384]{1,0:T(8,128)(2,1)S(1)}, bf16[64,384]{1,0:T(8,128)(2,1)S(1)}, bf16[64,384]{1,0:T(8,128)(2,1)S(1)}) custom-call(s32[2]{0:T(128)S(1)} %get-tuple-element.26.tiles_ref.place_ref, f32[768,128]{1,0:T(8,128)S(1)} %get-tuple-element.27.late_wanted_ref, ...), custom_call_target="tpu_custom_call" | custom-call | tf_op jit(solution)/shard_map/pallas_call | solution.py:461
  50.8 1.6 %collective-permute-start = (bf16[64,384]{1,0:T(8,128)(2,1)S(1)}, bf16[64,384]{1,0:T(8,128)(2,1)S(1)}, u32[]{:S(2)}, u32[]{:S(2)}) collective-permute-start(bf16[64,384]{1,0:T(8,128)(2,1)S(1)} %get-tuple-element.40), channel_id=1, source_target_pairs={{0,2},{1,3},{2,4},{3,5},{4,6},{5,7},{6,0},{7,1},{8,10},{9,11},{10,... | collective-permute-start | bytes 147464 | tf_op jit(solution)/shard_map/ppermute | solution.py:632
  52.4 2.7 %collective-permute-start.1 = (bf16[64,384]{1,0:T(8,128)(2,1)S(1)}, bf16[64,384]{1,0:T(8,128)(2,1)S(1)}, u32[]{:S(2)}, u32[]{:S(2)}) collective-permute-start(bf16[64,384]{1,0:T(8,128)(2,1)S(1)} %get-tuple-element.41), channel_id=1, source_target_pairs={{0,4},{1,5},{2,6},{3,7},{4,0},{5,1},{6,2},{7,3},{8,12},{9,13},{10,... | collective-permute-start | bytes 147464 | tf_op jit(solution)/shard_map/ppermute | solution.py:632
  55.1 1.4 %collective-permute-start.2 = (bf16[64,384]{1,0:T(8,128)(2,1)S(1)}, bf16[64,384]{1,0:T(8,128)(2,1)S(1)}, u32[]{:S(2)}, u32[]{:S(2)}) collective-permute-start(bf16[64,384]{1,0:T(8,128)(2,1)S(1)} %get-tuple-element.42), channel_id=1, source_target_pairs={{0,6},{1,7},{2,0},{3,1},{4,2},{5,3},{6,4},{7,5},{8,14},{9,15},{10,... | collective-permute-start | bytes 147464 | tf_op jit(solution)/shard_map/ppermute | solution.py:632
  56.5 0.0 collective-permute-start.3
  56.5 0.5 collective-permute-start.4
  57.0 0.9 %collective-permute-done.1.refs_2_ = bf16[64,384]{1,0:T(8,128)(2,1)S(1)} collective-permute-done((bf16[64,384]{1,0:T(8,128)(2,1)S(1)}, bf16[64,384]{1,0:T(8,128)(2,1)S(1)}, u32[]{:S(2)}, u32[]{:S(2)}) %collective-permute-start.1) | collective-permute-done | bytes 49184 | tf_op jit(solution)/shard_map/ppermute | solution.py:632
  58.0 0.0 collective-permute-start.5
  58.0 1.2 %collective-permute-done.2.refs_3_ = bf16[64,384]{1,0:T(8,128)(2,1)S(1)} collective-permute-done((bf16[64,384]{1,0:T(8,128)(2,1)S(1)}, bf16[64,384]{1,0:T(8,128)(2,1)S(1)}, u32[]{:S(2)}, u32[]{:S(2)}) %collective-permute-start.2) | collective-permute-done | bytes 49184 | tf_op jit(solution)/shard_map/ppermute | solution.py:632
  59.2 0.0 collective-permute-start.6
  59.2 0.0 collective-permute-done.3.refs_4_
  59.2 1.2 %collective-permute-done.6.refs_7_ = bf16[64,384]{1,0:T(8,128)(2,1)S(1)} collective-permute-done((bf16[64,384]{1,0:T(8,128)(2,1)S(1)}, bf16[64,384]{1,0:T(8,128)(2,1)S(1)}, u32[]{:S(2)}, u32[]{:S(2)}) %collective-permute-start.6) | collective-permute-done | bytes 49184 | tf_op jit(solution)/shard_map/ppermute | solution.py:643
  60.4 3.2 %shard_map.184 = (bf16[64,384]{1,0:T(8,128)(2,1)S(1)}, bf16[64,384]{1,0:T(8,128)(2,1)S(1)}, bf16[64,384]{1,0:T(8,128)(2,1)S(1)}, bf16[64,384]{1,0:T(8,128)(2,1)S(1)}) custom-call(bf16[64,384]{1,0:T(8,128)(2,1)S(1)} %get-tuple-element.39.refs_0_, bf16[64,384]{1,0:T(8,128)(2,1)S(1)} %collective-permute-done.refs_1_, ...), custom_call_target="tpu_custom_call" | custom-call | tf_op jit(solution)/shard_map/pallas_call | solution.py:461
  63.7 2.7 %collective-permute-start.7 = (bf16[64,384]{1,0:T(8,128)(2,1)S(1)}, bf16[64,384]{1,0:T(8,128)(2,1)S(1)}, u32[]{:S(2)}, u32[]{:S(2)}) collective-permute-start(bf16[64,384]{1,0:T(8,128)(2,1)S(1)} %get-tuple-element.44), channel_id=1, source_target_pairs={{0,6},{1,7},{2,0},{3,1},{4,2},{5,3},{6,4},{7,5},{8,14},{9,15},{10,... | collective-permute-start | bytes 147464 | tf_op jit(solution)/shard_map/ppermute | solution.py:632
  66.4 1.0 %collective-permute-start.9 = (bf16[64,384]{1,0:T(8,128)(2,1)S(1)}, bf16[64,384]{1,0:T(8,128)(2,1)S(1)}, u32[]{:S(2)}, u32[]{:S(2)}) collective-permute-start(bf16[64,384]{1,0:T(8,128)(2,1)S(1)} %get-tuple-element.46), channel_id=1, source_target_pairs={{0,2},{1,3},{2,4},{3,5},{4,6},{5,7},{6,0},{7,1},{8,10},{9,11},{10,... | collective-permute-start | bytes 147464 | tf_op jit(solution)/shard_map/ppermute | solution.py:632
  67.4 0.1 compare_convert_fusion.live_ref
  67.5 1.3 %collective-permute-done.7.part1_ref = bf16[64,384]{1,0:T(8,128)(2,1)S(1)} collective-permute-done((bf16[64,384]{1,0:T(8,128)(2,1)S(1)}, bf16[64,384]{1,0:T(8,128)(2,1)S(1)}, u32[]{:S(2)}, u32[]{:S(2)}) %collective-permute-start.7) | collective-permute-done | bytes 49184 | tf_op jit(solution)/shard_map/ppermute | solution.py:632
  68.8 3.2 %collective-permute-done.8.part2_ref = bf16[64,384]{1,0:T(8,128)(2,1)S(1)} collective-permute-done((bf16[64,384]{1,0:T(8,128)(2,1)S(1)}, bf16[64,384]{1,0:T(8,128)(2,1)S(1)}, u32[]{:S(2)}, u32[]{:S(2)}) %collective-permute-start.8) | collective-permute-done | bytes 49184 | tf_op jit(solution)/shard_map/ppermute | solution.py:632
  72.0 0.2 collective-permute-done.9.part3_ref
  72.2 1.7 %shard_map.185 = bf16[2,192,256]{2,1,0:T(8,128)(2,1)} custom-call(s32[2]{0:T(128)S(1)} %get-tuple-element.26.tiles_ref.place_ref, bf16[256,384]{1,0:T(8,128)(2,1)S(1)} %get-tuple-element.38.state_ref, bf16[64,384]{1,0:T(8,128)(2,1)S(1)} %get-tuple-element.43.part0_ref, bf16[64,384]{1,0:T(8,128)(2,1)S(1)} %collective-permute-done.7.part1_ref, ...), custom_call_target="tpu_custom_call" | custom-call | tf_op jit(solution)/shard_map/pallas_call | solution.py:461
  (26 shorter events, 0.1 us)
Async XLA Ops:
  2.3 12.0 %copy-start.14 = (s32[256]{0:T(256)S(1)}, s32[256]{0:T(256)}, u32[]{:S(2)}) copy-start(s32[256]{0:T(256)} %param.25) | copy-start | bytes 3076
  2.3 12.5 %copy-start.12 = (bf16[384,192]{0,1:T(8,128)(2,1)S(1)}, bf16[384,192]{0,1:T(8,128)(2,1)}, u32[]{:S(2)}) copy-start(bf16[384,192]{0,1:T(8,128)(2,1)} %param.29) | copy-start | bytes 442372
  2.4 12.6 %copy-start.11 = (bf16[576,192]{0,1:T(8,128)(2,1)S(1)}, bf16[576,192]{0,1:T(8,128)(2,1)}, u32[]{:S(2)}) copy-start(bf16[576,192]{0,1:T(8,128)(2,1)} %param.26) | copy-start | bytes 663556
  2.4 12.8 %copy-start.15 = (s32[16]{0:T(128)S(1)}, s32[16]{0:T(128)}, u32[]{:S(2)}) copy-start(s32[16]{0:T(128)} %param.23) | copy-start | bytes 196
  2.4 12.8 %copy-start.13 = (s32[2048]{0:T(1024)S(1)}, s32[2048]{0:T(1024)}, u32[]{:S(2)}) copy-start(s32[2048]{0:T(1024)} %param.22) | copy-start | bytes 24580
  2.4 12.9 %copy-start = (bf16[192,192]{1,0:T(8,128)(2,1)S(1)}, bf16[192,192]{1,0:T(8,128)(2,1)}, u32[]{:S(2)}) copy-start(bf16[192,192]{1,0:T(8,128)(2,1)} %w_out_ref.3) | copy-start | bytes 221188
  2.4 12.9 %copy-start.6 = (s32[2048]{0:T(1024)S(1)}, s32[2048]{0:T(1024)}, u32[]{:S(2)}) copy-start(s32[2048]{0:T(1024)} %param.21) | copy-start | bytes 24580
  2.4 12.9 %copy-start.7 = (f32[192]{0:T(256)S(1)}, f32[192]{0:T(256)}, u32[]{:S(2)}) copy-start(f32[192]{0:T(256)} %param.27) | copy-start | bytes 2308
  2.4 42.7 %all-to-all-start = ((bf16[32,48,384]{2,1,0:T(8,128)(2,1)}), bf16[32,48,384]{2,1,0:T(8,128)(2,1)S(1)}, u32[]{:S(2)}, u32[]{:S(2)}) async-start(bf16[32,48,384]{2,1,0:T(8,128)(2,1)} %bitcast.11), calls=%async_computation | async-start | bytes 2359296 | tf_op jit(solution)/shard_map/all_to_all | solution.py:531
  14.3 30.9 %copy-start.1 = (bf16[192,192]{1,0:T(8,128)(2,1)S(1)}, bf16[192,192]{1,0:T(8,128)(2,1)}, u32[]{:S(2)}) copy-start(bf16[192,192]{1,0:T(8,128)(2,1)} %node_w_out_ref.1) | copy-start | bytes 221188
  14.3 30.9 %copy-start.8 = (f32[192]{0:T(256)S(1)}, f32[192]{0:T(256)}, u32[]{:S(2)}) copy-start(f32[192]{0:T(256)} %param.30) | copy-start | bytes 2308
  14.3 30.9 %copy-start.9 = (f32[192]{0:T(256)S(1)}, f32[192]{0:T(256)}, u32[]{:S(2)}) copy-start(f32[192]{0:T(256)} %param.32) | copy-start | bytes 2308
  14.3 30.9 %copy-start.10 = (f32[192]{0:T(256)S(1)}, f32[192]{0:T(256)}, u32[]{:S(2)}) copy-start(f32[192]{0:T(256)} %param.33) | copy-start | bytes 2308
  45.2 15.2 %copy-start.2 = (bf16[192,192]{1,0:T(8,128)(2,1)S(1)}, bf16[192,192]{1,0:T(8,128)(2,1)}, u32[]{:S(2)}) copy-start(bf16[192,192]{1,0:T(8,128)(2,1)} %refs_9_.1) | copy-start | bytes 221188
  45.2 15.2 %copy-start.3 = (bf16[192,192]{1,0:T(8,128)(2,1)S(1)}, bf16[192,192]{1,0:T(8,128)(2,1)}, u32[]{:S(2)}) copy-start(bf16[192,192]{1,0:T(8,128)(2,1)} %refs_10_.1) | copy-start | bytes 221188
  45.2 15.2 %copy-start.4 = (bf16[192,192]{1,0:T(8,128)(2,1)S(1)}, bf16[192,192]{1,0:T(8,128)(2,1)}, u32[]{:S(2)}) copy-start(bf16[192,192]{1,0:T(8,128)(2,1)} %refs_11_.1) | copy-start | bytes 221188
  45.2 27.0 %copy-start.5 = (bf16[192,192]{1,0:T(8,128)(2,1)S(1)}, bf16[192,192]{1,0:T(8,128)(2,1)}, u32[]{:S(2)}) copy-start(bf16[192,192]{1,0:T(8,128)(2,1)} %weight_ref.1) | copy-start | bytes 221188
  50.8 5.8 %collective-permute-start = (bf16[64,384]{1,0:T(8,128)(2,1)S(1)}, bf16[64,384]{1,0:T(8,128)(2,1)S(1)}, u32[]{:S(2)}, u32[]{:S(2)}) collective-permute-start(bf16[64,384]{1,0:T(8,128)(2,1)S(1)} %get-tuple-element.40), channel_id=1, source_target_pairs={{0,2},{1,3},{2,4},{3,5},{4,6},{5,7},{6,0},{7,1},{8,10},{9,11},{10,... | collective-permute-start | bytes 147464 | tf_op jit(solution)/shard_map/ppermute | solution.py:632
  52.4 5.6 %collective-permute-start.1 = (bf16[64,384]{1,0:T(8,128)(2,1)S(1)}, bf16[64,384]{1,0:T(8,128)(2,1)S(1)}, u32[]{:S(2)}, u32[]{:S(2)}) collective-permute-start(bf16[64,384]{1,0:T(8,128)(2,1)S(1)} %get-tuple-element.41), channel_id=1, source_target_pairs={{0,4},{1,5},{2,6},{3,7},{4,0},{5,1},{6,2},{7,3},{8,12},{9,13},{10,... | collective-permute-start | bytes 147464 | tf_op jit(solution)/shard_map/ppermute | solution.py:632
  55.1 4.1 %collective-permute-start.2 = (bf16[64,384]{1,0:T(8,128)(2,1)S(1)}, bf16[64,384]{1,0:T(8,128)(2,1)S(1)}, u32[]{:S(2)}, u32[]{:S(2)}) collective-permute-start(bf16[64,384]{1,0:T(8,128)(2,1)S(1)} %get-tuple-element.42), channel_id=1, source_target_pairs={{0,6},{1,7},{2,0},{3,1},{4,2},{5,3},{6,4},{7,5},{8,14},{9,15},{10,... | collective-permute-start | bytes 147464 | tf_op jit(solution)/shard_map/ppermute | solution.py:632
  56.5 2.7 %collective-permute-start.3 = (bf16[64,384]{1,0:T(8,128)(2,1)S(1)}, bf16[64,384]{1,0:T(8,128)(2,1)S(1)}, u32[]{:S(2)}, u32[]{:S(2)}) collective-permute-start(bf16[64,384]{1,0:T(8,128)(2,1)S(1)} %get-tuple-element.39.refs_0_), channel_id=1, source_target_pairs={{0,1},{1,0},{2,3},{3,2},{4,5},{5,4},{6,7},{7,6},{8,9},{9,8},{10,11... | collective-permute-start | bytes 147464 | tf_op jit(solution)/shard_map/ppermute | solution.py:643
  56.5 2.6 %collective-permute-start.4 = (bf16[64,384]{1,0:T(8,128)(2,1)S(1)}, bf16[64,384]{1,0:T(8,128)(2,1)S(1)}, u32[]{:S(2)}, u32[]{:S(2)}) collective-permute-start(bf16[64,384]{1,0:T(8,128)(2,1)S(1)} %collective-permute-done.refs_1_), channel_id=1, source_target_pairs={{0,1},{1,0},{2,3},{3,2},{4,5},{5,4},{6,7},{7,6},{8,9},{9,8},{10,11... | collective-permute-start | bytes 147464 | tf_op jit(solution)/shard_map/ppermute | solution.py:643
  58.0 1.3 %collective-permute-start.5 = (bf16[64,384]{1,0:T(8,128)(2,1)S(1)}, bf16[64,384]{1,0:T(8,128)(2,1)S(1)}, u32[]{:S(2)}, u32[]{:S(2)}) collective-permute-start(bf16[64,384]{1,0:T(8,128)(2,1)S(1)} %collective-permute-done.1.refs_2_), channel_id=1, source_target_pairs={{0,1},{1,0},{2,3},{3,2},{4,5},{5,4},{6,7},{7,6},{8,9},{9,8},{10,11... | collective-permute-start | bytes 147464 | tf_op jit(solution)/shard_map/ppermute | solution.py:643
  59.2 1.2 %collective-permute-start.6 = (bf16[64,384]{1,0:T(8,128)(2,1)S(1)}, bf16[64,384]{1,0:T(8,128)(2,1)S(1)}, u32[]{:S(2)}, u32[]{:S(2)}) collective-permute-start(bf16[64,384]{1,0:T(8,128)(2,1)S(1)} %collective-permute-done.2.refs_3_), channel_id=1, source_target_pairs={{0,1},{1,0},{2,3},{3,2},{4,5},{5,4},{6,7},{7,6},{8,9},{9,8},{10,11... | collective-permute-start | bytes 147464 | tf_op jit(solution)/shard_map/ppermute | solution.py:643
  63.7 5.1 %collective-permute-start.7 = (bf16[64,384]{1,0:T(8,128)(2,1)S(1)}, bf16[64,384]{1,0:T(8,128)(2,1)S(1)}, u32[]{:S(2)}, u32[]{:S(2)}) collective-permute-start(bf16[64,384]{1,0:T(8,128)(2,1)S(1)} %get-tuple-element.44), channel_id=1, source_target_pairs={{0,6},{1,7},{2,0},{3,1},{4,2},{5,3},{6,4},{7,5},{8,14},{9,15},{10,... | collective-permute-start | bytes 147464 | tf_op jit(solution)/shard_map/ppermute | solution.py:632
  66.4 5.6 %collective-permute-start.8 = (bf16[64,384]{1,0:T(8,128)(2,1)S(1)}, bf16[64,384]{1,0:T(8,128)(2,1)S(1)}, u32[]{:S(2)}, u32[]{:S(2)}) collective-permute-start(bf16[64,384]{1,0:T(8,128)(2,1)S(1)} %get-tuple-element.45), channel_id=1, source_target_pairs={{0,4},{1,5},{2,6},{3,7},{4,0},{5,1},{6,2},{7,3},{8,12},{9,13},{10,... | collective-permute-start | bytes 147464 | tf_op jit(solution)/shard_map/ppermute | solution.py:632
  66.4 5.8 %collective-permute-start.9 = (bf16[64,384]{1,0:T(8,128)(2,1)S(1)}, bf16[64,384]{1,0:T(8,128)(2,1)S(1)}, u32[]{:S(2)}, u32[]{:S(2)}) collective-permute-start(bf16[64,384]{1,0:T(8,128)(2,1)S(1)} %get-tuple-element.46), channel_id=1, source_target_pairs={{0,2},{1,3},{2,4},{3,5},{4,6},{5,7},{6,0},{7,1},{8,10},{9,11},{10,... | collective-permute-start | bytes 147464 | tf_op jit(solution)/shard_map/ppermute | solution.py:632

commit v5 on v4

--- a/solution.py
+++ b/solution.py
@@ -116,12 +116,16 @@
     w_in_ref,
     bias_ref,
     w_out_ref,
+    node_w_in_ref,
+    node_bias_ref,
     tiles_ref,
     late_wanted_ref,
     pre0_ref,
     pre1_ref,
-    late_deliver_ref,
+    receivers_ref,
     own_rows_ref,
+    node_pre0_ref,
+    node_pre1_ref,
     sum0_ref,
     sum1_ref,
     pre0_hbm,
@@ -172,11 +176,14 @@
     remote_tiles = (jnp.sum(is_remote).astype(jnp.int32) + WIDE - 1) // WIDE
     used_tiles = (jnp.sum(1.0 - is_empty).astype(jnp.int32) + WIDE - 1) // WIDE
     late_tiles = jnp.maximum(remote_tiles, LATE_TILES)
-    tiles_ref[0] = late_tiles
-    tiles_ref[1] = place_ref[0]
+    slot = lax.broadcasted_iota(jnp.int32, tiles_ref.shape, 1)
+    tiles_ref[...] = jnp.where(slot == 0, late_tiles, place_ref[0])
     for fetch in fetches:
         fetch.wait()
     own_rows_ref[...] = dot_lanes(eye, own_ref[...]).astype(BF16)
+    own_pair = level_pair(own_rows_ref[...], node_w_in_ref[0:width, :])
+    node_pre0_ref[:, 0:width] = own_pair[0] + node_bias_ref[...]
+    node_pre1_ref[:, 0:width] = own_pair[1] + node_bias_ref[...]
     table_ref[width:, :] = jnp.zeros((table_ref.shape[0] - width, edge_count), BF16)
     for index in range(tile_count):
         lanes = slice(index * tile, (index + 1) * tile)
@@ -219,20 +226,26 @@
         recv0, recv1 = level_pair(recv_rows, w_recv)
         nodes = lax.broadcasted_iota(jnp.int32, (node_dev, WIDE), 0).astype(F32)
         deliver = jnp.where(nodes == receiver_row, 1.0, 0.0).astype(BF16)
-        return base + send0 + recv0, base + send1 + recv1, deliver, sender_column - node_dev
+        return (
+            base + send0 + recv0,
+            base + send1 + recv1,
+            deliver,
+            sender_column - node_dev,
+            receiver_row,
+        )
 
     @pl.loop(0, LATE_TILES)
     def _(index):
-        pre0, pre1, deliver, wanted = arrange(index)
+        pre0, pre1, _, wanted, receiver_row = arrange(index)
         rows = pl.ds(pl.multiple_of(index * WIDE, WIDE), WIDE)
-        pre0_ref[rows, :] = pre0
-        pre1_ref[rows, :] = pre1
-        late_deliver_ref[index] = deliver
+        pre0_ref[rows, 0:width] = pre0
+        pre1_ref[rows, 0:width] = pre1
+        receivers_ref[index] = jnp.broadcast_to(receiver_row, receivers_ref.shape[1:])
         late_wanted_ref[rows, :] = jnp.broadcast_to(wanted, (WIDE, 128))
 
     @pl.loop(LATE_TILES, late_tiles)
     def _(index):
-        rest0_ref[...], rest1_ref[...], rest3_ref[0], wanted = arrange(index)
+        rest0_ref[...], rest1_ref[...], rest3_ref[0], wanted, _ = arrange(index)
         rest2_ref[...] = jnp.broadcast_to(wanted, rest2_ref.shape)
         sends = [
             pltpu.make_async_copy(source, target.at[index - LATE_TILES], sent.at[slot])
@@ -252,19 +265,21 @@
 
     @pl.loop(late_tiles, jnp.maximum(used_tiles, late_tiles))
     def _(index):
-        pre0, pre1, deliver, _ = arrange(index)
+        pre0, pre1, deliver, _, _ = arrange(index)
         w_out = w_out_ref[...]
-        sum0_ref[...] += dot(deliver, dot(silu(pre0).astype(BF16), w_out).astype(BF16))
-        sum1_ref[...] += dot(deliver, dot(silu(pre1).astype(BF16), w_out).astype(BF16))
+        sum0_ref[:, 0:width] += dot(deliver, dot(silu(pre0).astype(BF16), w_out).astype(BF16))
+        sum1_ref[:, 0:width] += dot(deliver, dot(silu(pre1).astype(BF16), w_out).astype(BF16))
 
 
 def edge_kernel(
     tiles_ref,
     late_wanted_ref,
+    receivers_ref,
     late_pre0_hbm,
     late_pre1_hbm,
-    late_deliver_hbm,
     own_hbm,
+    node_pre0_hbm,
+    node_pre1_hbm,
     sum0_hbm,
     sum1_hbm,
     pre0_hbm,
@@ -274,7 +289,6 @@
     w_in_ref,
     w_out_ref,
     node_w_in_ref,
-    node_bias_ref,
     node_w_out_ref,
     node_gain_ref,
     attention_gain_ref,
@@ -285,9 +299,10 @@
     out2_ref,
     out3_ref,
     normed_ref,
-    pre0_ref,
-    pre1_ref,
-    late_deliver_ref,
+    late_pre0_ref,
+    late_pre1_ref,
+    node_pre0_ref,
+    node_pre1_ref,
     own_ref,
     total0_ref,
     total1_ref,
@@ -303,11 +318,12 @@
         pltpu.make_async_copy(source, target, early_arrived.at[slot])
         for slot, (source, target) in enumerate(
             (
-                (late_pre0_hbm, pre0_ref),
-                (late_pre1_hbm, pre1_ref),
-                (late_deliver_hbm, late_deliver_ref),
+                (late_pre0_hbm, late_pre0_ref),
+                (late_pre1_hbm, late_pre1_ref),
                 (sum0_hbm, total0_ref),
                 (sum1_hbm, total1_ref),
+                (node_pre0_hbm, node_pre0_ref),
+                (node_pre1_hbm, node_pre1_ref),
                 (own_hbm, own_ref),
             )
         )
@@ -332,16 +348,24 @@
 
     sent0, sent1 = gather(late_wanted_ref[...])
     early[0].wait()
-    message0 = messages(pre0_ref[...], sent0)
+    message0 = messages(late_pre0_ref[:, 0:width], sent0)
     early[1].wait()
-    message1 = messages(pre1_ref[...], sent1)
+    message1 = messages(late_pre1_ref[:, 0:width], sent1)
+    nodes = lax.broadcasted_iota(jnp.int32, (state_ref.shape[0], WIDE), 0).astype(F32)
+    deliver = jnp.concatenate(
+        [
+            jnp.where(nodes == receivers_ref[block][0:1, :], 1.0, 0.0).astype(BF16)
+            for block in range(LATE_TILES)
+        ],
+        axis=1,
+    )
+    arrived0, arrived1 = dot(deliver, message0), dot(deliver, message1)
     for fetch in early[2:]:
         fetch.wait()
-    deliver = jnp.concatenate([late_deliver_ref[i] for i in range(LATE_TILES)], axis=1)
-    total0_ref[...] += dot(deliver, message0)
-    total1_ref[...] += dot(deliver, message1)
-
-    @pl.loop(LATE_TILES, tiles_ref[0])
+    total0_ref[:, 0:width] += arrived0
+    total1_ref[:, 0:width] += arrived1
+
+    @pl.loop(LATE_TILES, tiles_ref[0, 0])
     def _(index):
         fetches = [
             pltpu.make_async_copy(source.at[index - LATE_TILES], target, arrived.at[slot])
@@ -359,19 +383,17 @@
         for fetch in fetches:
             fetch.wait()
         sent0, sent1 = gather(rest2_ref[...])
-        total0_ref[...] += dot(rest3_ref[0], messages(rest0_ref[...], sent0))
-        total1_ref[...] += dot(rest3_ref[0], messages(rest1_ref[...], sent1))
+        total0_ref[:, 0:width] += dot(rest3_ref[0], messages(rest0_ref[...], sent0))
+        total1_ref[:, 0:width] += dot(rest3_ref[0], messages(rest1_ref[...], sent1))
 
     own = own_ref[...]
-    own_pair = level_pair(own, node_w_in_ref[0:width, :])
+    own_pair = (node_pre0_ref[:, 0:width], node_pre1_ref[:, 0:width])
     own_values = (own[:, :width], own[:, width:])
     states = []
     normed = []
     for level, total_ref in enumerate((total0_ref, total1_ref)):
-        summed = total_ref[...].astype(BF16)
-        node_pre = (
-            own_pair[level] + dot(summed, node_w_in_ref[width : 2 * width, :]) + node_bias_ref[...]
-        )
+        summed = total_ref[:, 0:width].astype(BF16)
+        node_pre = own_pair[level] + dot(summed, node_w_in_ref[width : 2 * width, :])
         update = dot(silu(node_pre).astype(BF16), node_w_out_ref[...])
         state = (
             own_values[level].astype(F32) + node_gain_ref[...] * normalize(update)
@@ -383,8 +405,9 @@
     state_ref[...] = merge_levels(*states)
     normed_ref[...] = merge_levels(*normed)
     share = out0_ref.shape[0]
+    place = tiles_ref[0, 1]
     for shift, out_ref in enumerate((out0_ref, out1_ref, out2_ref, out3_ref)):
-        block = lax.rem(tiles_ref[1] + shift, CHIPS)
+        block = lax.rem(place + shift, CHIPS)
         out_ref[...] = normed_ref[pl.ds(pl.multiple_of(block * share, share), share), :]
 
 
@@ -413,26 +436,32 @@
 
     def rows_of(pair, part):
         items = slice(part * CHUNK, (part + 1) * CHUNK)
-        return jnp.concatenate([p[:, items, :].reshape(-1, width) for p in pair], axis=0)
+        return jnp.concatenate([p[:, items, :].reshape(-1, width) for p in pair], axis=0).astype(BF16)
 
     def per_head(rows):
         return jnp.concatenate(
-            [jnp.where(head_of == head, rows, 0.0).astype(BF16) for head in range(HEADS)], axis=0
+            [rows * jnp.where(head_of == head, 1.0, 0.0).astype(BF16) for head in range(HEADS)],
+            axis=0,
         )
 
     queries = project(CHIPS, query_ref)
     keys, values = project(block_count, key_ref), project(block_count, value_ref)
-    ones = per_head(jnp.ones((key_total, width), F32))
+    ones = per_head(jnp.ones((key_total, width), BF16))
+    all_powers, mixes = [], []
     for part in range(item_count // CHUNK):
         bias = jnp.where(same_node, bias_ref[part], -1e30)
-        scores = dot_lanes(rows_of(queries, part).astype(BF16), per_head(rows_of(keys, part)))
+        scores = dot_lanes(rows_of(queries, part), per_head(rows_of(keys, part)))
         powers = []
         for head in range(HEADS):
             own_scores = scores[:, head * key_total : (head + 1) * key_total] * scale + bias
             top = jnp.max(own_scores, axis=-1, keepdims=True)
             powers.append(jnp.exp(own_scores - top).astype(BF16))
         powers = jnp.concatenate(powers, axis=1)
-        attended = dot(powers, per_head(rows_of(values, part))) / dot(powers, ones)
+        all_powers.append(powers)
+        mixes.append(dot(powers, per_head(rows_of(values, part))))
+    sums = dot(jnp.concatenate(all_powers, axis=0), ones)
+    for part, mix in enumerate(mixes):
+        attended = mix / sums[part * query_total : (part + 1) * query_total]
         mix_ref[:, :, part * CHUNK : (part + 1) * CHUNK, :] = attended.reshape(
             2, CHIPS, CHUNK, width
         )
@@ -446,8 +475,9 @@
 ):
     width = weight_ref.shape[0]
     share = part0_ref.shape[0]
+    place = place_ref[0, 1]
     for shift, part_ref in enumerate((part0_ref, part1_ref, part2_ref, part3_ref)):
-        block = lax.rem(place_ref[1] + shift, CHIPS)
+        block = lax.rem(place + shift, CHIPS)
         attended_ref[pl.ds(pl.multiple_of(block * share, share), share), :] = part_ref[...]
     mixed = level_pair(attended_ref[...], weight_ref[...])
     state = state_ref[...].astype(F32)
@@ -564,17 +594,16 @@
         ((WIDE, 128), F32),
         ((1, node_dev, WIDE), BF16),
     ]
-    tiles, wanted, *tail = call(
+    tiles, wanted, pre0, pre1, late_receivers, *tail = call(
         local_kernel,
         (
-            shape((2,), jnp.int32),
+            pltpu.VMEM((8, 128), jnp.int32),
             pltpu.VMEM((late, 128), F32),
-            pltpu.HBM((late, width), F32),
-            pltpu.HBM((late, width), F32),
-            pltpu.HBM((LATE_TILES, node_dev, WIDE), BF16),
+            pltpu.HBM((late, WIDE), F32),
+            pltpu.HBM((late, WIDE), F32),
+            pltpu.VMEM((LATE_TILES, 8, WIDE), F32),
             pltpu.HBM((node_dev, merged), BF16),
-            pltpu.HBM((node_dev, width), F32),
-            pltpu.HBM((node_dev, width), F32),
+            *[pltpu.HBM((node_dev, WIDE), F32)] * 4,
             pltpu.HBM((rest, WIDE, width), F32),
             pltpu.HBM((rest, WIDE, width), F32),
             pltpu.HBM((rest, WIDE, 128), F32),
@@ -588,6 +617,8 @@
         edge_w_in,
         edge_bias[None, :],
         edge_w_out,
+        node_w_in,
+        node_bias[None, :],
         scratch=[
             pltpu.VMEM((merged, node_dev), BF16),
             pltpu.VMEM((tile_count, 128), F32),
@@ -596,36 +627,39 @@
             pltpu.SemaphoreType.DMA((4,)),
             pltpu.SemaphoreType.DMA((2,)),
         ],
-        in_specs=[IN_SMEM] + [IN_VMEM] * 2 + [ANYWHERE] * 2 + [IN_VMEM] * 3,
-        out_specs=[IN_SMEM] + [IN_VMEM] * 7 + [ANYWHERE] * 4,
+        in_specs=[IN_SMEM] + [IN_VMEM] * 2 + [ANYWHERE] * 2 + [IN_VMEM] * 5,
+        out_specs=[IN_VMEM] * 10 + [ANYWHERE] * 4,
     )
     state, *blocks = call(
         edge_kernel,
         (pltpu.VMEM((node_dev, merged), BF16), *[shape((share, merged))] * CHIPS),
-        tiles,
+        kept(tiles),
         kept(wanted),
+        kept(late_receivers),
+        in_hbm(pre0),
+        in_hbm(pre1),
         *(in_hbm(array) for array in tail),
         edge_w_in,
         edge_w_out,
         node_w_in,
-        node_bias[None, :],
         node_w_out,
         node_gain[None, :],
         attention_gain[None, :],
         incoming,
         scratch=[
             pltpu.VMEM((node_dev, merged), BF16),
-            pltpu.VMEM((late, width), F32),
-            pltpu.VMEM((late, width), F32),
-            pltpu.VMEM((LATE_TILES, node_dev, WIDE), BF16),
+            pltpu.VMEM((late, WIDE), F32),
+            pltpu.VMEM((late, WIDE), F32),
+            pltpu.VMEM((node_dev, WIDE), F32),
+            pltpu.VMEM((node_dev, WIDE), F32),
             pltpu.VMEM((node_dev, merged), BF16),
-            pltpu.VMEM((node_dev, width), F32),
-            pltpu.VMEM((node_dev, width), F32),
+            pltpu.VMEM((node_dev, WIDE), F32),
+            pltpu.VMEM((node_dev, WIDE), F32),
             *(pltpu.VMEM(*entry) for entry in rest_shapes),
-            pltpu.SemaphoreType.DMA((6,)),
+            pltpu.SemaphoreType.DMA((7,)),
             pltpu.SemaphoreType.DMA((4,)),
         ],
-        in_specs=[IN_SMEM, IN_VMEM] + [ANYWHERE] * 10 + [IN_VMEM] * 8,
+        in_specs=[IN_VMEM] * 3 + [ANYWHERE] * 11 + [IN_VMEM] * 7,
     )
 
     def to_chip(array, shift):
@@ -658,13 +692,12 @@
     out = call(
         output_kernel,
         shape((lev_dev, width, node_dev)),
-        tiles,
+        kept(tiles),
         kept(state),
         *returned,
         live,
         output_weight,
         scratch=[pltpu.VMEM((node_dev, merged), BF16)],
-        in_specs=[IN_SMEM] + [IN_VMEM] * 7,
     )
     return out.transpose(2, 0, 1)
 

time: 74.2 us -> 72.7 us (0.980)
  Pallas kernels: 28.7 us -> 22.4 us
  waiting for transfers between devices: 22.1 us -> 26.9 us
    pallas_call x5, Pallas kernels: 28.7 us -> 22.4 us  [call(): pl.pallas_call(kernel, out_shape=out_shape, **specs, scratch_shapes=list(...]
    all_to_all x1, waiting for transfers between devices: 14 us -> 18.8 us  [per_device(): lax.all_to_all(outgoing.reshape(patch_count, slot_count, merged), 'patch'...]
  transfers between devices with their start and end apart: 11 -> 11, of which waited for: 7 -> 7; matrix products, arithmetic and copies ran while one was open for 1% -> 1% of each run, Pallas kernels for 22% -> 15%
where the time goes in v5:
time: 72.7 us; the launch traced here: 72.4 us
  waiting for transfers between devices  26.9 us (37%)
  Pallas kernels  22.4 us (31%)
  starting transfers between devices  21.8 us (30%)
  local copies, waits for them, and re-layouts  0.82 us (1%)
    pallas_call x5, Pallas kernels, call(): pl.pallas_call(kernel, out_shape=out_shape, **specs, scratch_shapes=list(...  22.4 us
    all_to_all x1, waiting for transfers between devices, per_device(): lax.all_to_all(outgoing.reshape(patch_count, slot_count, merged), 'patch'...  18.8 us
    all_to_all x1, starting transfers between devices, per_device(): lax.all_to_all(outgoing.reshape(patch_count, slot_count, merged), 'patch'...  11.8 us
    ppermute x6, starting transfers between devices, to_chip(): lax.ppermute(array, 'lev', [(a * CORES + b, (a + shift) % CHIPS * CORES +...  9.41 us
    ppermute x6, waiting for transfers between devices, to_chip(): lax.ppermute(array, 'lev', [(a * CORES + b, (a + shift) % CHIPS * CORES +...  6.9 us
  transfers between devices with their start and end apart: 11, of which 7 were waited for; matrix products, arithmetic and copies ran while one was open for 1% of the time, Pallas kernels for 15%

profile of v5, /device:TPU:8, one launch (start us, length us, event | category | flops | bytes accessed | tf_op | source)
XLA Modules:
  0.0 72.4 jit_solution(12697122479832434891)
XLA Ops:
  0.0 2.3 %shard_map.182 = bf16[1536,384]{1,0:T(8,128)(2,1)} custom-call(s32[32,48]{1,0:T(8,128)} %halo_hbm.1, bf16[384,256]{1,0:T(8,128)(2,1)} %bitcast.29), custom_call_target="tpu_custom_call" | custom-call | tf_op jit(solution)/shard_map/pallas_call | solution.py:491
  2.3 0.0 copy-start.14
  2.3 0.0 copy-start.12
  2.4 0.0 copy-start.11
  2.4 0.0 copy-start.15
  2.4 0.0 copy-start.13
  2.4 0.0 copy-start
  2.4 0.0 copy-start.6
  2.4 0.0 copy-start.7
  2.4 0.0 copy-start.8
  2.4 11.8 %all-to-all-start = ((bf16[32,48,384]{2,1,0:T(8,128)(2,1)}), bf16[32,48,384]{2,1,0:T(8,128)(2,1)S(1)}, u32[]{:S(2)}, u32[]{:S(2)}) async-start(bf16[32,48,384]{2,1,0:T(8,128)(2,1)} %bitcast.11), calls=%async_computation | async-start | bytes 2359296 | tf_op jit(solution)/shard_map/all_to_all | solution.py:561
  14.3 0.1 dynamic_slice.3
  14.4 0.1 lt.75
  14.5 0.1 lt.71
  14.6 0.1 lt.72
  14.7 0.0 copy-start.1
  14.7 0.0 copy-start.9
  14.7 0.0 copy-start.10
  14.7 0.1 lt.77
  14.8 0.1 copy.25.node_w_in_ref
  15.0 0.2 copy.24.w_in_ref
  15.2 0.1 fusion.receiver_ref
  15.3 11.0 %shard_map.181 = (s32[8,128]{1,0:T(8,128)S(1)}, f32[768,128]{1,0:T(8,128)S(1)}, f32[768,256]{1,0:T(8,128)}, f32[768,256]{1,0:T(8,128)}, f32[3,8,256]{2,1,0:T(8,1...) custom-call(s32[1]{0:T(128)} %bitcast.place_ref, ...), custom_call_target="tpu_custom_call" | custom-call | tf_op jit(solution)/shard_map/pallas_call | solution.py:491
  26.3 18.8 %all-to-all-done = bf16[32,48,384]{2,1,0:T(8,128)(2,1)S(1)} async-done(((bf16[32,48,384]{2,1,0:T(8,128)(2,1)}), bf16[32,48,384]{2,1,0:T(8,128)(2,1)S(1)}, u32[]{:S(2)}, u32[]{:S(2)}) %all-to-all-start) | async-done | bytes 1179680 | tf_op jit(solution)/shard_map/all_to_all | solution.py:561
  45.2 0.0 copy-start.3
  45.2 0.0 copy-start.4
  45.2 0.0 copy-start.5
  45.2 0.0 copy-start.2
  45.2 4.7 %shard_map.183 = (bf16[256,384]{1,0:T(8,128)(2,1)S(1)}, bf16[64,384]{1,0:T(8,128)(2,1)S(1)}, bf16[64,384]{1,0:T(8,128)(2,1)S(1)}, bf16[64,384]{1,0:T(8,128)(2,1)S(1)}, bf16[64,384]{1,0:T(8,128)(2,1)S(1)}) custom-call(s32[8,128]{1,0:T(8,128)S(1)} %get-tuple-element.28.tiles_ref.place_ref, f32[768,128]{1,0:T(8,128)S(1)} %get-tuple-element.29.late_wanted_ref, ...), custom_call_target="tpu_custom_call" | custom-call | tf_op jit(solution)/shard_map/pallas_call | solution.py:491
  49.9 1.6 %collective-permute-start = (bf16[64,384]{1,0:T(8,128)(2,1)S(1)}, bf16[64,384]{1,0:T(8,128)(2,1)S(1)}, u32[]{:S(2)}, u32[]{:S(2)}) collective-permute-start(bf16[64,384]{1,0:T(8,128)(2,1)S(1)} %get-tuple-element.44), channel_id=1, source_target_pairs={{0,2},{1,3},{2,4},{3,5},{4,6},{5,7},{6,0},{7,1},{8,10},{9,11},{10,... | collective-permute-start | bytes 147464 | tf_op jit(solution)/shard_map/ppermute | solution.py:666
  51.5 2.7 %collective-permute-start.1 = (bf16[64,384]{1,0:T(8,128)(2,1)S(1)}, bf16[64,384]{1,0:T(8,128)(2,1)S(1)}, u32[]{:S(2)}, u32[]{:S(2)}) collective-permute-start(bf16[64,384]{1,0:T(8,128)(2,1)S(1)} %get-tuple-element.45), channel_id=1, source_target_pairs={{0,4},{1,5},{2,6},{3,7},{4,0},{5,1},{6,2},{7,3},{8,12},{9,13},{10,... | collective-permute-start | bytes 147464 | tf_op jit(solution)/shard_map/ppermute | solution.py:666
  54.2 1.4 %collective-permute-start.2 = (bf16[64,384]{1,0:T(8,128)(2,1)S(1)}, bf16[64,384]{1,0:T(8,128)(2,1)S(1)}, u32[]{:S(2)}, u32[]{:S(2)}) collective-permute-start(bf16[64,384]{1,0:T(8,128)(2,1)S(1)} %get-tuple-element.46), channel_id=1, source_target_pairs={{0,6},{1,7},{2,0},{3,1},{4,2},{5,3},{6,4},{7,5},{8,14},{9,15},{10,... | collective-permute-start | bytes 147464 | tf_op jit(solution)/shard_map/ppermute | solution.py:666
  55.7 0.0 collective-permute-start.3
  55.7 0.0 collective-permute-done.refs_1_
  55.7 0.5 collective-permute-start.4
  56.2 0.9 %collective-permute-done.1.refs_2_ = bf16[64,384]{1,0:T(8,128)(2,1)S(1)} collective-permute-done((bf16[64,384]{1,0:T(8,128)(2,1)S(1)}, bf16[64,384]{1,0:T(8,128)(2,1)S(1)}, u32[]{:S(2)}, u32[]{:S(2)}) %collective-permute-start.1) | collective-permute-done | bytes 49184 | tf_op jit(solution)/shard_map/ppermute | solution.py:666
  57.1 1.2 %collective-permute-done.2.refs_3_ = bf16[64,384]{1,0:T(8,128)(2,1)S(1)} collective-permute-done((bf16[64,384]{1,0:T(8,128)(2,1)S(1)}, bf16[64,384]{1,0:T(8,128)(2,1)S(1)}, u32[]{:S(2)}, u32[]{:S(2)}) %collective-permute-start.2) | collective-permute-done | bytes 49184 | tf_op jit(solution)/shard_map/ppermute | solution.py:666
  58.3 0.0 collective-permute-start.6
  58.3 0.0 collective-permute-done.3.refs_4_
  58.3 1.2 %collective-permute-done.6.refs_7_ = bf16[64,384]{1,0:T(8,128)(2,1)S(1)} collective-permute-done((bf16[64,384]{1,0:T(8,128)(2,1)S(1)}, bf16[64,384]{1,0:T(8,128)(2,1)S(1)}, u32[]{:S(2)}, u32[]{:S(2)}) %collective-permute-start.6) | collective-permute-done | bytes 49184 | tf_op jit(solution)/shard_map/ppermute | solution.py:677
  59.5 3.1 %shard_map.184 = (bf16[64,384]{1,0:T(8,128)(2,1)S(1)}, bf16[64,384]{1,0:T(8,128)(2,1)S(1)}, bf16[64,384]{1,0:T(8,128)(2,1)S(1)}, bf16[64,384]{1,0:T(8,128)(2,1)S(1)}) custom-call(bf16[64,384]{1,0:T(8,128)(2,1)S(1)} %get-tuple-element.43.refs_0_, bf16[64,384]{1,0:T(8,128)(2,1)S(1)} %collective-permute-done.refs_1_, ...), custom_call_target="tpu_custom_call" | custom-call | tf_op jit(solution)/shard_map/pallas_call | solution.py:491
  62.6 2.7 %collective-permute-start.7 = (bf16[64,384]{1,0:T(8,128)(2,1)S(1)}, bf16[64,384]{1,0:T(8,128)(2,1)S(1)}, u32[]{:S(2)}, u32[]{:S(2)}) collective-permute-start(bf16[64,384]{1,0:T(8,128)(2,1)S(1)} %get-tuple-element.48), channel_id=1, source_target_pairs={{0,6},{1,7},{2,0},{3,1},{4,2},{5,3},{6,4},{7,5},{8,14},{9,15},{10,... | collective-permute-start | bytes 147464 | tf_op jit(solution)/shard_map/ppermute | solution.py:666
  65.3 1.0 %collective-permute-start.9 = (bf16[64,384]{1,0:T(8,128)(2,1)S(1)}, bf16[64,384]{1,0:T(8,128)(2,1)S(1)}, u32[]{:S(2)}, u32[]{:S(2)}) collective-permute-start(bf16[64,384]{1,0:T(8,128)(2,1)S(1)} %get-tuple-element.50), channel_id=1, source_target_pairs={{0,2},{1,3},{2,4},{3,5},{4,6},{5,7},{6,0},{7,1},{8,10},{9,11},{10,... | collective-permute-start | bytes 147464 | tf_op jit(solution)/shard_map/ppermute | solution.py:666
  66.3 0.1 compare_convert_fusion.live_ref
  66.4 1.3 %collective-permute-done.7.part1_ref = bf16[64,384]{1,0:T(8,128)(2,1)S(1)} collective-permute-done((bf16[64,384]{1,0:T(8,128)(2,1)S(1)}, bf16[64,384]{1,0:T(8,128)(2,1)S(1)}, u32[]{:S(2)}, u32[]{:S(2)}) %collective-permute-start.7) | collective-permute-done | bytes 49184 | tf_op jit(solution)/shard_map/ppermute | solution.py:666
  67.7 3.2 %collective-permute-done.8.part2_ref = bf16[64,384]{1,0:T(8,128)(2,1)S(1)} collective-permute-done((bf16[64,384]{1,0:T(8,128)(2,1)S(1)}, bf16[64,384]{1,0:T(8,128)(2,1)S(1)}, u32[]{:S(2)}, u32[]{:S(2)}) %collective-permute-start.8) | collective-permute-done | bytes 49184 | tf_op jit(solution)/shard_map/ppermute | solution.py:666
  71.0 0.2 collective-permute-done.9.part3_ref
  71.2 1.3 %shard_map.185 = bf16[2,192,256]{2,1,0:T(8,128)(2,1)} custom-call(s32[8,128]{1,0:T(8,128)S(1)} %get-tuple-element.28.tiles_ref.place_ref, bf16[256,384]{1,0:T(8,128)(2,1)S(1)} %get-tuple-element.42.state_ref, bf16[64,384]{1,0:T(8,128)(2,1)S(1)} %get-tuple-element.47.part0_ref, bf16[64,384]{1,0:T(8,128)(2,1)S(1)} %collective-permute-done.7.part1_ref, ...), custom_call_target="tpu_custom_call" | custom-call | tf_op jit(solution)/shard_map/pallas_call | solution.py:491
  (26 shorter events, 0.1 us)
Async XLA Ops:
  2.3 12.0 %copy-start.14 = (s32[256]{0:T(256)S(1)}, s32[256]{0:T(256)}, u32[]{:S(2)}) copy-start(s32[256]{0:T(256)} %param.25) | copy-start | bytes 3076
  2.3 12.5 %copy-start.12 = (bf16[384,192]{0,1:T(8,128)(2,1)S(1)}, bf16[384,192]{0,1:T(8,128)(2,1)}, u32[]{:S(2)}) copy-start(bf16[384,192]{0,1:T(8,128)(2,1)} %param.29) | copy-start | bytes 442372
  2.4 12.6 %copy-start.11 = (bf16[576,192]{0,1:T(8,128)(2,1)S(1)}, bf16[576,192]{0,1:T(8,128)(2,1)}, u32[]{:S(2)}) copy-start(bf16[576,192]{0,1:T(8,128)(2,1)} %param.26) | copy-start | bytes 663556
  2.4 12.8 %copy-start.15 = (s32[16]{0:T(128)S(1)}, s32[16]{0:T(128)}, u32[]{:S(2)}) copy-start(s32[16]{0:T(128)} %param.23) | copy-start | bytes 196
  2.4 12.8 %copy-start.13 = (s32[2048]{0:T(1024)S(1)}, s32[2048]{0:T(1024)}, u32[]{:S(2)}) copy-start(s32[2048]{0:T(1024)} %param.22) | copy-start | bytes 24580
  2.4 12.9 %copy-start = (bf16[192,192]{1,0:T(8,128)(2,1)S(1)}, bf16[192,192]{1,0:T(8,128)(2,1)}, u32[]{:S(2)}) copy-start(bf16[192,192]{1,0:T(8,128)(2,1)} %w_out_ref.3) | copy-start | bytes 221188
  2.4 12.9 %copy-start.6 = (s32[2048]{0:T(1024)S(1)}, s32[2048]{0:T(1024)}, u32[]{:S(2)}) copy-start(s32[2048]{0:T(1024)} %param.21) | copy-start | bytes 24580
  2.4 12.8 %copy-start.7 = (f32[192]{0:T(256)S(1)}, f32[192]{0:T(256)}, u32[]{:S(2)}) copy-start(f32[192]{0:T(256)} %param.27) | copy-start | bytes 2308
  2.4 12.8 %copy-start.8 = (f32[192]{0:T(256)S(1)}, f32[192]{0:T(256)}, u32[]{:S(2)}) copy-start(f32[192]{0:T(256)} %param.30) | copy-start | bytes 2308
  2.4 42.7 %all-to-all-start = ((bf16[32,48,384]{2,1,0:T(8,128)(2,1)}), bf16[32,48,384]{2,1,0:T(8,128)(2,1)S(1)}, u32[]{:S(2)}, u32[]{:S(2)}) async-start(bf16[32,48,384]{2,1,0:T(8,128)(2,1)} %bitcast.11), calls=%async_computation | async-start | bytes 2359296 | tf_op jit(solution)/shard_map/all_to_all | solution.py:561
  14.7 30.5 %copy-start.1 = (bf16[192,192]{1,0:T(8,128)(2,1)S(1)}, bf16[192,192]{1,0:T(8,128)(2,1)}, u32[]{:S(2)}) copy-start(bf16[192,192]{1,0:T(8,128)(2,1)} %node_w_out_ref.1) | copy-start | bytes 221188
  14.7 30.5 %copy-start.9 = (f32[192]{0:T(256)S(1)}, f32[192]{0:T(256)}, u32[]{:S(2)}) copy-start(f32[192]{0:T(256)} %param.32) | copy-start | bytes 2308
  14.7 30.5 %copy-start.10 = (f32[192]{0:T(256)S(1)}, f32[192]{0:T(256)}, u32[]{:S(2)}) copy-start(f32[192]{0:T(256)} %param.33) | copy-start | bytes 2308
  45.2 14.4 %copy-start.3 = (bf16[192,192]{1,0:T(8,128)(2,1)S(1)}, bf16[192,192]{1,0:T(8,128)(2,1)}, u32[]{:S(2)}) copy-start(bf16[192,192]{1,0:T(8,128)(2,1)} %refs_9_.1) | copy-start | bytes 221188
  45.2 14.3 %copy-start.4 = (bf16[192,192]{1,0:T(8,128)(2,1)S(1)}, bf16[192,192]{1,0:T(8,128)(2,1)}, u32[]{:S(2)}) copy-start(bf16[192,192]{1,0:T(8,128)(2,1)} %refs_10_.1) | copy-start | bytes 221188
  45.2 14.3 %copy-start.5 = (bf16[192,192]{1,0:T(8,128)(2,1)S(1)}, bf16[192,192]{1,0:T(8,128)(2,1)}, u32[]{:S(2)}) copy-start(bf16[192,192]{1,0:T(8,128)(2,1)} %refs_11_.1) | copy-start | bytes 221188
  45.2 25.9 %copy-start.2 = (bf16[192,192]{1,0:T(8,128)(2,1)S(1)}, bf16[192,192]{1,0:T(8,128)(2,1)}, u32[]{:S(2)}) copy-start(bf16[192,192]{1,0:T(8,128)(2,1)} %weight_ref.1) | copy-start | bytes 221188
  49.9 5.8 %collective-permute-start = (bf16[64,384]{1,0:T(8,128)(2,1)S(1)}, bf16[64,384]{1,0:T(8,128)(2,1)S(1)}, u32[]{:S(2)}, u32[]{:S(2)}) collective-permute-start(bf16[64,384]{1,0:T(8,128)(2,1)S(1)} %get-tuple-element.44), channel_id=1, source_target_pairs={{0,2},{1,3},{2,4},{3,5},{4,6},{5,7},{6,0},{7,1},{8,10},{9,11},{10,... | collective-permute-start | bytes 147464 | tf_op jit(solution)/shard_map/ppermute | solution.py:666
  51.5 5.6 %collective-permute-start.1 = (bf16[64,384]{1,0:T(8,128)(2,1)S(1)}, bf16[64,384]{1,0:T(8,128)(2,1)S(1)}, u32[]{:S(2)}, u32[]{:S(2)}) collective-permute-start(bf16[64,384]{1,0:T(8,128)(2,1)S(1)} %get-tuple-element.45), channel_id=1, source_target_pairs={{0,4},{1,5},{2,6},{3,7},{4,0},{5,1},{6,2},{7,3},{8,12},{9,13},{10,... | collective-permute-start | bytes 147464 | tf_op jit(solution)/shard_map/ppermute | solution.py:666
  54.2 4.1 %collective-permute-start.2 = (bf16[64,384]{1,0:T(8,128)(2,1)S(1)}, bf16[64,384]{1,0:T(8,128)(2,1)S(1)}, u32[]{:S(2)}, u32[]{:S(2)}) collective-permute-start(bf16[64,384]{1,0:T(8,128)(2,1)S(1)} %get-tuple-element.46), channel_id=1, source_target_pairs={{0,6},{1,7},{2,0},{3,1},{4,2},{5,3},{6,4},{7,5},{8,14},{9,15},{10,... | collective-permute-start | bytes 147464 | tf_op jit(solution)/shard_map/ppermute | solution.py:666
  55.7 2.7 %collective-permute-start.3 = (bf16[64,384]{1,0:T(8,128)(2,1)S(1)}, bf16[64,384]{1,0:T(8,128)(2,1)S(1)}, u32[]{:S(2)}, u32[]{:S(2)}) collective-permute-start(bf16[64,384]{1,0:T(8,128)(2,1)S(1)} %get-tuple-element.43.refs_0_), channel_id=1, source_target_pairs={{0,1},{1,0},{2,3},{3,2},{4,5},{5,4},{6,7},{7,6},{8,9},{9,8},{10,11... | collective-permute-start | bytes 147464 | tf_op jit(solution)/shard_map/ppermute | solution.py:677
  55.7 2.6 %collective-permute-start.4 = (bf16[64,384]{1,0:T(8,128)(2,1)S(1)}, bf16[64,384]{1,0:T(8,128)(2,1)S(1)}, u32[]{:S(2)}, u32[]{:S(2)}) collective-permute-start(bf16[64,384]{1,0:T(8,128)(2,1)S(1)} %collective-permute-done.refs_1_), channel_id=1, source_target_pairs={{0,1},{1,0},{2,3},{3,2},{4,5},{5,4},{6,7},{7,6},{8,9},{9,8},{10,11... | collective-permute-start | bytes 147464 | tf_op jit(solution)/shard_map/ppermute | solution.py:677
  57.1 1.3 %collective-permute-start.5 = (bf16[64,384]{1,0:T(8,128)(2,1)S(1)}, bf16[64,384]{1,0:T(8,128)(2,1)S(1)}, u32[]{:S(2)}, u32[]{:S(2)}) collective-permute-start(bf16[64,384]{1,0:T(8,128)(2,1)S(1)} %collective-permute-done.1.refs_2_), channel_id=1, source_target_pairs={{0,1},{1,0},{2,3},{3,2},{4,5},{5,4},{6,7},{7,6},{8,9},{9,8},{10,11... | collective-permute-start | bytes 147464 | tf_op jit(solution)/shard_map/ppermute | solution.py:677
  58.3 1.2 %collective-permute-start.6 = (bf16[64,384]{1,0:T(8,128)(2,1)S(1)}, bf16[64,384]{1,0:T(8,128)(2,1)S(1)}, u32[]{:S(2)}, u32[]{:S(2)}) collective-permute-start(bf16[64,384]{1,0:T(8,128)(2,1)S(1)} %collective-permute-done.2.refs_3_), channel_id=1, source_target_pairs={{0,1},{1,0},{2,3},{3,2},{4,5},{5,4},{6,7},{7,6},{8,9},{9,8},{10,11... | collective-permute-start | bytes 147464 | tf_op jit(solution)/shard_map/ppermute | solution.py:677
  62.6 5.1 %collective-permute-start.7 = (bf16[64,384]{1,0:T(8,128)(2,1)S(1)}, bf16[64,384]{1,0:T(8,128)(2,1)S(1)}, u32[]{:S(2)}, u32[]{:S(2)}) collective-permute-start(bf16[64,384]{1,0:T(8,128)(2,1)S(1)} %get-tuple-element.48), channel_id=1, source_target_pairs={{0,6},{1,7},{2,0},{3,1},{4,2},{5,3},{6,4},{7,5},{8,14},{9,15},{10,... | collective-permute-start | bytes 147464 | tf_op jit(solution)/shard_map/ppermute | solution.py:666
  65.3 5.6 %collective-permute-start.8 = (bf16[64,384]{1,0:T(8,128)(2,1)S(1)}, bf16[64,384]{1,0:T(8,128)(2,1)S(1)}, u32[]{:S(2)}, u32[]{:S(2)}) collective-permute-start(bf16[64,384]{1,0:T(8,128)(2,1)S(1)} %get-tuple-element.49), channel_id=1, source_target_pairs={{0,4},{1,5},{2,6},{3,7},{4,0},{5,1},{6,2},{7,3},{8,12},{9,13},{10,... | collective-permute-start | bytes 147464 | tf_op jit(solution)/shard_map/ppermute | solution.py:666
  65.3 5.8 %collective-permute-start.9 = (bf16[64,384]{1,0:T(8,128)(2,1)S(1)}, bf16[64,384]{1,0:T(8,128)(2,1)S(1)}, u32[]{:S(2)}, u32[]{:S(2)}) collective-permute-start(bf16[64,384]{1,0:T(8,128)(2,1)S(1)} %get-tuple-element.50), channel_id=1, source_target_pairs={{0,2},{1,3},{2,4},{3,5},{4,6},{5,7},{6,0},{7,1},{8,10},{9,11},{10,... | collective-permute-start | bytes 147464 | tf_op jit(solution)/shard_map/ppermute | solution.py:666

commit v6 on v5

--- a/solution.py
+++ b/solution.py
@@ -30,10 +30,14 @@
     return v / (1.0 + jnp.exp(-v))
 
 
-def normalize(values):
-    centered = values - jnp.mean(values, axis=-1, keepdims=True)
-    spread = jnp.mean(centered * centered, axis=-1, keepdims=True)
-    return centered * lax.rsqrt(spread + 1e-05)
+def normalize_all(arrays):
+    means = [jnp.mean(values, axis=-1, keepdims=True) for values in arrays]
+    centered = [values - mean for values, mean in zip(arrays, means, strict=True)]
+    spreads = [jnp.mean(values * values, axis=-1, keepdims=True) for values in centered]
+    return [
+        values * lax.rsqrt(spread + 1e-05)
+        for values, spread in zip(centered, spreads, strict=True)
+    ]
 
 
 def onehot(column, width):
@@ -389,19 +393,19 @@
     own = own_ref[...]
     own_pair = (node_pre0_ref[:, 0:width], node_pre1_ref[:, 0:width])
     own_values = (own[:, :width], own[:, width:])
-    states = []
-    normed = []
-    for level, total_ref in enumerate((total0_ref, total1_ref)):
-        summed = total_ref[:, 0:width].astype(BF16)
-        node_pre = own_pair[level] + dot(summed, node_w_in_ref[width : 2 * width, :])
-        update = dot(silu(node_pre).astype(BF16), node_w_out_ref[...])
-        state = (
-            own_values[level].astype(F32) + node_gain_ref[...] * normalize(update)
-        ).astype(BF16)
-        states.append(state)
-        normed.append(
-            (attention_gain_ref[...] * normalize(state.astype(F32))).astype(BF16)
-        )
+    levels = range(2)
+    summed = [total0_ref[:, 0:width].astype(BF16), total1_ref[:, 0:width].astype(BF16)]
+    w_summed = node_w_in_ref[width : 2 * width, :]
+    node_pre = [own_pair[level] + dot(summed[level], w_summed) for level in levels]
+    hidden = [silu(node_pre[level]).astype(BF16) for level in levels]
+    update = [dot(hidden[level], node_w_out_ref[...]) for level in levels]
+    update = normalize_all(update)
+    states = [
+        (own_values[level].astype(F32) + node_gain_ref[...] * update[level]).astype(BF16)
+        for level in levels
+    ]
+    normed = normalize_all([state.astype(F32) for state in states])
+    normed = [(attention_gain_ref[...] * rows).astype(BF16) for rows in normed]
     state_ref[...] = merge_levels(*states)
     normed_ref[...] = merge_levels(*normed)
     share = out0_ref.shape[0]
@@ -422,46 +426,50 @@
     key_total = 2 * block_count * CHUNK
     query_total = 2 * CHIPS * CHUNK
     head_of = lax.broadcasted_iota(jnp.int32, (1, width), 1) // head_width
+    in_head = [jnp.where(head_of == head, 1.0, 0.0) for head in range(HEADS)]
     same_node = (
-        lax.broadcasted_iota(jnp.int32, (query_total, key_total), 0) % CHUNK
-        == lax.broadcasted_iota(jnp.int32, (query_total, key_total), 1) % CHUNK
+        lax.broadcasted_iota(jnp.int32, (HEADS * query_total, key_total), 0) % CHUNK
+        == lax.broadcasted_iota(jnp.int32, (HEADS * query_total, key_total), 1) % CHUNK
     )
     blocks = jnp.concatenate([ref[...] for ref in block_refs], axis=0)
 
-    def project(count, weight_ref):
+    def project(count, weight):
         return [
-            p.reshape(count, item_count, width)
-            for p in level_pair(blocks[: count * item_count], weight_ref[...])
+            p.reshape(count, item_count, weight.shape[1])
+            for p in level_pair(blocks[: count * item_count], weight)
         ]
 
     def rows_of(pair, part):
         items = slice(part * CHUNK, (part + 1) * CHUNK)
-        return jnp.concatenate([p[:, items, :].reshape(-1, width) for p in pair], axis=0).astype(BF16)
-
-    def per_head(rows):
         return jnp.concatenate(
-            [rows * jnp.where(head_of == head, 1.0, 0.0).astype(BF16) for head in range(HEADS)],
-            axis=0,
-        )
-
-    queries = project(CHIPS, query_ref)
-    keys, values = project(block_count, key_ref), project(block_count, value_ref)
-    ones = per_head(jnp.ones((key_total, width), BF16))
-    all_powers, mixes = [], []
-    for part in range(item_count // CHUNK):
-        bias = jnp.where(same_node, bias_ref[part], -1e30)
-        scores = dot_lanes(rows_of(queries, part), per_head(rows_of(keys, part)))
-        powers = []
-        for head in range(HEADS):
-            own_scores = scores[:, head * key_total : (head + 1) * key_total] * scale + bias
-            top = jnp.max(own_scores, axis=-1, keepdims=True)
-            powers.append(jnp.exp(own_scores - top).astype(BF16))
-        powers = jnp.concatenate(powers, axis=1)
-        all_powers.append(powers)
-        mixes.append(dot(powers, per_head(rows_of(values, part))))
-    sums = dot(jnp.concatenate(all_powers, axis=0), ones)
+            [p[:, items, :].reshape(-1, p.shape[2]) for p in pair], axis=0
+        ).astype(BF16)
+
+    queries = project(CHIPS, query_ref[...])
+    keys = project(block_count, key_ref[...])
+    wide_value = jnp.concatenate(
+        [value_ref[...], jnp.zeros((width, WIDE - width), BF16)], axis=1
+    )
+    lanes = lax.broadcasted_iota(jnp.int32, (1, 1, WIDE), 2)
+    values = [p + jnp.where(lanes < width, 0.0, 1.0) for p in project(block_count, wide_value)]
+    parts = range(item_count // CHUNK)
+    headed = [rows_of(queries, part) for part in parts]
+    headed = [
+        jnp.concatenate([rows * mask.astype(BF16) for mask in in_head], axis=0) for rows in headed
+    ]
+    scores = [dot_lanes(headed[part], rows_of(keys, part)) for part in parts]
+    scores = [
+        scores[part] * scale + jnp.where(same_node, bias_ref[part], -1e30) for part in parts
+    ]
+    tops = [jnp.max(part_scores, axis=-1, keepdims=True) for part_scores in scores]
+    powers = [jnp.exp(scores[part] - tops[part]).astype(BF16) for part in parts]
+    mixes = [dot(powers[part], rows_of(values, part)) for part in parts]
     for part, mix in enumerate(mixes):
-        attended = mix / sums[part * query_total : (part + 1) * query_total]
+        mix = mix[:, :width] * (1.0 / mix[:, width : width + 1])
+        attended = sum(
+            mix[head * query_total : (head + 1) * query_total] * mask
+            for head, mask in enumerate(in_head)
+        )
         mix_ref[:, :, part * CHUNK : (part + 1) * CHUNK, :] = attended.reshape(
             2, CHIPS, CHUNK, width
         )

time: 72.7 us -> 71 us (0.977)
  Pallas kernels: 22.4 us -> 20.6 us
    pallas_call x5, Pallas kernels: 22.4 us -> 20.6 us  [call(): pl.pallas_call(kernel, out_shape=out_shape, **specs, scratch_shapes=list(...]
  transfers between devices with their start and end apart: 11 -> 11, of which waited for: 7 -> 7; matrix products, arithmetic and copies ran while one was open for 1% -> 1% of each run, Pallas kernels for 15% -> 16%
where the time goes in v6:
time: 71 us; the launch traced here: 70.7 us
  waiting for transfers between devices  26.9 us (38%)
  starting transfers between devices  21.8 us (31%)
  Pallas kernels  20.6 us (29%)
  local copies, waits for them, and re-layouts  0.82 us (1%)
    pallas_call x5, Pallas kernels, call(): pl.pallas_call(kernel, out_shape=out_shape, **specs, scratch_shapes=list(...  20.6 us
    all_to_all x1, waiting for transfers between devices, per_device(): lax.all_to_all(outgoing.reshape(patch_count, slot_count, merged), 'patch'...  18.8 us
    all_to_all x1, starting transfers between devices, per_device(): lax.all_to_all(outgoing.reshape(patch_count, slot_count, merged), 'patch'...  11.8 us
    ppermute x6, starting transfers between devices, to_chip(): lax.ppermute(array, 'lev', [(a * CORES + b, (a + shift) % CHIPS * CORES +...  9.42 us
    ppermute x6, waiting for transfers between devices, to_chip(): lax.ppermute(array, 'lev', [(a * CORES + b, (a + shift) % CHIPS * CORES +...  6.9 us
  transfers between devices with their start and end apart: 11, of which 7 were waited for; matrix products, arithmetic and copies ran while one was open for 1% of the time, Pallas kernels for 16%

profile of v6, /device:TPU:8, one launch (start us, length us, event | category | flops | bytes accessed | tf_op | source)
XLA Modules:
  0.0 70.7 jit_solution(16312528938387393608)
XLA Ops:
  0.0 2.3 %shard_map.182 = bf16[1536,384]{1,0:T(8,128)(2,1)} custom-call(s32[32,48]{1,0:T(8,128)} %halo_hbm.1, bf16[384,256]{1,0:T(8,128)(2,1)} %bitcast.29), custom_call_target="tpu_custom_call" | custom-call | tf_op jit(solution)/shard_map/pallas_call | solution.py:499
  2.3 0.0 copy-start.14
  2.3 0.0 copy-start.12
  2.4 0.0 copy-start.11
  2.4 0.0 copy-start.15
  2.4 0.0 copy-start.13
  2.4 0.0 copy-start
  2.4 0.0 copy-start.6
  2.4 0.0 copy-start.7
  2.4 0.0 copy-start.8
  2.4 11.8 %all-to-all-start = ((bf16[32,48,384]{2,1,0:T(8,128)(2,1)}), bf16[32,48,384]{2,1,0:T(8,128)(2,1)S(1)}, u32[]{:S(2)}, u32[]{:S(2)}) async-start(bf16[32,48,384]{2,1,0:T(8,128)(2,1)} %bitcast.11), calls=%async_computation | async-start | bytes 2359296 | tf_op jit(solution)/shard_map/all_to_all | solution.py:569
  14.3 0.1 dynamic_slice.3
  14.4 0.1 lt.75
  14.5 0.1 lt.71
  14.6 0.1 lt.72
  14.7 0.0 copy-start.1
  14.7 0.0 copy-start.9
  14.7 0.0 copy-start.10
  14.7 0.1 lt.77
  14.8 0.1 copy.25.node_w_in_ref
  15.0 0.2 copy.24.w_in_ref
  15.2 0.1 fusion.receiver_ref
  15.3 11.0 %shard_map.181 = (s32[8,128]{1,0:T(8,128)S(1)}, f32[768,128]{1,0:T(8,128)S(1)}, f32[768,256]{1,0:T(8,128)}, f32[768,256]{1,0:T(8,128)}, f32[3,8,256]{2,1,0:T(8,1...) custom-call(s32[1]{0:T(128)} %bitcast.place_ref, ...), custom_call_target="tpu_custom_call" | custom-call | tf_op jit(solution)/shard_map/pallas_call | solution.py:499
  26.3 18.8 %all-to-all-done = bf16[32,48,384]{2,1,0:T(8,128)(2,1)S(1)} async-done(((bf16[32,48,384]{2,1,0:T(8,128)(2,1)}), bf16[32,48,384]{2,1,0:T(8,128)(2,1)S(1)}, u32[]{:S(2)}, u32[]{:S(2)}) %all-to-all-start) | async-done | bytes 1179680 | tf_op jit(solution)/shard_map/all_to_all | solution.py:569
  45.2 0.0 copy-start.3
  45.2 0.0 copy-start.4
  45.2 0.0 copy-start.5
  45.2 0.0 copy-start.2
  45.2 4.7 %shard_map.183 = (bf16[256,384]{1,0:T(8,128)(2,1)S(1)}, bf16[64,384]{1,0:T(8,128)(2,1)S(1)}, bf16[64,384]{1,0:T(8,128)(2,1)S(1)}, bf16[64,384]{1,0:T(8,128)(2,1)S(1)}, bf16[64,384]{1,0:T(8,128)(2,1)S(1)}) custom-call(s32[8,128]{1,0:T(8,128)S(1)} %get-tuple-element.28.tiles_ref.place_ref, f32[768,128]{1,0:T(8,128)S(1)} %get-tuple-element.29.late_wanted_ref, ...), custom_call_target="tpu_custom_call" | custom-call | tf_op jit(solution)/shard_map/pallas_call | solution.py:499
  49.9 1.6 %collective-permute-start = (bf16[64,384]{1,0:T(8,128)(2,1)S(1)}, bf16[64,384]{1,0:T(8,128)(2,1)S(1)}, u32[]{:S(2)}, u32[]{:S(2)}) collective-permute-start(bf16[64,384]{1,0:T(8,128)(2,1)S(1)} %get-tuple-element.44), channel_id=1, source_target_pairs={{0,2},{1,3},{2,4},{3,5},{4,6},{5,7},{6,0},{7,1},{8,10},{9,11},{10,... | collective-permute-start | bytes 147464 | tf_op jit(solution)/shard_map/ppermute | solution.py:674
  51.5 2.7 %collective-permute-start.1 = (bf16[64,384]{1,0:T(8,128)(2,1)S(1)}, bf16[64,384]{1,0:T(8,128)(2,1)S(1)}, u32[]{:S(2)}, u32[]{:S(2)}) collective-permute-start(bf16[64,384]{1,0:T(8,128)(2,1)S(1)} %get-tuple-element.45), channel_id=1, source_target_pairs={{0,4},{1,5},{2,6},{3,7},{4,0},{5,1},{6,2},{7,3},{8,12},{9,13},{10,... | collective-permute-start | bytes 147464 | tf_op jit(solution)/shard_map/ppermute | solution.py:674
  54.2 1.4 %collective-permute-start.2 = (bf16[64,384]{1,0:T(8,128)(2,1)S(1)}, bf16[64,384]{1,0:T(8,128)(2,1)S(1)}, u32[]{:S(2)}, u32[]{:S(2)}) collective-permute-start(bf16[64,384]{1,0:T(8,128)(2,1)S(1)} %get-tuple-element.46), channel_id=1, source_target_pairs={{0,6},{1,7},{2,0},{3,1},{4,2},{5,3},{6,4},{7,5},{8,14},{9,15},{10,... | collective-permute-start | bytes 147464 | tf_op jit(solution)/shard_map/ppermute | solution.py:674
  55.7 0.0 collective-permute-start.3
  55.7 0.0 collective-permute-done.refs_1_
  55.7 0.5 collective-permute-start.4
  56.2 0.9 %collective-permute-done.1.refs_2_ = bf16[64,384]{1,0:T(8,128)(2,1)S(1)} collective-permute-done((bf16[64,384]{1,0:T(8,128)(2,1)S(1)}, bf16[64,384]{1,0:T(8,128)(2,1)S(1)}, u32[]{:S(2)}, u32[]{:S(2)}) %collective-permute-start.1) | collective-permute-done | bytes 49184 | tf_op jit(solution)/shard_map/ppermute | solution.py:674
  57.1 1.2 %collective-permute-done.2.refs_3_ = bf16[64,384]{1,0:T(8,128)(2,1)S(1)} collective-permute-done((bf16[64,384]{1,0:T(8,128)(2,1)S(1)}, bf16[64,384]{1,0:T(8,128)(2,1)S(1)}, u32[]{:S(2)}, u32[]{:S(2)}) %collective-permute-start.2) | collective-permute-done | bytes 49184 | tf_op jit(solution)/shard_map/ppermute | solution.py:674
  58.3 0.0 collective-permute-start.6
  58.3 0.0 collective-permute-done.3.refs_4_
  58.4 1.2 %collective-permute-done.6.refs_7_ = bf16[64,384]{1,0:T(8,128)(2,1)S(1)} collective-permute-done((bf16[64,384]{1,0:T(8,128)(2,1)S(1)}, bf16[64,384]{1,0:T(8,128)(2,1)S(1)}, u32[]{:S(2)}, u32[]{:S(2)}) %collective-permute-start.6) | collective-permute-done | bytes 49184 | tf_op jit(solution)/shard_map/ppermute | solution.py:685
  59.6 1.3 %shard_map.184 = (bf16[64,384]{1,0:T(8,128)(2,1)S(1)}, bf16[64,384]{1,0:T(8,128)(2,1)S(1)}, bf16[64,384]{1,0:T(8,128)(2,1)S(1)}, bf16[64,384]{1,0:T(8,128)(2,1)S(1)}) custom-call(bf16[64,384]{1,0:T(8,128)(2,1)S(1)} %get-tuple-element.43.refs_0_, bf16[64,384]{1,0:T(8,128)(2,1)S(1)} %collective-permute-done.refs_1_, ...), custom_call_target="tpu_custom_call" | custom-call | tf_op jit(solution)/shard_map/pallas_call | solution.py:499
  60.9 2.7 %collective-permute-start.7 = (bf16[64,384]{1,0:T(8,128)(2,1)S(1)}, bf16[64,384]{1,0:T(8,128)(2,1)S(1)}, u32[]{:S(2)}, u32[]{:S(2)}) collective-permute-start(bf16[64,384]{1,0:T(8,128)(2,1)S(1)} %get-tuple-element.48), channel_id=1, source_target_pairs={{0,6},{1,7},{2,0},{3,1},{4,2},{5,3},{6,4},{7,5},{8,14},{9,15},{10,... | collective-permute-start | bytes 147464 | tf_op jit(solution)/shard_map/ppermute | solution.py:674
  63.6 1.0 %collective-permute-start.9 = (bf16[64,384]{1,0:T(8,128)(2,1)S(1)}, bf16[64,384]{1,0:T(8,128)(2,1)S(1)}, u32[]{:S(2)}, u32[]{:S(2)}) collective-permute-start(bf16[64,384]{1,0:T(8,128)(2,1)S(1)} %get-tuple-element.50), channel_id=1, source_target_pairs={{0,2},{1,3},{2,4},{3,5},{4,6},{5,7},{6,0},{7,1},{8,10},{9,11},{10,... | collective-permute-start | bytes 147464 | tf_op jit(solution)/shard_map/ppermute | solution.py:674
  64.6 0.1 compare_convert_fusion.live_ref
  64.7 1.3 %collective-permute-done.7.part1_ref = bf16[64,384]{1,0:T(8,128)(2,1)S(1)} collective-permute-done((bf16[64,384]{1,0:T(8,128)(2,1)S(1)}, bf16[64,384]{1,0:T(8,128)(2,1)S(1)}, u32[]{:S(2)}, u32[]{:S(2)}) %collective-permute-start.7) | collective-permute-done | bytes 49184 | tf_op jit(solution)/shard_map/ppermute | solution.py:674
  66.0 3.2 %collective-permute-done.8.part2_ref = bf16[64,384]{1,0:T(8,128)(2,1)S(1)} collective-permute-done((bf16[64,384]{1,0:T(8,128)(2,1)S(1)}, bf16[64,384]{1,0:T(8,128)(2,1)S(1)}, u32[]{:S(2)}, u32[]{:S(2)}) %collective-permute-start.8) | collective-permute-done | bytes 49184 | tf_op jit(solution)/shard_map/ppermute | solution.py:674
  69.3 0.2 collective-permute-done.9.part3_ref
  69.5 1.3 %shard_map.185 = bf16[2,192,256]{2,1,0:T(8,128)(2,1)} custom-call(s32[8,128]{1,0:T(8,128)S(1)} %get-tuple-element.28.tiles_ref.place_ref, bf16[256,384]{1,0:T(8,128)(2,1)S(1)} %get-tuple-element.42.state_ref, bf16[64,384]{1,0:T(8,128)(2,1)S(1)} %get-tuple-element.47.part0_ref, bf16[64,384]{1,0:T(8,128)(2,1)S(1)} %collective-permute-done.7.part1_ref, ...), custom_call_target="tpu_custom_call" | custom-call | tf_op jit(solution)/shard_map/pallas_call | solution.py:499
  (26 shorter events, 0.1 us)
Async XLA Ops:
  2.3 12.0 %copy-start.14 = (s32[256]{0:T(256)S(1)}, s32[256]{0:T(256)}, u32[]{:S(2)}) copy-start(s32[256]{0:T(256)} %param.25) | copy-start | bytes 3076
  2.3 12.5 %copy-start.12 = (bf16[384,192]{0,1:T(8,128)(2,1)S(1)}, bf16[384,192]{0,1:T(8,128)(2,1)}, u32[]{:S(2)}) copy-start(bf16[384,192]{0,1:T(8,128)(2,1)} %param.29) | copy-start | bytes 442372
  2.4 12.6 %copy-start.11 = (bf16[576,192]{0,1:T(8,128)(2,1)S(1)}, bf16[576,192]{0,1:T(8,128)(2,1)}, u32[]{:S(2)}) copy-start(bf16[576,192]{0,1:T(8,128)(2,1)} %param.26) | copy-start | bytes 663556
  2.4 12.8 %copy-start.15 = (s32[16]{0:T(128)S(1)}, s32[16]{0:T(128)}, u32[]{:S(2)}) copy-start(s32[16]{0:T(128)} %param.23) | copy-start | bytes 196
  2.4 12.8 %copy-start.13 = (s32[2048]{0:T(1024)S(1)}, s32[2048]{0:T(1024)}, u32[]{:S(2)}) copy-start(s32[2048]{0:T(1024)} %param.22) | copy-start | bytes 24580
  2.4 12.9 %copy-start = (bf16[192,192]{1,0:T(8,128)(2,1)S(1)}, bf16[192,192]{1,0:T(8,128)(2,1)}, u32[]{:S(2)}) copy-start(bf16[192,192]{1,0:T(8,128)(2,1)} %w_out_ref.3) | copy-start | bytes 221188
  2.4 12.9 %copy-start.6 = (s32[2048]{0:T(1024)S(1)}, s32[2048]{0:T(1024)}, u32[]{:S(2)}) copy-start(s32[2048]{0:T(1024)} %param.21) | copy-start | bytes 24580
  2.4 12.8 %copy-start.7 = (f32[192]{0:T(256)S(1)}, f32[192]{0:T(256)}, u32[]{:S(2)}) copy-start(f32[192]{0:T(256)} %param.27) | copy-start | bytes 2308
  2.4 12.8 %copy-start.8 = (f32[192]{0:T(256)S(1)}, f32[192]{0:T(256)}, u32[]{:S(2)}) copy-start(f32[192]{0:T(256)} %param.30) | copy-start | bytes 2308
  2.4 42.7 %all-to-all-start = ((bf16[32,48,384]{2,1,0:T(8,128)(2,1)}), bf16[32,48,384]{2,1,0:T(8,128)(2,1)S(1)}, u32[]{:S(2)}, u32[]{:S(2)}) async-start(bf16[32,48,384]{2,1,0:T(8,128)(2,1)} %bitcast.11), calls=%async_computation | async-start | bytes 2359296 | tf_op jit(solution)/shard_map/all_to_all | solution.py:569
  14.7 30.5 %copy-start.1 = (bf16[192,192]{1,0:T(8,128)(2,1)S(1)}, bf16[192,192]{1,0:T(8,128)(2,1)}, u32[]{:S(2)}) copy-start(bf16[192,192]{1,0:T(8,128)(2,1)} %node_w_out_ref.1) | copy-start | bytes 221188
  14.7 30.5 %copy-start.9 = (f32[192]{0:T(256)S(1)}, f32[192]{0:T(256)}, u32[]{:S(2)}) copy-start(f32[192]{0:T(256)} %param.32) | copy-start | bytes 2308
  14.7 30.5 %copy-start.10 = (f32[192]{0:T(256)S(1)}, f32[192]{0:T(256)}, u32[]{:S(2)}) copy-start(f32[192]{0:T(256)} %param.33) | copy-start | bytes 2308
  45.2 14.4 %copy-start.3 = (bf16[192,192]{1,0:T(8,128)(2,1)S(1)}, bf16[192,192]{1,0:T(8,128)(2,1)}, u32[]{:S(2)}) copy-start(bf16[192,192]{1,0:T(8,128)(2,1)} %refs_9_.1) | copy-start | bytes 221188
  45.2 14.4 %copy-start.4 = (bf16[192,192]{1,0:T(8,128)(2,1)S(1)}, bf16[192,192]{1,0:T(8,128)(2,1)}, u32[]{:S(2)}) copy-start(bf16[192,192]{1,0:T(8,128)(2,1)} %refs_10_.1) | copy-start | bytes 221188
  45.2 14.4 %copy-start.5 = (bf16[192,192]{1,0:T(8,128)(2,1)S(1)}, bf16[192,192]{1,0:T(8,128)(2,1)}, u32[]{:S(2)}) copy-start(bf16[192,192]{1,0:T(8,128)(2,1)} %refs_11_.1) | copy-start | bytes 221188
  45.2 24.2 %copy-start.2 = (bf16[192,192]{1,0:T(8,128)(2,1)S(1)}, bf16[192,192]{1,0:T(8,128)(2,1)}, u32[]{:S(2)}) copy-start(bf16[192,192]{1,0:T(8,128)(2,1)} %weight_ref.1) | copy-start | bytes 221188
  49.9 5.8 %collective-permute-start = (bf16[64,384]{1,0:T(8,128)(2,1)S(1)}, bf16[64,384]{1,0:T(8,128)(2,1)S(1)}, u32[]{:S(2)}, u32[]{:S(2)}) collective-permute-start(bf16[64,384]{1,0:T(8,128)(2,1)S(1)} %get-tuple-element.44), channel_id=1, source_target_pairs={{0,2},{1,3},{2,4},{3,5},{4,6},{5,7},{6,0},{7,1},{8,10},{9,11},{10,... | collective-permute-start | bytes 147464 | tf_op jit(solution)/shard_map/ppermute | solution.py:674
  51.5 5.6 %collective-permute-start.1 = (bf16[64,384]{1,0:T(8,128)(2,1)S(1)}, bf16[64,384]{1,0:T(8,128)(2,1)S(1)}, u32[]{:S(2)}, u32[]{:S(2)}) collective-permute-start(bf16[64,384]{1,0:T(8,128)(2,1)S(1)} %get-tuple-element.45), channel_id=1, source_target_pairs={{0,4},{1,5},{2,6},{3,7},{4,0},{5,1},{6,2},{7,3},{8,12},{9,13},{10,... | collective-permute-start | bytes 147464 | tf_op jit(solution)/shard_map/ppermute | solution.py:674
  54.2 4.1 %collective-permute-start.2 = (bf16[64,384]{1,0:T(8,128)(2,1)S(1)}, bf16[64,384]{1,0:T(8,128)(2,1)S(1)}, u32[]{:S(2)}, u32[]{:S(2)}) collective-permute-start(bf16[64,384]{1,0:T(8,128)(2,1)S(1)} %get-tuple-element.46), channel_id=1, source_target_pairs={{0,6},{1,7},{2,0},{3,1},{4,2},{5,3},{6,4},{7,5},{8,14},{9,15},{10,... | collective-permute-start | bytes 147464 | tf_op jit(solution)/shard_map/ppermute | solution.py:674
  55.7 2.7 %collective-permute-start.3 = (bf16[64,384]{1,0:T(8,128)(2,1)S(1)}, bf16[64,384]{1,0:T(8,128)(2,1)S(1)}, u32[]{:S(2)}, u32[]{:S(2)}) collective-permute-start(bf16[64,384]{1,0:T(8,128)(2,1)S(1)} %get-tuple-element.43.refs_0_), channel_id=1, source_target_pairs={{0,1},{1,0},{2,3},{3,2},{4,5},{5,4},{6,7},{7,6},{8,9},{9,8},{10,11... | collective-permute-start | bytes 147464 | tf_op jit(solution)/shard_map/ppermute | solution.py:685
  55.7 2.6 %collective-permute-start.4 = (bf16[64,384]{1,0:T(8,128)(2,1)S(1)}, bf16[64,384]{1,0:T(8,128)(2,1)S(1)}, u32[]{:S(2)}, u32[]{:S(2)}) collective-permute-start(bf16[64,384]{1,0:T(8,128)(2,1)S(1)} %collective-permute-done.refs_1_), channel_id=1, source_target_pairs={{0,1},{1,0},{2,3},{3,2},{4,5},{5,4},{6,7},{7,6},{8,9},{9,8},{10,11... | collective-permute-start | bytes 147464 | tf_op jit(solution)/shard_map/ppermute | solution.py:685
  57.1 1.3 %collective-permute-start.5 = (bf16[64,384]{1,0:T(8,128)(2,1)S(1)}, bf16[64,384]{1,0:T(8,128)(2,1)S(1)}, u32[]{:S(2)}, u32[]{:S(2)}) collective-permute-start(bf16[64,384]{1,0:T(8,128)(2,1)S(1)} %collective-permute-done.1.refs_2_), channel_id=1, source_target_pairs={{0,1},{1,0},{2,3},{3,2},{4,5},{5,4},{6,7},{7,6},{8,9},{9,8},{10,11... | collective-permute-start | bytes 147464 | tf_op jit(solution)/shard_map/ppermute | solution.py:685
  58.3 1.2 %collective-permute-start.6 = (bf16[64,384]{1,0:T(8,128)(2,1)S(1)}, bf16[64,384]{1,0:T(8,128)(2,1)S(1)}, u32[]{:S(2)}, u32[]{:S(2)}) collective-permute-start(bf16[64,384]{1,0:T(8,128)(2,1)S(1)} %collective-permute-done.2.refs_3_), channel_id=1, source_target_pairs={{0,1},{1,0},{2,3},{3,2},{4,5},{5,4},{6,7},{7,6},{8,9},{9,8},{10,11... | collective-permute-start | bytes 147464 | tf_op jit(solution)/shard_map/ppermute | solution.py:685
  60.9 5.1 %collective-permute-start.7 = (bf16[64,384]{1,0:T(8,128)(2,1)S(1)}, bf16[64,384]{1,0:T(8,128)(2,1)S(1)}, u32[]{:S(2)}, u32[]{:S(2)}) collective-permute-start(bf16[64,384]{1,0:T(8,128)(2,1)S(1)} %get-tuple-element.48), channel_id=1, source_target_pairs={{0,6},{1,7},{2,0},{3,1},{4,2},{5,3},{6,4},{7,5},{8,14},{9,15},{10,... | collective-permute-start | bytes 147464 | tf_op jit(solution)/shard_map/ppermute | solution.py:674
  63.6 5.6 %collective-permute-start.8 = (bf16[64,384]{1,0:T(8,128)(2,1)S(1)}, bf16[64,384]{1,0:T(8,128)(2,1)S(1)}, u32[]{:S(2)}, u32[]{:S(2)}) collective-permute-start(bf16[64,384]{1,0:T(8,128)(2,1)S(1)} %get-tuple-element.49), channel_id=1, source_target_pairs={{0,4},{1,5},{2,6},{3,7},{4,0},{5,1},{6,2},{7,3},{8,12},{9,13},{10,... | collective-permute-start | bytes 147464 | tf_op jit(solution)/shard_map/ppermute | solution.py:674
  63.6 5.8 %collective-permute-start.9 = (bf16[64,384]{1,0:T(8,128)(2,1)S(1)}, bf16[64,384]{1,0:T(8,128)(2,1)S(1)}, u32[]{:S(2)}, u32[]{:S(2)}) collective-permute-start(bf16[64,384]{1,0:T(8,128)(2,1)S(1)} %get-tuple-element.50), channel_id=1, source_target_pairs={{0,2},{1,3},{2,4},{3,5},{4,6},{5,7},{6,0},{7,1},{8,10},{9,11},{10,... | collective-permute-start | bytes 147464 | tf_op jit(solution)/shard_map/ppermute | solution.py:674

commit v7 on v6

--- a/solution.py
+++ b/solution.py
@@ -27,7 +27,8 @@
 
 
 def silu(v):
-    return v / (1.0 + jnp.exp(-v))
+    half = 0.5 * v
+    return half + half * jnp.tanh(half)
 
 
 def normalize_all(arrays):
@@ -55,6 +56,21 @@
     return (
         dot(merged[:, : half + half - cut], first),
         dot(merged[:, cut:], second),
+    )
+
+
+def put_pair(ref, rows, first, second):
+    width = first.shape[1]
+    ref[rows, 0:width] = first
+    ref[rows, WIDE:] = second[:, : 2 * width - WIDE]
+    ref[rows, width:WIDE] = second[:, 2 * width - WIDE :]
+
+
+def get_pair(ref):
+    width = ref.shape[1] // 2
+    return (
+        ref[:, 0:width],
+        jnp.concatenate([ref[:, WIDE:], ref[:, width:WIDE]], axis=1),
     )
 
 
@@ -120,23 +136,19 @@
     w_in_ref,
     bias_ref,
     w_out_ref,
-    node_w_in_ref,
-    node_bias_ref,
     tiles_ref,
     late_wanted_ref,
-    pre0_ref,
-    pre1_ref,
+    late_pre_ref,
     receivers_ref,
     own_rows_ref,
-    node_pre0_ref,
-    node_pre1_ref,
-    sum0_ref,
-    sum1_ref,
+    sums_ref,
     pre0_hbm,
     pre1_hbm,
     wanted_hbm,
     deliver_hbm,
     own_ref,
+    sum0_ref,
+    sum1_ref,
     position_ref,
     table_ref,
     rest0_ref,
@@ -185,9 +197,6 @@
     for fetch in fetches:
         fetch.wait()
     own_rows_ref[...] = dot_lanes(eye, own_ref[...]).astype(BF16)
-    own_pair = level_pair(own_rows_ref[...], node_w_in_ref[0:width, :])
-    node_pre0_ref[:, 0:width] = own_pair[0] + node_bias_ref[...]
-    node_pre1_ref[:, 0:width] = own_pair[1] + node_bias_ref[...]
     table_ref[width:, :] = jnp.zeros((table_ref.shape[0] - width, edge_count), BF16)
     for index in range(tile_count):
         lanes = slice(index * tile, (index + 1) * tile)
@@ -242,8 +251,7 @@
     def _(index):
         pre0, pre1, _, wanted, receiver_row = arrange(index)
         rows = pl.ds(pl.multiple_of(index * WIDE, WIDE), WIDE)
-        pre0_ref[rows, 0:width] = pre0
-        pre1_ref[rows, 0:width] = pre1
+        put_pair(late_pre_ref, rows, pre0, pre1)
         receivers_ref[index] = jnp.broadcast_to(receiver_row, receivers_ref.shape[1:])
         late_wanted_ref[rows, :] = jnp.broadcast_to(wanted, (WIDE, 128))
 
@@ -271,21 +279,19 @@
     def _(index):
         pre0, pre1, deliver, _, _ = arrange(index)
         w_out = w_out_ref[...]
-        sum0_ref[:, 0:width] += dot(deliver, dot(silu(pre0).astype(BF16), w_out).astype(BF16))
-        sum1_ref[:, 0:width] += dot(deliver, dot(silu(pre1).astype(BF16), w_out).astype(BF16))
+        sum0_ref[...] += dot(deliver, dot(silu(pre0).astype(BF16), w_out).astype(BF16))
+        sum1_ref[...] += dot(deliver, dot(silu(pre1).astype(BF16), w_out).astype(BF16))
+
+    put_pair(sums_ref, slice(None), sum0_ref[...], sum1_ref[...])
 
 
 def edge_kernel(
     tiles_ref,
     late_wanted_ref,
     receivers_ref,
-    late_pre0_hbm,
-    late_pre1_hbm,
+    late_pre_hbm,
     own_hbm,
-    node_pre0_hbm,
-    node_pre1_hbm,
-    sum0_hbm,
-    sum1_hbm,
+    sums_hbm,
     pre0_hbm,
     pre1_hbm,
     wanted_hbm,
@@ -293,6 +299,7 @@
     w_in_ref,
     w_out_ref,
     node_w_in_ref,
+    node_bias_ref,
     node_w_out_ref,
     node_gain_ref,
     attention_gain_ref,
@@ -303,10 +310,8 @@
     out2_ref,
     out3_ref,
     normed_ref,
-    late_pre0_ref,
-    late_pre1_ref,
-    node_pre0_ref,
-    node_pre1_ref,
+    late_pre_ref,
+    sums_ref,
     own_ref,
     total0_ref,
     total1_ref,
@@ -322,12 +327,8 @@
         pltpu.make_async_copy(source, target, early_arrived.at[slot])
         for slot, (source, target) in enumerate(
             (
-                (late_pre0_hbm, late_pre0_ref),
-                (late_pre1_hbm, late_pre1_ref),
-                (sum0_hbm, total0_ref),
-                (sum1_hbm, total1_ref),
-                (node_pre0_hbm, node_pre0_ref),
-                (node_pre1_hbm, node_pre1_ref),
+                (late_pre_hbm, late_pre_ref),
+                (sums_hbm, sums_ref),
                 (own_hbm, own_ref),
             )
         )
@@ -352,9 +353,9 @@
 
     sent0, sent1 = gather(late_wanted_ref[...])
     early[0].wait()
-    message0 = messages(late_pre0_ref[:, 0:width], sent0)
-    early[1].wait()
-    message1 = messages(late_pre1_ref[:, 0:width], sent1)
+    late_pre0, late_pre1 = get_pair(late_pre_ref)
+    message0 = messages(late_pre0, sent0)
+    message1 = messages(late_pre1, sent1)
     nodes = lax.broadcasted_iota(jnp.int32, (state_ref.shape[0], WIDE), 0).astype(F32)
     deliver = jnp.concatenate(
         [
@@ -364,10 +365,11 @@
         axis=1,
     )
     arrived0, arrived1 = dot(deliver, message0), dot(deliver, message1)
-    for fetch in early[2:]:
+    for fetch in early[1:]:
         fetch.wait()
-    total0_ref[:, 0:width] += arrived0
-    total1_ref[:, 0:width] += arrived1
+    sum0, sum1 = get_pair(sums_ref)
+    total0_ref[...] = sum0 + arrived0
+    total1_ref[...] = sum1 + arrived1
 
     @pl.loop(LATE_TILES, tiles_ref[0, 0])
     def _(index):
@@ -387,14 +389,16 @@
         for fetch in fetches:
             fetch.wait()
         sent0, sent1 = gather(rest2_ref[...])
-        total0_ref[:, 0:width] += dot(rest3_ref[0], messages(rest0_ref[...], sent0))
-        total1_ref[:, 0:width] += dot(rest3_ref[0], messages(rest1_ref[...], sent1))
+        total0_ref[...] += dot(rest3_ref[0], messages(rest0_ref[...], sent0))
+        total1_ref[...] += dot(rest3_ref[0], messages(rest1_ref[...], sent1))
 
     own = own_ref[...]
-    own_pair = (node_pre0_ref[:, 0:width], node_pre1_ref[:, 0:width])
+    own_pair = [
+        rows + node_bias_ref[...] for rows in level_pair(own, node_w_in_ref[0:width, :])
+    ]
     own_values = (own[:, :width], own[:, width:])
     levels = range(2)
-    summed = [total0_ref[:, 0:width].astype(BF16), total1_ref[:, 0:width].astype(BF16)]
+    summed = [total0_ref[...].astype(BF16), total1_ref[...].astype(BF16)]
     w_summed = node_w_in_ref[width : 2 * width, :]
     node_pre = [own_pair[level] + dot(summed[level], w_summed) for level in levels]
     hidden = [silu(node_pre[level]).astype(BF16) for level in levels]
@@ -478,8 +482,8 @@
 
 
 def output_kernel(
-    place_ref, state_ref, part0_ref, part1_ref, part2_ref, part3_ref, live_ref, weight_ref, out_ref,
-    attended_ref,
+    place_ref, state_ref, part0_ref, part1_ref, part2_ref, part3_ref, live_ref, weight_ref, out_hbm,
+    attended_ref, out_ref, sent,
 ):
     width = weight_ref.shape[0]
     share = part0_ref.shape[0]
@@ -489,10 +493,15 @@
         attended_ref[pl.ds(pl.multiple_of(block * share, share), share), :] = part_ref[...]
     mixed = level_pair(attended_ref[...], weight_ref[...])
     state = state_ref[...].astype(F32)
+    sends = []
     for level in range(2):
         live_part = mixed[level] * live_ref[:, level : level + 1]
         result = state[:, level * width : (level + 1) * width] + live_part
         out_ref[level] = result.T.astype(BF16)
+        sends.append(pltpu.make_async_copy(out_ref.at[level], out_hbm.at[level], sent.at[level]))
+        sends[-1].start()
+    for send in sends:
+        send.wait()
 
 
 def call(kernel, out_shape, *operands, scratch=(), **specs):
@@ -602,16 +611,15 @@
         ((WIDE, 128), F32),
         ((1, node_dev, WIDE), BF16),
     ]
-    tiles, wanted, pre0, pre1, late_receivers, *tail = call(
+    tiles, wanted, late_pre, late_receivers, *tail = call(
         local_kernel,
         (
             pltpu.VMEM((8, 128), jnp.int32),
             pltpu.VMEM((late, 128), F32),
-            pltpu.HBM((late, WIDE), F32),
-            pltpu.HBM((late, WIDE), F32),
+            pltpu.HBM((late, merged), F32),
             pltpu.VMEM((LATE_TILES, 8, WIDE), F32),
             pltpu.HBM((node_dev, merged), BF16),
-            *[pltpu.HBM((node_dev, WIDE), F32)] * 4,
+            pltpu.HBM((node_dev, merged), F32),
             pltpu.HBM((rest, WIDE, width), F32),
             pltpu.HBM((rest, WIDE, width), F32),
             pltpu.HBM((rest, WIDE, 128), F32),
@@ -625,18 +633,18 @@
         edge_w_in,
         edge_bias[None, :],
         edge_w_out,
-        node_w_in,
-        node_bias[None, :],
         scratch=[
             pltpu.VMEM((merged, node_dev), BF16),
+            pltpu.VMEM((node_dev, width), F32),
+            pltpu.VMEM((node_dev, width), F32),
             pltpu.VMEM((tile_count, 128), F32),
             pltpu.VMEM((width + 16, edge_count), BF16),
             *(pltpu.VMEM(*entry) for entry in rest_shapes),
             pltpu.SemaphoreType.DMA((4,)),
             pltpu.SemaphoreType.DMA((2,)),
         ],
-        in_specs=[IN_SMEM] + [IN_VMEM] * 2 + [ANYWHERE] * 2 + [IN_VMEM] * 5,
-        out_specs=[IN_VMEM] * 10 + [ANYWHERE] * 4,
+        in_specs=[IN_SMEM] + [IN_VMEM] * 2 + [ANYWHERE] * 2 + [IN_VMEM] * 3,
+        out_specs=[IN_VMEM] * 6 + [ANYWHERE] * 4,
     )
     state, *blocks = call(
         edge_kernel,
@@ -644,30 +652,28 @@
         kept(tiles),
         kept(wanted),
         kept(late_receivers),
-        in_hbm(pre0),
-        in_hbm(pre1),
+        in_hbm(late_pre),
         *(in_hbm(array) for array in tail),
         edge_w_in,
         edge_w_out,
         node_w_in,
+        node_bias[None, :],
         node_w_out,
         node_gain[None, :],
         attention_gain[None, :],
         incoming,
         scratch=[
             pltpu.VMEM((node_dev, merged), BF16),
-            pltpu.VMEM((late, WIDE), F32),
-            pltpu.VMEM((late, WIDE), F32),
-            pltpu.VMEM((node_dev, WIDE), F32),
-            pltpu.VMEM((node_dev, WIDE), F32),
+            pltpu.VMEM((late, merged), F32),
+            pltpu.VMEM((node_dev, merged), F32),
             pltpu.VMEM((node_dev, merged), BF16),
-            pltpu.VMEM((node_dev, WIDE), F32),
-            pltpu.VMEM((node_dev, WIDE), F32),
+            pltpu.VMEM((node_dev, width), F32),
+            pltpu.VMEM((node_dev, width), F32),
             *(pltpu.VMEM(*entry) for entry in rest_shapes),
-            pltpu.SemaphoreType.DMA((7,)),
+            pltpu.SemaphoreType.DMA((3,)),
             pltpu.SemaphoreType.DMA((4,)),
         ],
-        in_specs=[IN_VMEM] * 3 + [ANYWHERE] * 11 + [IN_VMEM] * 7,
+        in_specs=[IN_VMEM] * 3 + [ANYWHERE] * 7 + [IN_VMEM] * 8,
     )
 
     def to_chip(array, shift):
@@ -705,7 +711,12 @@
         *returned,
         live,
         output_weight,
-        scratch=[pltpu.VMEM((node_dev, merged), BF16)],
+        scratch=[
+            pltpu.VMEM((node_dev, merged), BF16),
+            pltpu.VMEM((lev_dev, width, node_dev), BF16),
+            pltpu.SemaphoreType.DMA((lev_dev,)),
+        ],
+        out_specs=ANYWHERE,
     )
     return out.transpose(2, 0, 1)
 

time: 71 us -> 71.1 us (level)
  waiting for transfers between devices: 26.9 us -> 28.9 us
  Pallas kernels: 20.6 us -> 18.7 us
    pallas_call x5, Pallas kernels: 20.6 us -> 18.7 us  [call(): pl.pallas_call(kernel, out_shape=out_shape, **specs, scratch_shapes=list(...]
    all_to_all x1, waiting for transfers between devices: 18.8 us -> 20.8 us  [per_device(): lax.all_to_all(outgoing.reshape(patch_count, slot_count, merged), 'patch'...]
  transfers between devices with their start and end apart: 11 -> 11, of which waited for: 7 -> 7; matrix products, arithmetic and copies ran while one was open for 1% -> 1% of each run, Pallas kernels for 16% -> 13%
where the time goes in v7:
time: 71.1 us; the launch traced here: 70.8 us
  waiting for transfers between devices  28.9 us (41%)
  starting transfers between devices  21.8 us (31%)
  Pallas kernels  18.7 us (26%)
  local copies, waits for them, and re-layouts  0.82 us (1%)
    all_to_all x1, waiting for transfers between devices, per_device(): lax.all_to_all(outgoing.reshape(patch_count, slot_count, merged), 'patch'...  20.8 us
    pallas_call x5, Pallas kernels, call(): pl.pallas_call(kernel, out_shape=out_shape, **specs, scratch_shapes=list(...  18.7 us
    all_to_all x1, starting transfers between devices, per_device(): lax.all_to_all(outgoing.reshape(patch_count, slot_count, merged), 'patch'...  11.8 us
    ppermute x6, starting transfers between devices, to_chip(): lax.ppermute(array, 'lev', [(a * CORES + b, (a + shift) % CHIPS * CORES +...  9.42 us
    ppermute x6, waiting for transfers between devices, to_chip(): lax.ppermute(array, 'lev', [(a * CORES + b, (a + shift) % CHIPS * CORES +...  6.9 us
  transfers between devices with their start and end apart: 11, of which 7 were waited for; matrix products, arithmetic and copies ran while one was open for 1% of the time, Pallas kernels for 13%

profile of v7, /device:TPU:8, one launch (start us, length us, event | category | flops | bytes accessed | tf_op | source)
XLA Modules:
  0.0 70.8 jit_solution(6354624738589184725)
XLA Ops:
  0.0 2.3 %shard_map.182 = bf16[1536,384]{1,0:T(8,128)(2,1)} custom-call(s32[32,48]{1,0:T(8,128)} %halo_hbm.1, bf16[384,256]{1,0:T(8,128)(2,1)} %bitcast.29), custom_call_target="tpu_custom_call" | custom-call | tf_op jit(solution)/shard_map/pallas_call | solution.py:508
  2.3 0.0 copy-start.14
  2.3 0.0 copy-start.12
  2.4 0.0 copy-start.11
  2.4 0.0 copy-start.15
  2.4 0.0 copy-start.13
  2.4 0.0 copy-start
  2.4 0.0 copy-start.6
  2.4 0.0 copy-start.10
  2.4 11.8 %all-to-all-start = ((bf16[32,48,384]{2,1,0:T(8,128)(2,1)}), bf16[32,48,384]{2,1,0:T(8,128)(2,1)S(1)}, u32[]{:S(2)}, u32[]{:S(2)}) async-start(bf16[32,48,384]{2,1,0:T(8,128)(2,1)} %bitcast.11), calls=%async_computation | async-start | bytes 2359296 | tf_op jit(solution)/shard_map/all_to_all | solution.py:578
  14.3 0.1 dynamic_slice.3
  14.4 0.1 lt.75
  14.5 0.1 lt.71
  14.6 0.1 lt.72
  14.7 0.1 lt.77
  14.8 0.0 copy-start.1
  14.8 0.0 copy-start.7
  14.8 0.0 copy-start.8
  14.8 0.0 copy-start.9
  14.8 0.1 copy.25.node_w_in_ref
  15.0 0.2 copy.23.w_in_ref
  15.2 0.1 fusion.receiver_ref
  15.3 9.1 %shard_map.181 = (s32[8,128]{1,0:T(8,128)S(1)}, f32[768,128]{1,0:T(8,128)S(1)}, f32[768,384]{1,0:T(8,128)}, f32[3,8,256]{2,1,0:T(8,128)S(1)}, bf16[256,384]{1,0:...) custom-call(s32[1]{0:T(128)} %bitcast.place_ref, ...), custom_call_target="tpu_custom_call" | custom-call | tf_op jit(solution)/shard_map/pallas_call | solution.py:508
  24.4 20.8 %all-to-all-done = bf16[32,48,384]{2,1,0:T(8,128)(2,1)S(1)} async-done(((bf16[32,48,384]{2,1,0:T(8,128)(2,1)}), bf16[32,48,384]{2,1,0:T(8,128)(2,1)S(1)}, u32[]{:S(2)}, u32[]{:S(2)}) %all-to-all-start) | async-done | bytes 1179680 | tf_op jit(solution)/shard_map/all_to_all | solution.py:578
  45.2 0.0 copy-start.3
  45.2 0.0 copy-start.4
  45.2 0.0 copy-start.5
  45.2 0.0 copy-start.2
  45.2 4.7 %shard_map.183 = (bf16[256,384]{1,0:T(8,128)(2,1)S(1)}, bf16[64,384]{1,0:T(8,128)(2,1)S(1)}, bf16[64,384]{1,0:T(8,128)(2,1)S(1)}, bf16[64,384]{1,0:T(8,128)(2,1)S(1)}, bf16[64,384]{1,0:T(8,128)(2,1)S(1)}) custom-call(s32[8,128]{1,0:T(8,128)S(1)} %get-tuple-element.24.tiles_ref.place_ref, f32[768,128]{1,0:T(8,128)S(1)} %get-tuple-element.25.late_wanted_ref, ...), custom_call_target="tpu_custom_call" | custom-call | tf_op jit(solution)/shard_map/pallas_call | solution.py:508
  49.9 1.6 %collective-permute-start = (bf16[64,384]{1,0:T(8,128)(2,1)S(1)}, bf16[64,384]{1,0:T(8,128)(2,1)S(1)}, u32[]{:S(2)}, u32[]{:S(2)}) collective-permute-start(bf16[64,384]{1,0:T(8,128)(2,1)S(1)} %get-tuple-element.36), channel_id=1, source_target_pairs={{0,2},{1,3},{2,4},{3,5},{4,6},{5,7},{6,0},{7,1},{8,10},{9,11},{10,... | collective-permute-start | bytes 147464 | tf_op jit(solution)/shard_map/ppermute | solution.py:680
  51.5 2.7 %collective-permute-start.1 = (bf16[64,384]{1,0:T(8,128)(2,1)S(1)}, bf16[64,384]{1,0:T(8,128)(2,1)S(1)}, u32[]{:S(2)}, u32[]{:S(2)}) collective-permute-start(bf16[64,384]{1,0:T(8,128)(2,1)S(1)} %get-tuple-element.37), channel_id=1, source_target_pairs={{0,4},{1,5},{2,6},{3,7},{4,0},{5,1},{6,2},{7,3},{8,12},{9,13},{10,... | collective-permute-start | bytes 147464 | tf_op jit(solution)/shard_map/ppermute | solution.py:680
  54.2 1.4 %collective-permute-start.2 = (bf16[64,384]{1,0:T(8,128)(2,1)S(1)}, bf16[64,384]{1,0:T(8,128)(2,1)S(1)}, u32[]{:S(2)}, u32[]{:S(2)}) collective-permute-start(bf16[64,384]{1,0:T(8,128)(2,1)S(1)} %get-tuple-element.38), channel_id=1, source_target_pairs={{0,6},{1,7},{2,0},{3,1},{4,2},{5,3},{6,4},{7,5},{8,14},{9,15},{10,... | collective-permute-start | bytes 147464 | tf_op jit(solution)/shard_map/ppermute | solution.py:680
  55.7 0.0 collective-permute-start.3
  55.7 0.0 collective-permute-done.refs_1_
  55.7 0.5 collective-permute-start.4
  56.2 0.9 %collective-permute-done.1.refs_2_ = bf16[64,384]{1,0:T(8,128)(2,1)S(1)} collective-permute-done((bf16[64,384]{1,0:T(8,128)(2,1)S(1)}, bf16[64,384]{1,0:T(8,128)(2,1)S(1)}, u32[]{:S(2)}, u32[]{:S(2)}) %collective-permute-start.1) | collective-permute-done | bytes 49184 | tf_op jit(solution)/shard_map/ppermute | solution.py:680
  57.1 0.0 collective-permute-start.5
  57.1 1.2 %collective-permute-done.2.refs_3_ = bf16[64,384]{1,0:T(8,128)(2,1)S(1)} collective-permute-done((bf16[64,384]{1,0:T(8,128)(2,1)S(1)}, bf16[64,384]{1,0:T(8,128)(2,1)S(1)}, u32[]{:S(2)}, u32[]{:S(2)}) %collective-permute-start.2) | collective-permute-done | bytes 49184 | tf_op jit(solution)/shard_map/ppermute | solution.py:680
  58.3 0.0 collective-permute-done.4.refs_5_
  58.4 1.2 %collective-permute-done.6.refs_7_ = bf16[64,384]{1,0:T(8,128)(2,1)S(1)} collective-permute-done((bf16[64,384]{1,0:T(8,128)(2,1)S(1)}, bf16[64,384]{1,0:T(8,128)(2,1)S(1)}, u32[]{:S(2)}, u32[]{:S(2)}) %collective-permute-start.6) | collective-permute-done | bytes 49184 | tf_op jit(solution)/shard_map/ppermute | solution.py:691
  59.6 1.3 %shard_map.184 = (bf16[64,384]{1,0:T(8,128)(2,1)S(1)}, bf16[64,384]{1,0:T(8,128)(2,1)S(1)}, bf16[64,384]{1,0:T(8,128)(2,1)S(1)}, bf16[64,384]{1,0:T(8,128)(2,1)S(1)}) custom-call(bf16[64,384]{1,0:T(8,128)(2,1)S(1)} %get-tuple-element.35.refs_0_, bf16[64,384]{1,0:T(8,128)(2,1)S(1)} %collective-permute-done.refs_1_, ...), custom_call_target="tpu_custom_call" | custom-call | tf_op jit(solution)/shard_map/pallas_call | solution.py:508
  60.9 2.7 %collective-permute-start.7 = (bf16[64,384]{1,0:T(8,128)(2,1)S(1)}, bf16[64,384]{1,0:T(8,128)(2,1)S(1)}, u32[]{:S(2)}, u32[]{:S(2)}) collective-permute-start(bf16[64,384]{1,0:T(8,128)(2,1)S(1)} %get-tuple-element.40), channel_id=1, source_target_pairs={{0,6},{1,7},{2,0},{3,1},{4,2},{5,3},{6,4},{7,5},{8,14},{9,15},{10,... | collective-permute-start | bytes 147464 | tf_op jit(solution)/shard_map/ppermute | solution.py:680
  63.6 1.0 %collective-permute-start.9 = (bf16[64,384]{1,0:T(8,128)(2,1)S(1)}, bf16[64,384]{1,0:T(8,128)(2,1)S(1)}, u32[]{:S(2)}, u32[]{:S(2)}) collective-permute-start(bf16[64,384]{1,0:T(8,128)(2,1)S(1)} %get-tuple-element.42), channel_id=1, source_target_pairs={{0,2},{1,3},{2,4},{3,5},{4,6},{5,7},{6,0},{7,1},{8,10},{9,11},{10,... | collective-permute-start | bytes 147464 | tf_op jit(solution)/shard_map/ppermute | solution.py:680
  64.6 0.1 compare_convert_fusion.live_ref
  64.7 1.3 %collective-permute-done.7.part1_ref = bf16[64,384]{1,0:T(8,128)(2,1)S(1)} collective-permute-done((bf16[64,384]{1,0:T(8,128)(2,1)S(1)}, bf16[64,384]{1,0:T(8,128)(2,1)S(1)}, u32[]{:S(2)}, u32[]{:S(2)}) %collective-permute-start.7) | collective-permute-done | bytes 49184 | tf_op jit(solution)/shard_map/ppermute | solution.py:680
  66.0 3.2 %collective-permute-done.8.part2_ref = bf16[64,384]{1,0:T(8,128)(2,1)S(1)} collective-permute-done((bf16[64,384]{1,0:T(8,128)(2,1)S(1)}, bf16[64,384]{1,0:T(8,128)(2,1)S(1)}, u32[]{:S(2)}, u32[]{:S(2)}) %collective-permute-start.8) | collective-permute-done | bytes 49184 | tf_op jit(solution)/shard_map/ppermute | solution.py:680
  69.3 0.2 collective-permute-done.9.part3_ref
  69.4 1.2 %shard_map.185 = bf16[2,192,256]{2,1,0:T(8,128)(2,1)} custom-call(s32[8,128]{1,0:T(8,128)S(1)} %get-tuple-element.24.tiles_ref.place_ref, bf16[256,384]{1,0:T(8,128)(2,1)S(1)} %get-tuple-element.34.state_ref, bf16[64,384]{1,0:T(8,128)(2,1)S(1)} %get-tuple-element.39.part0_ref, bf16[64,384]{1,0:T(8,128)(2,1)S(1)} %collective-permute-done.7.part1_ref, ...), custom_call_target="tpu_custom_call" | custom-call | tf_op jit(solution)/shard_map/pallas_call | solution.py:508
  (26 shorter events, 0.1 us)
Async XLA Ops:
  2.3 12.0 %copy-start.14 = (s32[256]{0:T(256)S(1)}, s32[256]{0:T(256)}, u32[]{:S(2)}) copy-start(s32[256]{0:T(256)} %param.25) | copy-start | bytes 3076
  2.3 12.4 %copy-start.12 = (bf16[384,192]{0,1:T(8,128)(2,1)S(1)}, bf16[384,192]{0,1:T(8,128)(2,1)}, u32[]{:S(2)}) copy-start(bf16[384,192]{0,1:T(8,128)(2,1)} %param.29) | copy-start | bytes 442372
  2.4 12.6 %copy-start.11 = (bf16[576,192]{0,1:T(8,128)(2,1)S(1)}, bf16[576,192]{0,1:T(8,128)(2,1)}, u32[]{:S(2)}) copy-start(bf16[576,192]{0,1:T(8,128)(2,1)} %param.26) | copy-start | bytes 663556
  2.4 12.8 %copy-start.15 = (s32[16]{0:T(128)S(1)}, s32[16]{0:T(128)}, u32[]{:S(2)}) copy-start(s32[16]{0:T(128)} %param.23) | copy-start | bytes 196
  2.4 12.8 %copy-start.13 = (s32[2048]{0:T(1024)S(1)}, s32[2048]{0:T(1024)}, u32[]{:S(2)}) copy-start(s32[2048]{0:T(1024)} %param.22) | copy-start | bytes 24580
  2.4 12.9 %copy-start = (bf16[192,192]{1,0:T(8,128)(2,1)S(1)}, bf16[192,192]{1,0:T(8,128)(2,1)}, u32[]{:S(2)}) copy-start(bf16[192,192]{1,0:T(8,128)(2,1)} %w_out_ref.3) | copy-start | bytes 221188
  2.4 12.9 %copy-start.6 = (s32[2048]{0:T(1024)S(1)}, s32[2048]{0:T(1024)}, u32[]{:S(2)}) copy-start(s32[2048]{0:T(1024)} %param.21) | copy-start | bytes 24580
  2.4 12.9 %copy-start.10 = (f32[192]{0:T(256)S(1)}, f32[192]{0:T(256)}, u32[]{:S(2)}) copy-start(f32[192]{0:T(256)} %param.27) | copy-start | bytes 2308
  2.4 42.7 %all-to-all-start = ((bf16[32,48,384]{2,1,0:T(8,128)(2,1)}), bf16[32,48,384]{2,1,0:T(8,128)(2,1)S(1)}, u32[]{:S(2)}, u32[]{:S(2)}) async-start(bf16[32,48,384]{2,1,0:T(8,128)(2,1)} %bitcast.11), calls=%async_computation | async-start | bytes 2359296 | tf_op jit(solution)/shard_map/all_to_all | solution.py:578
  14.8 30.4 %copy-start.1 = (bf16[192,192]{1,0:T(8,128)(2,1)S(1)}, bf16[192,192]{1,0:T(8,128)(2,1)}, u32[]{:S(2)}) copy-start(bf16[192,192]{1,0:T(8,128)(2,1)} %node_w_out_ref.1) | copy-start | bytes 221188
  14.8 30.4 %copy-start.7 = (f32[192]{0:T(256)S(1)}, f32[192]{0:T(256)}, u32[]{:S(2)}) copy-start(f32[192]{0:T(256)} %param.30) | copy-start | bytes 2308
  14.8 30.4 %copy-start.8 = (f32[192]{0:T(256)S(1)}, f32[192]{0:T(256)}, u32[]{:S(2)}) copy-start(f32[192]{0:T(256)} %param.32) | copy-start | bytes 2308
  14.8 30.3 %copy-start.9 = (f32[192]{0:T(256)S(1)}, f32[192]{0:T(256)}, u32[]{:S(2)}) copy-start(f32[192]{0:T(256)} %param.33) | copy-start | bytes 2308
  45.2 14.4 %copy-start.3 = (bf16[192,192]{1,0:T(8,128)(2,1)S(1)}, bf16[192,192]{1,0:T(8,128)(2,1)}, u32[]{:S(2)}) copy-start(bf16[192,192]{1,0:T(8,128)(2,1)} %refs_9_.1) | copy-start | bytes 221188
  45.2 14.4 %copy-start.4 = (bf16[192,192]{1,0:T(8,128)(2,1)S(1)}, bf16[192,192]{1,0:T(8,128)(2,1)}, u32[]{:S(2)}) copy-start(bf16[192,192]{1,0:T(8,128)(2,1)} %refs_10_.1) | copy-start | bytes 221188
  45.2 14.4 %copy-start.5 = (bf16[192,192]{1,0:T(8,128)(2,1)S(1)}, bf16[192,192]{1,0:T(8,128)(2,1)}, u32[]{:S(2)}) copy-start(bf16[192,192]{1,0:T(8,128)(2,1)} %refs_11_.1) | copy-start | bytes 221188
  45.2 24.2 %copy-start.2 = (bf16[192,192]{1,0:T(8,128)(2,1)S(1)}, bf16[192,192]{1,0:T(8,128)(2,1)}, u32[]{:S(2)}) copy-start(bf16[192,192]{1,0:T(8,128)(2,1)} %weight_ref.1) | copy-start | bytes 221188
  49.9 5.8 %collective-permute-start = (bf16[64,384]{1,0:T(8,128)(2,1)S(1)}, bf16[64,384]{1,0:T(8,128)(2,1)S(1)}, u32[]{:S(2)}, u32[]{:S(2)}) collective-permute-start(bf16[64,384]{1,0:T(8,128)(2,1)S(1)} %get-tuple-element.36), channel_id=1, source_target_pairs={{0,2},{1,3},{2,4},{3,5},{4,6},{5,7},{6,0},{7,1},{8,10},{9,11},{10,... | collective-permute-start | bytes 147464 | tf_op jit(solution)/shard_map/ppermute | solution.py:680
  51.5 5.6 %collective-permute-start.1 = (bf16[64,384]{1,0:T(8,128)(2,1)S(1)}, bf16[64,384]{1,0:T(8,128)(2,1)S(1)}, u32[]{:S(2)}, u32[]{:S(2)}) collective-permute-start(bf16[64,384]{1,0:T(8,128)(2,1)S(1)} %get-tuple-element.37), channel_id=1, source_target_pairs={{0,4},{1,5},{2,6},{3,7},{4,0},{5,1},{6,2},{7,3},{8,12},{9,13},{10,... | collective-permute-start | bytes 147464 | tf_op jit(solution)/shard_map/ppermute | solution.py:680
  54.2 4.1 %collective-permute-start.2 = (bf16[64,384]{1,0:T(8,128)(2,1)S(1)}, bf16[64,384]{1,0:T(8,128)(2,1)S(1)}, u32[]{:S(2)}, u32[]{:S(2)}) collective-permute-start(bf16[64,384]{1,0:T(8,128)(2,1)S(1)} %get-tuple-element.38), channel_id=1, source_target_pairs={{0,6},{1,7},{2,0},{3,1},{4,2},{5,3},{6,4},{7,5},{8,14},{9,15},{10,... | collective-permute-start | bytes 147464 | tf_op jit(solution)/shard_map/ppermute | solution.py:680
  55.7 2.7 %collective-permute-start.3 = (bf16[64,384]{1,0:T(8,128)(2,1)S(1)}, bf16[64,384]{1,0:T(8,128)(2,1)S(1)}, u32[]{:S(2)}, u32[]{:S(2)}) collective-permute-start(bf16[64,384]{1,0:T(8,128)(2,1)S(1)} %get-tuple-element.35.refs_0_), channel_id=1, source_target_pairs={{0,1},{1,0},{2,3},{3,2},{4,5},{5,4},{6,7},{7,6},{8,9},{9,8},{10,11... | collective-permute-start | bytes 147464 | tf_op jit(solution)/shard_map/ppermute | solution.py:691
  55.7 2.6 %collective-permute-start.4 = (bf16[64,384]{1,0:T(8,128)(2,1)S(1)}, bf16[64,384]{1,0:T(8,128)(2,1)S(1)}, u32[]{:S(2)}, u32[]{:S(2)}) collective-permute-start(bf16[64,384]{1,0:T(8,128)(2,1)S(1)} %collective-permute-done.refs_1_), channel_id=1, source_target_pairs={{0,1},{1,0},{2,3},{3,2},{4,5},{5,4},{6,7},{7,6},{8,9},{9,8},{10,11... | collective-permute-start | bytes 147464 | tf_op jit(solution)/shard_map/ppermute | solution.py:691
  57.1 1.3 %collective-permute-start.5 = (bf16[64,384]{1,0:T(8,128)(2,1)S(1)}, bf16[64,384]{1,0:T(8,128)(2,1)S(1)}, u32[]{:S(2)}, u32[]{:S(2)}) collective-permute-start(bf16[64,384]{1,0:T(8,128)(2,1)S(1)} %collective-permute-done.1.refs_2_), channel_id=1, source_target_pairs={{0,1},{1,0},{2,3},{3,2},{4,5},{5,4},{6,7},{7,6},{8,9},{9,8},{10,11... | collective-permute-start | bytes 147464 | tf_op jit(solution)/shard_map/ppermute | solution.py:691
  58.3 1.2 %collective-permute-start.6 = (bf16[64,384]{1,0:T(8,128)(2,1)S(1)}, bf16[64,384]{1,0:T(8,128)(2,1)S(1)}, u32[]{:S(2)}, u32[]{:S(2)}) collective-permute-start(bf16[64,384]{1,0:T(8,128)(2,1)S(1)} %collective-permute-done.2.refs_3_), channel_id=1, source_target_pairs={{0,1},{1,0},{2,3},{3,2},{4,5},{5,4},{6,7},{7,6},{8,9},{9,8},{10,11... | collective-permute-start | bytes 147464 | tf_op jit(solution)/shard_map/ppermute | solution.py:691
  60.9 5.1 %collective-permute-start.7 = (bf16[64,384]{1,0:T(8,128)(2,1)S(1)}, bf16[64,384]{1,0:T(8,128)(2,1)S(1)}, u32[]{:S(2)}, u32[]{:S(2)}) collective-permute-start(bf16[64,384]{1,0:T(8,128)(2,1)S(1)} %get-tuple-element.40), channel_id=1, source_target_pairs={{0,6},{1,7},{2,0},{3,1},{4,2},{5,3},{6,4},{7,5},{8,14},{9,15},{10,... | collective-permute-start | bytes 147464 | tf_op jit(solution)/shard_map/ppermute | solution.py:680
  63.6 5.6 %collective-permute-start.8 = (bf16[64,384]{1,0:T(8,128)(2,1)S(1)}, bf16[64,384]{1,0:T(8,128)(2,1)S(1)}, u32[]{:S(2)}, u32[]{:S(2)}) collective-permute-start(bf16[64,384]{1,0:T(8,128)(2,1)S(1)} %get-tuple-element.41), channel_id=1, source_target_pairs={{0,4},{1,5},{2,6},{3,7},{4,0},{5,1},{6,2},{7,3},{8,12},{9,13},{10,... | collective-permute-start | bytes 147464 | tf_op jit(solution)/shard_map/ppermute | solution.py:680
  63.6 5.8 %collective-permute-start.9 = (bf16[64,384]{1,0:T(8,128)(2,1)S(1)}, bf16[64,384]{1,0:T(8,128)(2,1)S(1)}, u32[]{:S(2)}, u32[]{:S(2)}) collective-permute-start(bf16[64,384]{1,0:T(8,128)(2,1)S(1)} %get-tuple-element.42), channel_id=1, source_target_pairs={{0,2},{1,3},{2,4},{3,5},{4,6},{5,7},{6,0},{7,1},{8,10},{9,11},{10,... | collective-permute-start | bytes 147464 | tf_op jit(solution)/shard_map/ppermute | solution.py:680

commit v8 on v7

--- a/solution.py
+++ b/solution.py
@@ -352,10 +352,6 @@
         return dot(silu(pre + sent).astype(BF16), w_out_ref[...]).astype(BF16)
 
     sent0, sent1 = gather(late_wanted_ref[...])
-    early[0].wait()
-    late_pre0, late_pre1 = get_pair(late_pre_ref)
-    message0 = messages(late_pre0, sent0)
-    message1 = messages(late_pre1, sent1)
     nodes = lax.broadcasted_iota(jnp.int32, (state_ref.shape[0], WIDE), 0).astype(F32)
     deliver = jnp.concatenate(
         [
@@ -364,6 +360,10 @@
         ],
         axis=1,
     )
+    early[0].wait()
+    late_pre0, late_pre1 = get_pair(late_pre_ref)
+    message0 = messages(late_pre0, sent0)
+    message1 = messages(late_pre1, sent1)
     arrived0, arrived1 = dot(deliver, message0), dot(deliver, message1)
     for fetch in early[1:]:
         fetch.wait()

time: 71.1 us -> 71.1 us (level)
  Pallas kernels: 18.7 us -> 22 us
  waiting for transfers between devices: 28.9 us -> 25.6 us
    pallas_call x5, Pallas kernels: 18.7 us -> 22 us  [call(): pl.pallas_call(kernel, out_shape=out_shape, **specs, scratch_shapes=list(...]
    all_to_all x1, waiting for transfers between devices: 20.8 us -> 17.5 us  [per_device(): lax.all_to_all(outgoing.reshape(patch_count, slot_count, merged), 'patch'...]
  transfers between devices with their start and end apart: 11 -> 11, of which waited for: 7 -> 7; matrix products, arithmetic and copies ran while one was open for 1% -> 1% of each run, Pallas kernels for 13% -> 18%
where the time goes in v8:
time: 71.1 us; the launch traced here: 70.8 us
  waiting for transfers between devices  25.6 us (36%)
  Pallas kernels  22 us (31%)
  starting transfers between devices  21.8 us (31%)
  local copies, waits for them, and re-layouts  0.82 us (1%)
    pallas_call x5, Pallas kernels, call(): pl.pallas_call(kernel, out_shape=out_shape, **specs, scratch_shapes=list(...  22 us
    all_to_all x1, waiting for transfers between devices, per_device(): lax.all_to_all(outgoing.reshape(patch_count, slot_count, merged), 'patch'...  17.5 us
    all_to_all x1, starting transfers between devices, per_device(): lax.all_to_all(outgoing.reshape(patch_count, slot_count, merged), 'patch'...  11.8 us
    ppermute x6, starting transfers between devices, to_chip(): lax.ppermute(array, 'lev', [(a * CORES + b, (a + shift) % CHIPS * CORES +...  9.41 us
    ppermute x6, waiting for transfers between devices, to_chip(): lax.ppermute(array, 'lev', [(a * CORES + b, (a + shift) % CHIPS * CORES +...  6.9 us
  transfers between devices with their start and end apart: 11, of which 7 were waited for; matrix products, arithmetic and copies ran while one was open for 1% of the time, Pallas kernels for 18%

profile of v8, /device:TPU:8, one launch (start us, length us, event | category | flops | bytes accessed | tf_op | source)
XLA Modules:
  0.0 70.8 jit_solution(3222874523569870228)
XLA Ops:
  0.0 2.3 %shard_map.182 = bf16[1536,384]{1,0:T(8,128)(2,1)} custom-call(s32[32,48]{1,0:T(8,128)} %halo_hbm.1, bf16[384,256]{1,0:T(8,128)(2,1)} %bitcast.29), custom_call_target="tpu_custom_call" | custom-call | tf_op jit(solution)/shard_map/pallas_call | solution.py:508
  2.3 0.0 copy-start.14
  2.3 0.0 copy-start.12
  2.4 0.0 copy-start.11
  2.4 0.0 copy-start.15
  2.4 0.0 copy-start.13
  2.4 0.0 copy-start
  2.4 0.0 copy-start.6
  2.4 0.0 copy-start.10
  2.4 11.8 %all-to-all-start = ((bf16[32,48,384]{2,1,0:T(8,128)(2,1)}), bf16[32,48,384]{2,1,0:T(8,128)(2,1)S(1)}, u32[]{:S(2)}, u32[]{:S(2)}) async-start(bf16[32,48,384]{2,1,0:T(8,128)(2,1)} %bitcast.11), calls=%async_computation | async-start | bytes 2359296 | tf_op jit(solution)/shard_map/all_to_all | solution.py:578
  14.3 0.1 dynamic_slice.3
  14.4 0.1 lt.75
  14.5 0.1 lt.71
  14.6 0.1 lt.72
  14.7 0.1 lt.77
  14.8 0.0 copy-start.1
  14.8 0.0 copy-start.7
  14.8 0.0 copy-start.8
  14.8 0.0 copy-start.9
  14.8 0.1 copy.25.node_w_in_ref
  15.0 0.2 copy.23.w_in_ref
  15.2 0.1 fusion.receiver_ref
  15.3 12.4 %shard_map.181 = (s32[8,128]{1,0:T(8,128)S(1)}, f32[768,128]{1,0:T(8,128)S(1)}, f32[768,384]{1,0:T(8,128)}, f32[3,8,256]{2,1,0:T(8,128)S(1)}, bf16[256,384]{1,0:...) custom-call(s32[1]{0:T(128)} %bitcast.place_ref, ...), custom_call_target="tpu_custom_call" | custom-call | tf_op jit(solution)/shard_map/pallas_call | solution.py:508
  27.7 17.5 %all-to-all-done = bf16[32,48,384]{2,1,0:T(8,128)(2,1)S(1)} async-done(((bf16[32,48,384]{2,1,0:T(8,128)(2,1)}), bf16[32,48,384]{2,1,0:T(8,128)(2,1)S(1)}, u32[]{:S(2)}, u32[]{:S(2)}) %all-to-all-start) | async-done | bytes 1179680 | tf_op jit(solution)/shard_map/all_to_all | solution.py:578
  45.2 0.0 copy-start.3
  45.2 0.0 copy-start.4
  45.2 0.0 copy-start.5
  45.2 0.0 copy-start.2
  45.2 4.7 %shard_map.183 = (bf16[256,384]{1,0:T(8,128)(2,1)S(1)}, bf16[64,384]{1,0:T(8,128)(2,1)S(1)}, bf16[64,384]{1,0:T(8,128)(2,1)S(1)}, bf16[64,384]{1,0:T(8,128)(2,1)S(1)}, bf16[64,384]{1,0:T(8,128)(2,1)S(1)}) custom-call(s32[8,128]{1,0:T(8,128)S(1)} %get-tuple-element.24.tiles_ref.place_ref, f32[768,128]{1,0:T(8,128)S(1)} %get-tuple-element.25.late_wanted_ref, ...), custom_call_target="tpu_custom_call" | custom-call | tf_op jit(solution)/shard_map/pallas_call | solution.py:508
  49.9 1.6 %collective-permute-start = (bf16[64,384]{1,0:T(8,128)(2,1)S(1)}, bf16[64,384]{1,0:T(8,128)(2,1)S(1)}, u32[]{:S(2)}, u32[]{:S(2)}) collective-permute-start(bf16[64,384]{1,0:T(8,128)(2,1)S(1)} %get-tuple-element.36), channel_id=1, source_target_pairs={{0,2},{1,3},{2,4},{3,5},{4,6},{5,7},{6,0},{7,1},{8,10},{9,11},{10,... | collective-permute-start | bytes 147464 | tf_op jit(solution)/shard_map/ppermute | solution.py:680
  51.5 2.7 %collective-permute-start.1 = (bf16[64,384]{1,0:T(8,128)(2,1)S(1)}, bf16[64,384]{1,0:T(8,128)(2,1)S(1)}, u32[]{:S(2)}, u32[]{:S(2)}) collective-permute-start(bf16[64,384]{1,0:T(8,128)(2,1)S(1)} %get-tuple-element.37), channel_id=1, source_target_pairs={{0,4},{1,5},{2,6},{3,7},{4,0},{5,1},{6,2},{7,3},{8,12},{9,13},{10,... | collective-permute-start | bytes 147464 | tf_op jit(solution)/shard_map/ppermute | solution.py:680
  54.2 1.4 %collective-permute-start.2 = (bf16[64,384]{1,0:T(8,128)(2,1)S(1)}, bf16[64,384]{1,0:T(8,128)(2,1)S(1)}, u32[]{:S(2)}, u32[]{:S(2)}) collective-permute-start(bf16[64,384]{1,0:T(8,128)(2,1)S(1)} %get-tuple-element.38), channel_id=1, source_target_pairs={{0,6},{1,7},{2,0},{3,1},{4,2},{5,3},{6,4},{7,5},{8,14},{9,15},{10,... | collective-permute-start | bytes 147464 | tf_op jit(solution)/shard_map/ppermute | solution.py:680
  55.7 0.0 collective-permute-start.3
  55.7 0.0 collective-permute-done.refs_1_
  55.7 0.5 collective-permute-start.4
  56.2 0.9 %collective-permute-done.1.refs_2_ = bf16[64,384]{1,0:T(8,128)(2,1)S(1)} collective-permute-done((bf16[64,384]{1,0:T(8,128)(2,1)S(1)}, bf16[64,384]{1,0:T(8,128)(2,1)S(1)}, u32[]{:S(2)}, u32[]{:S(2)}) %collective-permute-start.1) | collective-permute-done | bytes 49184 | tf_op jit(solution)/shard_map/ppermute | solution.py:680
  57.1 1.2 %collective-permute-done.2.refs_3_ = bf16[64,384]{1,0:T(8,128)(2,1)S(1)} collective-permute-done((bf16[64,384]{1,0:T(8,128)(2,1)S(1)}, bf16[64,384]{1,0:T(8,128)(2,1)S(1)}, u32[]{:S(2)}, u32[]{:S(2)}) %collective-permute-start.2) | collective-permute-done | bytes 49184 | tf_op jit(solution)/shard_map/ppermute | solution.py:680
  58.3 0.0 collective-permute-start.6
  58.3 0.0 collective-permute-done.3.refs_4_
  58.4 1.2 %collective-permute-done.6.refs_7_ = bf16[64,384]{1,0:T(8,128)(2,1)S(1)} collective-permute-done((bf16[64,384]{1,0:T(8,128)(2,1)S(1)}, bf16[64,384]{1,0:T(8,128)(2,1)S(1)}, u32[]{:S(2)}, u32[]{:S(2)}) %collective-permute-start.6) | collective-permute-done | bytes 49184 | tf_op jit(solution)/shard_map/ppermute | solution.py:691
  59.6 1.3 %shard_map.184 = (bf16[64,384]{1,0:T(8,128)(2,1)S(1)}, bf16[64,384]{1,0:T(8,128)(2,1)S(1)}, bf16[64,384]{1,0:T(8,128)(2,1)S(1)}, bf16[64,384]{1,0:T(8,128)(2,1)S(1)}) custom-call(bf16[64,384]{1,0:T(8,128)(2,1)S(1)} %get-tuple-element.35.refs_0_, bf16[64,384]{1,0:T(8,128)(2,1)S(1)} %collective-permute-done.refs_1_, ...), custom_call_target="tpu_custom_call" | custom-call | tf_op jit(solution)/shard_map/pallas_call | solution.py:508
  60.9 2.7 %collective-permute-start.7 = (bf16[64,384]{1,0:T(8,128)(2,1)S(1)}, bf16[64,384]{1,0:T(8,128)(2,1)S(1)}, u32[]{:S(2)}, u32[]{:S(2)}) collective-permute-start(bf16[64,384]{1,0:T(8,128)(2,1)S(1)} %get-tuple-element.40), channel_id=1, source_target_pairs={{0,6},{1,7},{2,0},{3,1},{4,2},{5,3},{6,4},{7,5},{8,14},{9,15},{10,... | collective-permute-start | bytes 147464 | tf_op jit(solution)/shard_map/ppermute | solution.py:680
  63.6 1.0 %collective-permute-start.9 = (bf16[64,384]{1,0:T(8,128)(2,1)S(1)}, bf16[64,384]{1,0:T(8,128)(2,1)S(1)}, u32[]{:S(2)}, u32[]{:S(2)}) collective-permute-start(bf16[64,384]{1,0:T(8,128)(2,1)S(1)} %get-tuple-element.42), channel_id=1, source_target_pairs={{0,2},{1,3},{2,4},{3,5},{4,6},{5,7},{6,0},{7,1},{8,10},{9,11},{10,... | collective-permute-start | bytes 147464 | tf_op jit(solution)/shard_map/ppermute | solution.py:680
  64.6 0.1 compare_convert_fusion.live_ref
  64.7 1.3 %collective-permute-done.7.part1_ref = bf16[64,384]{1,0:T(8,128)(2,1)S(1)} collective-permute-done((bf16[64,384]{1,0:T(8,128)(2,1)S(1)}, bf16[64,384]{1,0:T(8,128)(2,1)S(1)}, u32[]{:S(2)}, u32[]{:S(2)}) %collective-permute-start.7) | collective-permute-done | bytes 49184 | tf_op jit(solution)/shard_map/ppermute | solution.py:680
  66.0 3.2 %collective-permute-done.8.part2_ref = bf16[64,384]{1,0:T(8,128)(2,1)S(1)} collective-permute-done((bf16[64,384]{1,0:T(8,128)(2,1)S(1)}, bf16[64,384]{1,0:T(8,128)(2,1)S(1)}, u32[]{:S(2)}, u32[]{:S(2)}) %collective-permute-start.8) | collective-permute-done | bytes 49184 | tf_op jit(solution)/shard_map/ppermute | solution.py:680
  69.3 0.2 collective-permute-done.9.part3_ref
  69.4 1.2 %shard_map.185 = bf16[2,192,256]{2,1,0:T(8,128)(2,1)} custom-call(s32[8,128]{1,0:T(8,128)S(1)} %get-tuple-element.24.tiles_ref.place_ref, bf16[256,384]{1,0:T(8,128)(2,1)S(1)} %get-tuple-element.34.state_ref, bf16[64,384]{1,0:T(8,128)(2,1)S(1)} %get-tuple-element.39.part0_ref, bf16[64,384]{1,0:T(8,128)(2,1)S(1)} %collective-permute-done.7.part1_ref, ...), custom_call_target="tpu_custom_call" | custom-call | tf_op jit(solution)/shard_map/pallas_call | solution.py:508
  (26 shorter events, 0.1 us)
Async XLA Ops:
  2.3 12.0 %copy-start.14 = (s32[256]{0:T(256)S(1)}, s32[256]{0:T(256)}, u32[]{:S(2)}) copy-start(s32[256]{0:T(256)} %param.25) | copy-start | bytes 3076
  2.3 12.4 %copy-start.12 = (bf16[384,192]{0,1:T(8,128)(2,1)S(1)}, bf16[384,192]{0,1:T(8,128)(2,1)}, u32[]{:S(2)}) copy-start(bf16[384,192]{0,1:T(8,128)(2,1)} %param.29) | copy-start | bytes 442372
  2.4 12.6 %copy-start.11 = (bf16[576,192]{0,1:T(8,128)(2,1)S(1)}, bf16[576,192]{0,1:T(8,128)(2,1)}, u32[]{:S(2)}) copy-start(bf16[576,192]{0,1:T(8,128)(2,1)} %param.26) | copy-start | bytes 663556
  2.4 12.8 %copy-start.15 = (s32[16]{0:T(128)S(1)}, s32[16]{0:T(128)}, u32[]{:S(2)}) copy-start(s32[16]{0:T(128)} %param.23) | copy-start | bytes 196
  2.4 12.8 %copy-start.13 = (s32[2048]{0:T(1024)S(1)}, s32[2048]{0:T(1024)}, u32[]{:S(2)}) copy-start(s32[2048]{0:T(1024)} %param.22) | copy-start | bytes 24580
  2.4 12.9 %copy-start = (bf16[192,192]{1,0:T(8,128)(2,1)S(1)}, bf16[192,192]{1,0:T(8,128)(2,1)}, u32[]{:S(2)}) copy-start(bf16[192,192]{1,0:T(8,128)(2,1)} %w_out_ref.3) | copy-start | bytes 221188
  2.4 12.9 %copy-start.6 = (s32[2048]{0:T(1024)S(1)}, s32[2048]{0:T(1024)}, u32[]{:S(2)}) copy-start(s32[2048]{0:T(1024)} %param.21) | copy-start | bytes 24580
  2.4 12.9 %copy-start.10 = (f32[192]{0:T(256)S(1)}, f32[192]{0:T(256)}, u32[]{:S(2)}) copy-start(f32[192]{0:T(256)} %param.27) | copy-start | bytes 2308
  2.4 42.7 %all-to-all-start = ((bf16[32,48,384]{2,1,0:T(8,128)(2,1)}), bf16[32,48,384]{2,1,0:T(8,128)(2,1)S(1)}, u32[]{:S(2)}, u32[]{:S(2)}) async-start(bf16[32,48,384]{2,1,0:T(8,128)(2,1)} %bitcast.11), calls=%async_computation | async-start | bytes 2359296 | tf_op jit(solution)/shard_map/all_to_all | solution.py:578
  14.8 30.4 %copy-start.1 = (bf16[192,192]{1,0:T(8,128)(2,1)S(1)}, bf16[192,192]{1,0:T(8,128)(2,1)}, u32[]{:S(2)}) copy-start(bf16[192,192]{1,0:T(8,128)(2,1)} %node_w_out_ref.1) | copy-start | bytes 221188
  14.8 30.4 %copy-start.7 = (f32[192]{0:T(256)S(1)}, f32[192]{0:T(256)}, u32[]{:S(2)}) copy-start(f32[192]{0:T(256)} %param.30) | copy-start | bytes 2308
  14.8 30.4 %copy-start.8 = (f32[192]{0:T(256)S(1)}, f32[192]{0:T(256)}, u32[]{:S(2)}) copy-start(f32[192]{0:T(256)} %param.32) | copy-start | bytes 2308
  14.8 30.3 %copy-start.9 = (f32[192]{0:T(256)S(1)}, f32[192]{0:T(256)}, u32[]{:S(2)}) copy-start(f32[192]{0:T(256)} %param.33) | copy-start | bytes 2308
  45.2 14.4 %copy-start.3 = (bf16[192,192]{1,0:T(8,128)(2,1)S(1)}, bf16[192,192]{1,0:T(8,128)(2,1)}, u32[]{:S(2)}) copy-start(bf16[192,192]{1,0:T(8,128)(2,1)} %refs_9_.1) | copy-start | bytes 221188
  45.2 14.4 %copy-start.4 = (bf16[192,192]{1,0:T(8,128)(2,1)S(1)}, bf16[192,192]{1,0:T(8,128)(2,1)}, u32[]{:S(2)}) copy-start(bf16[192,192]{1,0:T(8,128)(2,1)} %refs_10_.1) | copy-start | bytes 221188
  45.2 14.3 %copy-start.5 = (bf16[192,192]{1,0:T(8,128)(2,1)S(1)}, bf16[192,192]{1,0:T(8,128)(2,1)}, u32[]{:S(2)}) copy-start(bf16[192,192]{1,0:T(8,128)(2,1)} %refs_11_.1) | copy-start | bytes 221188
  45.2 24.2 %copy-start.2 = (bf16[192,192]{1,0:T(8,128)(2,1)S(1)}, bf16[192,192]{1,0:T(8,128)(2,1)}, u32[]{:S(2)}) copy-start(bf16[192,192]{1,0:T(8,128)(2,1)} %weight_ref.1) | copy-start | bytes 221188
  49.9 5.8 %collective-permute-start = (bf16[64,384]{1,0:T(8,128)(2,1)S(1)}, bf16[64,384]{1,0:T(8,128)(2,1)S(1)}, u32[]{:S(2)}, u32[]{:S(2)}) collective-permute-start(bf16[64,384]{1,0:T(8,128)(2,1)S(1)} %get-tuple-element.36), channel_id=1, source_target_pairs={{0,2},{1,3},{2,4},{3,5},{4,6},{5,7},{6,0},{7,1},{8,10},{9,11},{10,... | collective-permute-start | bytes 147464 | tf_op jit(solution)/shard_map/ppermute | solution.py:680
  51.5 5.6 %collective-permute-start.1 = (bf16[64,384]{1,0:T(8,128)(2,1)S(1)}, bf16[64,384]{1,0:T(8,128)(2,1)S(1)}, u32[]{:S(2)}, u32[]{:S(2)}) collective-permute-start(bf16[64,384]{1,0:T(8,128)(2,1)S(1)} %get-tuple-element.37), channel_id=1, source_target_pairs={{0,4},{1,5},{2,6},{3,7},{4,0},{5,1},{6,2},{7,3},{8,12},{9,13},{10,... | collective-permute-start | bytes 147464 | tf_op jit(solution)/shard_map/ppermute | solution.py:680
  54.2 4.1 %collective-permute-start.2 = (bf16[64,384]{1,0:T(8,128)(2,1)S(1)}, bf16[64,384]{1,0:T(8,128)(2,1)S(1)}, u32[]{:S(2)}, u32[]{:S(2)}) collective-permute-start(bf16[64,384]{1,0:T(8,128)(2,1)S(1)} %get-tuple-element.38), channel_id=1, source_target_pairs={{0,6},{1,7},{2,0},{3,1},{4,2},{5,3},{6,4},{7,5},{8,14},{9,15},{10,... | collective-permute-start | bytes 147464 | tf_op jit(solution)/shard_map/ppermute | solution.py:680
  55.7 2.7 %collective-permute-start.3 = (bf16[64,384]{1,0:T(8,128)(2,1)S(1)}, bf16[64,384]{1,0:T(8,128)(2,1)S(1)}, u32[]{:S(2)}, u32[]{:S(2)}) collective-permute-start(bf16[64,384]{1,0:T(8,128)(2,1)S(1)} %get-tuple-element.35.refs_0_), channel_id=1, source_target_pairs={{0,1},{1,0},{2,3},{3,2},{4,5},{5,4},{6,7},{7,6},{8,9},{9,8},{10,11... | collective-permute-start | bytes 147464 | tf_op jit(solution)/shard_map/ppermute | solution.py:691
  55.7 2.6 %collective-permute-start.4 = (bf16[64,384]{1,0:T(8,128)(2,1)S(1)}, bf16[64,384]{1,0:T(8,128)(2,1)S(1)}, u32[]{:S(2)}, u32[]{:S(2)}) collective-permute-start(bf16[64,384]{1,0:T(8,128)(2,1)S(1)} %collective-permute-done.refs_1_), channel_id=1, source_target_pairs={{0,1},{1,0},{2,3},{3,2},{4,5},{5,4},{6,7},{7,6},{8,9},{9,8},{10,11... | collective-permute-start | bytes 147464 | tf_op jit(solution)/shard_map/ppermute | solution.py:691
  57.1 1.3 %collective-permute-start.5 = (bf16[64,384]{1,0:T(8,128)(2,1)S(1)}, bf16[64,384]{1,0:T(8,128)(2,1)S(1)}, u32[]{:S(2)}, u32[]{:S(2)}) collective-permute-start(bf16[64,384]{1,0:T(8,128)(2,1)S(1)} %collective-permute-done.1.refs_2_), channel_id=1, source_target_pairs={{0,1},{1,0},{2,3},{3,2},{4,5},{5,4},{6,7},{7,6},{8,9},{9,8},{10,11... | collective-permute-start | bytes 147464 | tf_op jit(solution)/shard_map/ppermute | solution.py:691
  58.3 1.2 %collective-permute-start.6 = (bf16[64,384]{1,0:T(8,128)(2,1)S(1)}, bf16[64,384]{1,0:T(8,128)(2,1)S(1)}, u32[]{:S(2)}, u32[]{:S(2)}) collective-permute-start(bf16[64,384]{1,0:T(8,128)(2,1)S(1)} %collective-permute-done.2.refs_3_), channel_id=1, source_target_pairs={{0,1},{1,0},{2,3},{3,2},{4,5},{5,4},{6,7},{7,6},{8,9},{9,8},{10,11... | collective-permute-start | bytes 147464 | tf_op jit(solution)/shard_map/ppermute | solution.py:691
  60.9 5.1 %collective-permute-start.7 = (bf16[64,384]{1,0:T(8,128)(2,1)S(1)}, bf16[64,384]{1,0:T(8,128)(2,1)S(1)}, u32[]{:S(2)}, u32[]{:S(2)}) collective-permute-start(bf16[64,384]{1,0:T(8,128)(2,1)S(1)} %get-tuple-element.40), channel_id=1, source_target_pairs={{0,6},{1,7},{2,0},{3,1},{4,2},{5,3},{6,4},{7,5},{8,14},{9,15},{10,... | collective-permute-start | bytes 147464 | tf_op jit(solution)/shard_map/ppermute | solution.py:680
  63.6 5.6 %collective-permute-start.8 = (bf16[64,384]{1,0:T(8,128)(2,1)S(1)}, bf16[64,384]{1,0:T(8,128)(2,1)S(1)}, u32[]{:S(2)}, u32[]{:S(2)}) collective-permute-start(bf16[64,384]{1,0:T(8,128)(2,1)S(1)} %get-tuple-element.41), channel_id=1, source_target_pairs={{0,4},{1,5},{2,6},{3,7},{4,0},{5,1},{6,2},{7,3},{8,12},{9,13},{10,... | collective-permute-start | bytes 147464 | tf_op jit(solution)/shard_map/ppermute | solution.py:680
  63.6 5.8 %collective-permute-start.9 = (bf16[64,384]{1,0:T(8,128)(2,1)S(1)}, bf16[64,384]{1,0:T(8,128)(2,1)S(1)}, u32[]{:S(2)}, u32[]{:S(2)}) collective-permute-start(bf16[64,384]{1,0:T(8,128)(2,1)S(1)} %get-tuple-element.42), channel_id=1, source_target_pairs={{0,2},{1,3},{2,4},{3,5},{4,6},{5,7},{6,0},{7,1},{8,10},{9,11},{10,... | collective-permute-start | bytes 147464 | tf_op jit(solution)/shard_map/ppermute | solution.py:680
